TPU v7x, 32 devices: a whole 2x2x4 slice. The times are simulated.
32 devices in a mesh: span: 8 (over z, y), seq: 4 (over x, core).
Axes of the slice: x: 2, y: 2, z: 4, core: 2. Of those that a mesh axis runs over, the one named last changes fastest.
Arguments:
- queries: bfloat16 [6144, 2560], P(('span', 'seq')), may hold values from -32 to 32
- keys: bfloat16 [6144, 2560], P(('span', 'seq')), may hold values from -32 to 32
- values: bfloat16 [6144, 2560], P(('span', 'seq')), may hold values from -6 to 6
- level_index: int32 [8], replicated, may hold values from 0 to 3
- plan: int32 [4], replicated, may hold values from 0 to 999
- gate_weight: float32 [256, 2560], replicated, may hold values from -0.375 to 0.375
Outputs:
- gated: bfloat16 [6144, 2560], P(('span', 'seq'))
All inputs are finite; a program needn't handle non-finite values.
Results may differ from a plain program's by a relative error of at most 0.009.
Values may be sent and summed in bfloat16 or wider, within the bound.
No kernel may reach another device: no remote copies, remote signals or barrier semaphores. Data moves between devices by JAX's collectives and lax.ppermute only.
A program may use at most 192 MiB of HBM per device.

v0:
```python
import math

import jax
import jax.numpy as jnp
from jax import lax
from jax.sharding import PartitionSpec as P

HEAD_DIM = 128
WINDOW = 4


def from_behind(block, axis, distance):
    devices = range(lax.axis_size(axis))
    route = [(i - distance, i) for i in devices if i - distance in devices]
    return lax.ppermute(block, axis, route)


def timestep_gate(level_index, plan, gate_weight, span_number):
    noise_level = jnp.sum(
        jnp.where(jnp.arange(level_index.shape[0], dtype=jnp.int32) == span_number, level_index, 0)
    )
    timestep = jnp.sum(
        jnp.where(jnp.arange(plan.shape[0], dtype=jnp.int32) == noise_level, plan, 0)
    )
    half_freq = gate_weight.shape[0] // 2
    frequencies = jnp.exp(-math.log(10000.0) * jnp.arange(half_freq, dtype=jnp.float32) / half_freq)
    angles = timestep.astype(jnp.float32) * frequencies
    embedding = jnp.concatenate([jnp.cos(angles), jnp.sin(angles)])[None, :]
    return jnp.dot(
        embedding, gate_weight, precision=lax.Precision.HIGHEST, preferred_element_type=jnp.float32
    )[0]


def attend(running, query_heads, key_heads, value_heads, usable):
    row_peak, denominator, numerator = running
    score_scale = 1.0 / math.sqrt(query_heads.shape[-1])
    scores = (
        jnp.einsum("qhd,khd->qhk", query_heads, key_heads, preferred_element_type=jnp.float32)
        * score_scale
    )
    new_peak = jnp.maximum(row_peak, jnp.max(scores, axis=2))
    rescale = jnp.exp(row_peak - new_peak)
    weights = jnp.exp(scores - new_peak[:, :, None]).astype(jnp.bfloat16)
    new_denominator = denominator * rescale + jnp.sum(weights.astype(jnp.float32), axis=2)
    new_numerator = numerator * rescale[:, :, None] + jnp.einsum(
        "qhk,khd->qhd", weights, value_heads, preferred_element_type=jnp.float32
    )
    return (
        jnp.where(usable, new_peak, row_peak),
        jnp.where(usable, new_denominator, denominator),
        jnp.where(usable, new_numerator, numerator),
    )


def shards(queries, keys, values, level_index, plan, gate_weight):
    span_number = lax.axis_index("span")
    gate_values = timestep_gate(level_index, plan, gate_weight, span_number)
    key_part, value_part = (
        lax.all_gather(keys, "seq", axis=0, tiled=True),
        lax.all_gather(values, "seq", axis=0, tiled=True),
    )
    query_rows = queries.shape[0]
    head_group = queries.shape[1] // HEAD_DIM

    def as_heads(block):
        return block.reshape(block.shape[0], head_group, HEAD_DIM)

    query_heads = as_heads(queries)
    running = (
        jnp.full((query_rows, head_group), -jnp.inf, jnp.float32),
        jnp.zeros((query_rows, head_group), jnp.float32),
        jnp.zeros((query_rows, head_group, HEAD_DIM), jnp.float32),
    )
    running = attend(running, query_heads, as_heads(key_part), as_heads(value_part), True)
    key_value = jnp.stack([key_part, value_part])
    earlier = key_value
    for distance in range(1, WINDOW + 1):
        earlier = from_behind(earlier, "span", 1)
        running = attend(
            running,
            query_heads,
            as_heads(earlier[0]),
            as_heads(earlier[1]),
            span_number >= distance,
        )
    row_peak, denominator, numerator = running
    attended = (
        (numerator / denominator[:, :, None])
        .reshape(query_rows, head_group * HEAD_DIM)
        .astype(jnp.bfloat16)
    )
    return (gate_values[None, :] * attended.astype(jnp.float32)).astype(jnp.bfloat16)


def solution(mesh):
    in_specs = (
        P(("span", "seq"), None),
        P(("span", "seq"), None),
        P(("span", "seq"), None),
        P(),
        P(),
        P(),
    )
    out_specs = P(("span", "seq"), None)
    return jax.shard_map(shards, mesh=mesh, in_specs=in_specs, out_specs=out_specs, check_vma=False)
```

profile of v0, /device:TPU:8, one launch (start us, length us, event | category | flops | bytes accessed | tf_op | source)
XLA Modules:
  0.0 859.5 jit_solution(3992450863860079158)
XLA Ops:
  8.0 35.1 %all-gather.5.cloned.1.call-done = bf16[768,2560]{1,0:T(8,128)(2,1)} async-done(((bf16[192,2560]{1,0:T(8,128)(2,1)}), bf16[768,2560]{1,0:T(8,128)(2,1)}) %all-gather.5.cloned.1.call-update) | async-done | bytes 3932176 | tf_op jit(solution)/shard_map/all_gather | solution.py:60
  43.1 6.3 copy.33
  49.4 28.3 %all-gather.3.cloned.1.call-done = bf16[768,2560]{1,0:T(8,128)(2,1)} async-done(((bf16[192,2560]{1,0:T(8,128)(2,1)}), bf16[768,2560]{1,0:T(8,128)(2,1)}) %all-gather.3.cloned.1.call-update) | async-done | bytes 3932176 | tf_op jit(solution)/shard_map/all_gather | solution.py:59
  77.7 6.2 copy.30
  83.9 7.1 pad_maximum_fusion
  94.4 171.0 %collective-permute-done = bf16[2,768,2560]{1,2,0:T(8,128)(2,1)S(1)} collective-permute-done((bf16[2,768,2560]{1,2,0:T(8,128)(2,1)}, bf16[2,768,2560]{1,2,0:T(8,128)(2,1)S(1)}, u32[]{:S(2)}, u32[]{:S(2)}) %collective-permute-start) | collective-permute-done | bytes 7864352 | tf_op jit(solution)/shard_map/ppermute | solution.py:15
  270.9 171.0 %collective-permute-done.1 = bf16[2,768,2560]{1,2,0:T(8,128)(2,1)} collective-permute-done((bf16[2,768,2560]{1,2,0:T(8,128)(2,1)S(1)}, bf16[2,768,2560]{1,2,0:T(8,128)(2,1)}, u32[]{:S(2)}, u32[]{:S(2)}) %collective-permute-start.1) | collective-permute-done | bytes 7864352 | tf_op jit(solution)/shard_map/ppermute | solution.py:15
  443.8 170.8 %collective-permute-done.2 = bf16[2,768,2560]{1,2,0:T(8,128)(2,1)} collective-permute-done((bf16[2,768,2560]{1,2,0:T(8,128)(2,1)}, bf16[2,768,2560]{1,2,0:T(8,128)(2,1)}, u32[]{:S(2)}, u32[]{:S(2)}) %collective-permute-start.2) | collective-permute-done | bytes 7864352 | tf_op jit(solution)/shard_map/ppermute | solution.py:15
  624.7 4.4 copy-done.2
  632.0 8.1 fusion.27
  640.1 4.9 fusion.51
  646.8 4.9 fusion.52
  651.7 5.9 bitcast_reduce_fusion.2
  657.6 4.9 fusion.54
  662.5 6.1 bitcast_reduce_fusion.1
  668.6 117.8 %collective-permute-done.3 = bf16[2,768,2560]{1,2,0:T(8,128)(2,1)} collective-permute-done((bf16[2,768,2560]{1,2,0:T(8,128)(2,1)}, bf16[2,768,2560]{1,2,0:T(8,128)(2,1)}, u32[]{:S(2)}, u32[]{:S(2)}) %collective-permute-start.3) | collective-permute-done | bytes 7864352 | tf_op jit(solution)/shard_map/ppermute | solution.py:15
  786.4 4.8 fusion.53
  791.2 6.0 bitcast_reduce_fusion
  797.2 9.2 %fusion.31 = f32[20,128,192]{1,2,0:T(8,128)} fusion(bf16[768,20,128]{0,2,1:T(8,128)(2,1)} %bitcast.166, f32[20,768,192]{1,2,0:T(8,128)} %get-tuple-element.30, f32[192,20]{0,1:T(8,128)S(1)} %get-tuple-element.13), kind=kOutput, calls=%fused_computation.53 | convolution fusion | flops 763822080 | bytes 17710080 | tf_op jit(solution)/shard_map/qhk,khd->qhd/dot_general | solution.py:45
  806.4 7.7 convert_reduce_fusion.2
  814.1 5.8 fusion.29
  819.9 9.4 %fusion.33 = f32[20,128,192]{1,2,0:T(8,128)} fusion(bf16[768,20,128]{0,2,1:T(8,128)(2,1)} %bitcast.165, f32[20,768,192]{1,2,0:T(8,128)} %get-tuple-element.28, f32[192,20]{0,1:T(8,128)S(1)} %get-tuple-element.11), kind=kOutput, calls=%fused_computation.54 | convolution fusion | flops 763822080 | bytes 17710080 | tf_op jit(solution)/shard_map/qhk,khd->qhd/dot_general | solution.py:45
  829.3 10.8 %convert_reduce_fusion = (f32[192,20]{0,1:T(8,128)S(1)}, f32[192,20]{0,1:T(8,128)S(1)}) fusion(f32[192,20]{0,1:T(8,128)S(1)} %get-tuple-element.10, f32[20,768,192]{1,2,0:T(8,128)} %get-tuple-element.26, f32[192,20]{0,1:T(8,128)S(1)} %get-tuple-element.11, f32[20,768,192]{1,2,0:T(8,128)} %get-tuple-element.28), kind=kLoop, calls=%fused_computation.20 | loop fusion | flops 29483520 | bytes 23654400 | tf_op jit(solution)/shard_map/reduce_sum | solution.py:44
  841.1 8.9 %convert_bitcast_fusion = f32[20,24,8,128]{3,2,1,0:T(8,128)} fusion(bf16[768,20,128]{0,2,1:T(8,128)(2,1)S(1)} %bitcast.171, f32[20,128,192]{1,2,0:T(8,128)} %fusion.33, f32[20,128,192]{1,2,0:T(8,128)S(1)} %copy-done.8, f32[20,128,192]{1,2,0:T(8,128)S(1)} %copy-done.9, f32[20,192,128]{2,1,0:T(8,128)S(1)} %copy-done.7, f32[192,20]{0,1:T(8,128)S(1)} %get-tuple-element.5, ...), kind=kOutput, calls=%fused_computation.39 | convolution fusion | flops 771686400 | bytes 25666564 | tf_op jit(solution)/shard_map/qhk,khd->qhd/dot_general | solution.py:45
  (49 shorter events, 30.0 us)
Async XLA Ops:
  6.5 612.6 %copy-start = (f32[256,2560]{1,0:T(8,128)S(1)}, f32[256,2560]{1,0:T(8,128)}, u32[]{:S(2)}) copy-start(f32[256,2560]{1,0:T(8,128)} %param.11) | copy-start | bytes 7864324
  6.5 36.6 %all-gather.5.cloned.1.call-start = ((), (), s32[]{:S(2)}) async-start(), calls=%async_computation.1 | async-start | bytes 4915200 | tf_op jit(solution)/shard_map/all_gather | solution.py:60
  7.3 70.4 %all-gather.3.cloned.1.call-start = ((), (), s32[]{:S(2)}) async-start(), calls=%async_computation | async-start | bytes 4915200 | tf_op jit(solution)/shard_map/all_gather | solution.py:59
  83.9 532.6 %copy-start.10 = (s32[8]{0:T(128)S(1)}, s32[8]{0:T(128)}, u32[]{:S(2)}) copy-start(s32[8]{0:T(128)} %param.9) | copy-start | bytes 100
  83.9 533.3 %copy-start.11 = (s32[4]{0:T(128)S(1)}, s32[4]{0:T(128)}, u32[]{:S(2)}) copy-start(s32[4]{0:T(128)} %param.10) | copy-start | bytes 52
  91.0 174.4 %collective-permute-start = (bf16[2,768,2560]{1,2,0:T(8,128)(2,1)}, bf16[2,768,2560]{1,2,0:T(8,128)(2,1)S(1)}, u32[]{:S(2)}, u32[]{:S(2)}) collective-permute-start(bf16[2,768,2560]{1,2,0:T(8,128)(2,1)} %pad_maximum_fusion), channel_id=1, source_target_pairs={{0,4},{4,8},{8,12},{12,16},{16,20},{20,24},{24,28},{1,5},{5,9},{9,... | collective-permute-start | bytes 23592968 | tf_op jit(solution)/shard_map/ppermute | solution.py:15
  265.3 3.1 copy-start.5
  268.4 173.4 %collective-permute-start.1 = (bf16[2,768,2560]{1,2,0:T(8,128)(2,1)S(1)}, bf16[2,768,2560]{1,2,0:T(8,128)(2,1)}, u32[]{:S(2)}, u32[]{:S(2)}) collective-permute-start(bf16[2,768,2560]{1,2,0:T(8,128)(2,1)S(1)} %collective-permute-done), channel_id=1, source_target_pairs={{0,4},{4,8},{8,12},{12,16},{16,20},{20,24},{24,28},{1,5},{5,9},{9,... | collective-permute-start | bytes 23592968 | tf_op jit(solution)/shard_map/ppermute | solution.py:15
  441.9 172.7 %collective-permute-start.2 = (bf16[2,768,2560]{1,2,0:T(8,128)(2,1)}, bf16[2,768,2560]{1,2,0:T(8,128)(2,1)}, u32[]{:S(2)}, u32[]{:S(2)}) collective-permute-start(bf16[2,768,2560]{1,2,0:T(8,128)(2,1)} %collective-permute-done.1), channel_id=1, source_target_pairs={{0,4},{4,8},{8,12},{12,16},{16,20},{20,24},{24,28},{1,5},{5,9},{9,... | collective-permute-start | bytes 23592968 | tf_op jit(solution)/shard_map/ppermute | solution.py:15
  614.6 171.8 %collective-permute-start.3 = (bf16[2,768,2560]{1,2,0:T(8,128)(2,1)}, bf16[2,768,2560]{1,2,0:T(8,128)(2,1)}, u32[]{:S(2)}, u32[]{:S(2)}) collective-permute-start(bf16[2,768,2560]{1,2,0:T(8,128)(2,1)} %collective-permute-done.2), channel_id=1, source_target_pairs={{0,4},{4,8},{8,12},{12,16},{16,20},{20,24},{24,28},{1,5},{5,9},{9,... | collective-permute-start | bytes 23592968 | tf_op jit(solution)/shard_map/ppermute | solution.py:15
  624.7 4.4 copy-start.2
  629.1 2.9 copy-start.3
  640.1 5.0 copy-start.4
  819.9 20.3 %slice-start = ((s8[11796480]{0:T(1024)(128)(4,1)}), s8[3407872]{0:T(1024)(128)(4,1)S(1)}, s32[]{:S(2)}) async-start(s8[11796480]{0:T(1024)(128)(4,1)} %bitcast.158), calls=%async_computation.2 | async-start | bytes 6815744
  819.9 20.3 %slice-start.1 = ((s8[11796480]{0:T(1024)(128)(4,1)}), s8[4194304]{0:T(1024)(128)(4,1)S(1)}, s32[]{:S(2)}) async-start(s8[11796480]{0:T(1024)(128)(4,1)} %bitcast.158), calls=%async_computation.3 | async-start | bytes 8388608
  829.3 10.9 %slice-start.2 = ((s8[11796480]{0:T(1024)(128)(4,1)}), s8[4194304]{0:T(1024)(128)(4,1)S(1)}, s32[]{:S(2)}) async-start(s8[11796480]{0:T(1024)(128)(4,1)} %bitcast.158), calls=%async_computation.4 | async-start | bytes 8388608
  829.3 10.9 %copy-start.6 = (bf16[1,768,2560]{1,2,0:T(8,128)(2,1)S(1)}, bf16[1,768,2560]{1,2,0:T(8,128)(2,1)}, u32[]{:S(2)}) copy-start(bf16[1,768,2560]{1,2,0:T(8,128)(2,1)} %get-tuple-element.21) | copy-start | bytes 11796484
  829.3 10.9 %copy-start.7 = (f32[20,192,128]{2,1,0:T(8,128)S(1)}, f32[20,192,128]{2,1,0:T(8,128)}, u32[]{:S(2)}) copy-start(f32[20,192,128]{2,1,0:T(8,128)} %fusion.27) | copy-start | bytes 5898244
  829.3 11.3 %copy-start.8 = (f32[20,128,192]{1,2,0:T(8,128)S(1)}, f32[20,128,192]{1,2,0:T(8,128)}, u32[]{:S(2)}) copy-start(f32[20,128,192]{1,2,0:T(8,128)} %fusion.31) | copy-start | bytes 5898244
  829.3 11.8 %copy-start.9 = (f32[20,128,192]{1,2,0:T(8,128)S(1)}, f32[20,128,192]{1,2,0:T(8,128)}, u32[]{:S(2)}) copy-start(f32[20,128,192]{1,2,0:T(8,128)} %fusion.29) | copy-start | bytes 5898244
  841.1 11.6 %copy-start.1 = (f32[256,2560]{1,0:T(8,128)S(1)}, f32[256,2560]{1,0:T(8,128)}, u32[]{:S(2)}) copy-start(f32[256,2560]{1,0:T(8,128)} %param.11) | copy-start | bytes 7864324
Sparse Core Ops, SparseCore 0:
  8.9 34.1 all-gather.4
  44.7 32.9 all-gather.2
where the time goes:
time: 860 us
  waiting for transfers between devices  695 us (81%)
  matrix products  66.7 us (8%)
  local copies, waits for them, and re-layouts  40.4 us (5%)
  other arithmetic  33.1 us (4%)
  between operations  14.2 us (2%)
  starting transfers between devices  9.7 us (1%)
    ppermute x4, waiting for transfers between devices, from_behind(): return lax.ppermute(block, axis, route)  631 us
    dot_general x5, matrix products, attend(): jnp.einsum('qhk,khd->qhd', weights, value_heads, preferred_element_type=j...  41.4 us
    all_gather x1, waiting for transfers between devices, shards(): lax.all_gather(values, 'seq', axis=0, tiled=True)  35.1 us
    all_gather x1, waiting for transfers between devices, shards(): lax.all_gather(keys, 'seq', axis=0, tiled=True)  28.3 us
    dot_general x5, matrix products, attend(): jnp.einsum('qhd,khd->qhk', query_heads, key_heads, preferred_element_type...  24 us
    reduce_sum x3, other arithmetic, attend(): jnp.sum(weights.astype(jnp.float32), axis=2)  21.3 us
  transfers between devices with their start and end apart: 6, of which 6 were waited for; matrix products, arithmetic and copies ran while one was open for 6% of the time, Pallas kernels for 0%

commit v1 on v0

v1 whole, which is shorter than its diff:
```python
import functools
import math

import jax
import jax.numpy as jnp
from jax import lax
from jax.experimental import pallas as pl
from jax.experimental.pallas import tpu as pltpu
from jax.sharding import PartitionSpec as P

HEAD_DIM = 128
AXES = ("span", "seq")
ANY = pl.BlockSpec(memory_space=pl.ANY)
SMEM = pl.BlockSpec(memory_space=pltpu.SMEM)
VMEM_LIMIT = 48 * 1024 * 1024
NT = (((1,), (1,)), ((), ()))
NN = (((1,), (0,)), ((), ()))


def params():
    return pltpu.CompilerParams(vmem_limit_bytes=VMEM_LIMIT)


def move(block, target):
    spans, members = lax.axis_size("span"), lax.axis_size("seq")
    route = []
    for device in range(spans * members):
        span, member = divmod(device, members)
        to_span, to_member = target(span, member)
        if 0 <= to_span < spans:
            route.append((device, to_span * members + to_member))
    return lax.ppermute(block, AXES, route)


def within_level(dx, dy):
    return lambda span, member: (span ^ dy, member ^ (2 * dx))


def other_core(span, member):
    return span, member ^ 1


def one_up(span, member):
    return span + 2, member


def one_down(span, member):
    return span - 2, member


PLACES = ((0, 0), (0, 1), (1, 0), (1, 1))


def timestep_gate(level_index, plan, gate_weight, span_number):
    noise_level = jnp.sum(
        jnp.where(jnp.arange(level_index.shape[0], dtype=jnp.int32) == span_number, level_index, 0)
    )
    timestep = jnp.sum(
        jnp.where(jnp.arange(plan.shape[0], dtype=jnp.int32) == noise_level, plan, 0)
    )
    half_freq = gate_weight.shape[0] // 2
    frequencies = jnp.exp(-math.log(10000.0) * jnp.arange(half_freq, dtype=jnp.float32) / half_freq)
    angles = timestep.astype(jnp.float32) * frequencies
    embedding = jnp.concatenate([jnp.cos(angles), jnp.sin(angles)])[None, :]
    return jnp.dot(
        embedding, gate_weight, precision=lax.Precision.HIGHEST, preferred_element_type=jnp.float32
    )


def pack_kernel(start, width, group_width, meta, q, k, v, *rest):
    outs, sems = rest[:4], rest[4]
    copies = []
    for j in range(4):
        column = pl.multiple_of(meta[j] * group_width + start, HEAD_DIM)
        for t, ref in enumerate((q, k, v)):
            copy = pltpu.make_async_copy(
                ref.at[:, pl.ds(column, width)],
                outs[j].at[:, pl.ds(t * width, width)],
                sems.at[j, t],
            )
            copy.start()
            copies.append(copy)
    for copy in copies:
        copy.wait()


def pack(meta, q, k, v, start, width, group_width):
    rows = q.shape[0]
    return pl.pallas_call(
        functools.partial(pack_kernel, start, width, group_width),
        out_shape=[jax.ShapeDtypeStruct((rows, 3 * width), q.dtype)] * 4,
        in_specs=[SMEM, ANY, ANY, ANY],
        out_specs=[ANY] * 4,
        scratch_shapes=[pltpu.SemaphoreType.DMA((4, 3))],
        compiler_params=params(),
        cost_estimate=pl.CostEstimate(flops=0, bytes_accessed=24 * rows * width * 2, transcendentals=0),
        name="pack",
    )(meta, q, k, v)


def stack_kernel(width, meta, *refs):
    pieces, (q_out, kv_out, sems) = refs[:4], refs[4:]
    rows = pieces[0].shape[0]
    copies = []
    for j, (dx, _) in enumerate(PLACES):
        parity = meta[4 + j]
        at = pl.ds(dx * rows, rows)
        for t, (source, target) in enumerate(
            (
                (pieces[j].at[:, pl.ds(width, 2 * width)], kv_out.at[parity, at]),
                (pieces[j].at[:, pl.ds(0, width)], q_out.at[parity, at]),
            )
        ):
            copy = pltpu.make_async_copy(source, target, sems.at[j, t])
            copy.start()
            copies.append(copy)
    for copy in copies:
        copy.wait()


def stack(meta, pieces, width):
    rows = pieces[0].shape[0]
    dtype = pieces[0].dtype
    return pl.pallas_call(
        functools.partial(stack_kernel, width),
        out_shape=[
            jax.ShapeDtypeStruct((2, 2 * rows, width), dtype),
            jax.ShapeDtypeStruct((2, 2 * rows, 2 * width), dtype),
        ],
        in_specs=[SMEM] + [ANY] * 4,
        out_specs=[ANY] * 2,
        scratch_shapes=[pltpu.SemaphoreType.DMA((4, 2))],
        compiler_params=params(),
        cost_estimate=pl.CostEstimate(flops=0, bytes_accessed=24 * rows * width * 2, transcendentals=0),
        name="stack",
    )(meta, *pieces)


def softmax_part(q, keys, values):
    scale = math.log2(math.e) / math.sqrt(HEAD_DIM)
    scores = [lax.dot_general(q, k, NT, preferred_element_type=jnp.float32) for k in keys]
    peak = functools.reduce(jnp.maximum, scores).max(axis=1, keepdims=True)
    peak = peak * scale
    weights = [jnp.exp2(s * scale - peak) for s in scores]
    total = functools.reduce(jnp.add, weights).sum(axis=1, keepdims=True)
    out = functools.reduce(
        jnp.add,
        [
            lax.dot_general(w.astype(jnp.bfloat16), v, NN, preferred_element_type=jnp.float32)
            for w, v in zip(weights, values)
        ],
    )
    return out / total, peak + jnp.log2(total)


def attend_rows(q_ref, p, pairs, o_ref, lse_ref, tile):
    rows = q_ref.shape[1]
    for start in range(0, rows, tile):
        at = pl.ds(start, tile)
        out, lse = softmax_part(
            q_ref[p, at], [k[i] for k, _, i in pairs], [v[i] for _, v, i in pairs]
        )
        o_ref[p, at] = out.astype(o_ref.dtype)
        lse_ref[0, :, pl.ds(p * rows + start, tile)] = jnp.broadcast_to(lse, (tile, 128)).T[:1]


TILE = 128


def remote_kernel(q, ka, va, kb, vb, o, lse):
    every = [(ka, va, 0), (kb, vb, 0), (ka, va, 1), (kb, vb, 1)]
    attend_rows(q, 0, every, o, lse, TILE)
    attend_rows(q, 1, every[2:], o, lse, TILE)


def own_kernel(meta, q, ka, va, kb, vb, ua, xa, ub, xb, o, lse):
    own = [(ka, va, 0), (kb, vb, 0), (ka, va, 1), (kb, vb, 1)]
    above = [(ua, xa, 0), (ub, xb, 0), (ua, xa, 1), (ub, xb, 1)]

    @pl.when(meta[8] >= 1)
    def _():
        attend_rows(q, 0, own[:2] + above, o, lse, TILE)
        attend_rows(q, 1, own + above, o, lse, TILE)

    @pl.when(meta[8] < 1)
    def _():
        attend_rows(q, 0, own[:2], o, lse, TILE)
        attend_rows(q, 1, own, o, lse, TILE)


def attention(body, meta, q, kvs, units, out_dtype, name):
    _, rows, width = q.shape
    heads = width // HEAD_DIM
    block = (2, rows, HEAD_DIM)
    head = pl.BlockSpec(block, lambda h: (0, 0, h))
    value = pl.BlockSpec(block, lambda h: (0, 0, heads + h))
    operands, specs = [], []
    if meta is not None:
        operands, specs = [meta], [SMEM]
    operands.append(q)
    specs.append(head)
    for kv in kvs:
        operands += [kv, kv]
        specs += [head, value]
    scores = heads * units * rows * 2 * rows
    return pl.pallas_call(
        body,
        grid=(heads,),
        out_shape=[
            jax.ShapeDtypeStruct((2, rows, width), out_dtype),
            jax.ShapeDtypeStruct((heads, 1, 2 * rows), jnp.float32),
        ],
        in_specs=specs,
        out_specs=[head, pl.BlockSpec((1, 1, 2 * rows), lambda h: (h, 0, 0))],
        compiler_params=params(),
        cost_estimate=pl.CostEstimate(
            flops=scores * HEAD_DIM * 4, bytes_accessed=4 * rows * width * 4, transcendentals=scores
        ),
        name=name,
    )(*operands)


def merge_kernel(meta, o, lse, o_far, lse_far, *rest):
    outs, scratch = rest[:4], rest[4]
    rows = o.shape[1]
    half = rows // 2
    far = jnp.where(meta[8] >= 2, 1.0, 0.0)
    share = far / (1.0 + jnp.exp2(lse[0] - lse_far[0]))
    for p in range(2):
        weight = jnp.broadcast_to(share[:, p * rows : (p + 1) * rows], (HEAD_DIM, rows)).T
        near = o[p].astype(jnp.float32)
        scratch[p] = near + weight * (o_far[p].astype(jnp.float32) - near)
    for j, (dx, _) in enumerate(PLACES):
        outs[j][...] = scratch[meta[4 + j], pl.ds(dx * half, half)].astype(outs[j].dtype)


def merge(meta, o, lse, o_far, lse_far):
    _, rows, width = o.shape
    heads = width // HEAD_DIM
    head = pl.BlockSpec((2, rows, HEAD_DIM), lambda h: (0, 0, h))
    row = pl.BlockSpec((1, 1, 2 * rows), lambda h: (h, 0, 0))
    return pl.pallas_call(
        merge_kernel,
        grid=(heads,),
        out_shape=[jax.ShapeDtypeStruct((rows // 2, width), jnp.bfloat16)] * 4,
        in_specs=[SMEM, head, row, head, row],
        out_specs=[pl.BlockSpec((rows // 2, HEAD_DIM), lambda h: (0, h))] * 4,
        scratch_shapes=[pltpu.VMEM((2, rows, HEAD_DIM), jnp.float32)],
        compiler_params=params(),
        cost_estimate=pl.CostEstimate(
            flops=8 * rows * width, bytes_accessed=20 * rows * width, transcendentals=0
        ),
        name="merge",
    )(meta, o, lse, o_far, lse_far)


def finish_kernel(starts, group_width, meta, gate, *refs):
    pieces, out = refs[:-1], refs[-1]
    for i, piece in enumerate(pieces):
        chunk, j = divmod(i, 4)
        width = piece.shape[1]
        at = pl.ds(pl.multiple_of(meta[j] * group_width + starts[chunk], HEAD_DIM), width)
        out[:, at] = (gate[:, at] * piece[...].astype(jnp.float32)).astype(out.dtype)


def finish(meta, gate, pieces, starts, group_width):
    rows = pieces[0].shape[0]
    whole = pl.BlockSpec(memory_space=pltpu.VMEM)
    return pl.pallas_call(
        functools.partial(finish_kernel, starts, group_width),
        out_shape=jax.ShapeDtypeStruct((rows, 4 * group_width), jnp.bfloat16),
        in_specs=[SMEM] + [whole] * (1 + len(pieces)),
        out_specs=whole,
        compiler_params=params(),
        cost_estimate=pl.CostEstimate(
            flops=rows * group_width * 4, bytes_accessed=rows * group_width * 16, transcendentals=0
        ),
        name="finish",
    )(meta, gate, *pieces)


def shards(queries, keys, values, level_index, plan, gate_weight):
    span = lax.axis_index("span")
    member = lax.axis_index("seq")
    x, y = member // 2, span % 2
    group_width = queries.shape[1] // 4
    group_heads = group_width // HEAD_DIM
    meta = jnp.stack(
        [2 * (x ^ dx) + (y ^ dy) for dx, dy in PLACES]
        + [y ^ dy for _, dy in PLACES]
        + [span // 2]
    ).astype(jnp.int32)
    gate = timestep_gate(level_index, plan, gate_weight, span)

    sizes = []
    while sum(sizes) < group_heads:
        sizes.append(min(2 if sizes else 1, group_heads - sum(sizes)))
    starts = [sum(sizes[:i]) * HEAD_DIM for i in range(len(sizes))]

    results = []
    for size, start in zip(sizes, starts):
        width = size * HEAD_DIM
        sent = pack(meta, queries, keys, values, start, width, group_width)
        pieces = [sent[0]] + [move(sent[j], within_level(*PLACES[j])) for j in (1, 2, 3)]
        q, kv = stack(meta, pieces, width)
        kv_up = move(kv, one_up)
        q_down = move(q, one_down)
        kv_other = move(kv, other_core)
        kv_up_other = move(kv_up, other_core)
        o_part, lse_part = attention(
            remote_kernel, None, q_down, (kv_up, kv_up_other), 3, jnp.bfloat16, "remote"
        )
        o_far, lse_far = move(o_part, one_up), move(lse_part, one_up)
        o, lse = attention(
            own_kernel, meta, q, (kv, kv_other, kv_up, kv_up_other), 7, jnp.float32, "own"
        )
        merged = merge(meta, o, lse, o_far, lse_far)
        results += [merged[0]] + [move(merged[j], within_level(*PLACES[j])) for j in (1, 2, 3)]
    return finish(meta, gate, results, starts, group_width)


def solution(mesh):
    rows = P(AXES, None)
    return jax.shard_map(
        shards,
        mesh=mesh,
        in_specs=(rows, rows, rows, P(), P(), P()),
        out_specs=rows,
        check_vma=False,
    )
```

time: 860 us -> 168 us (0.20)
  waiting for transfers between devices: 695 us -> 43.6 us
  matrix products: 66.7 us -> 1.34 us
  Pallas kernels: 0 us -> 53.9 us
  starting transfers between devices: 9.7 us -> 57.1 us
  local copies, waits for them, and re-layouts: 40.4 us -> 8.57 us
  other arithmetic: 33.1 us -> 1.84 us
  between operations: 14.2 us -> 1.11 us
    ppermute x4 -> x36, waiting for transfers between devices: 631 us -> 43.6 us  [move(): return lax.ppermute(block, AXES, route)]
    dot_general x10 -> x0, matrix products: 65.4 us -> none  [the longest x5 41.4 us: attend(): jnp.einsum('qhk,khd->qhd', weights, value_heads, preferred_element_type=j...]
    all_gather x2 -> x0, waiting for transfers between devices: 63.4 us -> none  [the longest x1 35.1 us: shards(): lax.all_gather(values, 'seq', axis=0, tiled=True)]
    pallas_call x0 -> x16, Pallas kernels: none -> 53.9 us  [the longest x6 43.1 us: attention(): pl.pallas_call(body, grid=(heads,), out_shape=[jax.ShapeDtypeStruct((2, r...]
    ppermute x4 -> x36, starting transfers between devices: 9.66 us -> 57.1 us  [move(): return lax.ppermute(block, AXES, route)]
    reduce_sum x3 -> x0, other arithmetic: 21.3 us -> none  [attend(): jnp.sum(weights.astype(jnp.float32), axis=2)]
    slice x4 -> x0, local copies, waits for them, and re-layouts: 19.5 us -> none  [the longest x2 9.82 us: shards(): earlier[1]]
    all_gather x2 -> x0, local copies, waits for them, and re-layouts: 12.4 us -> none  [the longest x1 6.27 us: shards(): lax.all_gather(values, 'seq', axis=0, tiled=True)]
  transfers between devices with their start and end apart: 6 -> 36, of which waited for: 6 -> 12; matrix products, arithmetic and copies ran while one was open for 6% -> 2% of each run, Pallas kernels for 0% -> 30%
where the time goes in v1:
time: 168 us; the launch traced here: 167 us
  starting transfers between devices  57.1 us (34%)
  Pallas kernels  53.9 us (32%)
  waiting for transfers between devices  43.6 us (26%)
  local copies, waits for them, and re-layouts  8.57 us (5%)
  other arithmetic  1.84 us (1%)
    ppermute x36, starting transfers between devices, move(): return lax.ppermute(block, AXES, route)  57.1 us
    ppermute x36, waiting for transfers between devices, move(): return lax.ppermute(block, AXES, route)  43.6 us
    pallas_call x6, Pallas kernels, attention(): pl.pallas_call(body, grid=(heads,), out_shape=[jax.ShapeDtypeStruct((2, r...  43.1 us
    unnamed x52, local copies, waits for them, and re-layouts  8.49 us
    pallas_call x3, Pallas kernels, stack(): pl.pallas_call(functools.partial(stack_kernel, width), out_shape=[jax.Sha...  3.73 us
  transfers between devices with their start and end apart: 36, of which 12 were waited for; matrix products, arithmetic and copies ran while one was open for 2% of the time, Pallas kernels for 30%

profile of v1, /device:TPU:8, one launch (start us, length us, event | category | flops | bytes accessed | tf_op | source)
XLA Modules:
  0.0 167.5 jit_solution(5240554531719962782)
XLA Ops:
  8.2 5.5 %collective-permute-done.12.refs_1_ = bf16[192,768]{1,0:T(8,128)(2,1)S(1)} collective-permute-done((bf16[192,768]{1,0:T(8,128)(2,1)S(1)}, bf16[192,768]{1,0:T(8,128)(2,1)S(1)}, u32[]{:S(2)}, u32[]{:S(2)}) %collective-permute-start.12) | collective-permute-done | bytes 294944 | tf_op jit(solution)/shard_map/ppermute | solution.py:32
  13.7 2.4 %collective-permute-done.13.refs_2_ = bf16[192,768]{1,0:T(8,128)(2,1)S(1)} collective-permute-done((bf16[192,768]{1,0:T(8,128)(2,1)S(1)}, bf16[192,768]{1,0:T(8,128)(2,1)S(1)}, u32[]{:S(2)}, u32[]{:S(2)}) %collective-permute-start.13) | collective-permute-done | bytes 294944 | tf_op jit(solution)/shard_map/ppermute | solution.py:32
  16.2 4.8 %collective-permute-done.14.refs_3_ = bf16[192,768]{1,0:T(8,128)(2,1)S(1)} collective-permute-done((bf16[192,768]{1,0:T(8,128)(2,1)S(1)}, bf16[192,768]{1,0:T(8,128)(2,1)S(1)}, u32[]{:S(2)}, u32[]{:S(2)}) %collective-permute-start.14) | collective-permute-done | bytes 294944 | tf_op jit(solution)/shard_map/ppermute | solution.py:32
  22.5 3.5 %collective-permute-start.16 = (bf16[2,384,512]{2,1,0:T(8,128)(2,1)}, bf16[2,384,512]{2,1,0:T(8,128)(2,1)S(1)}, u32[]{:S(2)}, u32[]{:S(2)}) collective-permute-start(bf16[2,384,512]{2,1,0:T(8,128)(2,1)} %get-tuple-element.66.ka.va), channel_id=1, source_target_pairs={{0,8},{1,9},{2,10},{3,11},{4,12},{5,13},{6,14},{7,15},{8,16},{9,17... | collective-permute-start | bytes 2359304 | tf_op jit(solution)/shard_map/ppermute | solution.py:32
  32.8 6.7 %collective-permute-done.24.refs_1_ = bf16[192,768]{1,0:T(8,128)(2,1)S(1)} collective-permute-done((bf16[192,768]{1,0:T(8,128)(2,1)S(1)}, bf16[192,768]{1,0:T(8,128)(2,1)S(1)}, u32[]{:S(2)}, u32[]{:S(2)}) %collective-permute-start.24) | collective-permute-done | bytes 294944 | tf_op jit(solution)/shard_map/ppermute | solution.py:32
  42.5 2.2 %collective-permute-done.26.refs_3_ = bf16[192,768]{1,0:T(8,128)(2,1)S(1)} collective-permute-done((bf16[192,768]{1,0:T(8,128)(2,1)S(1)}, bf16[192,768]{1,0:T(8,128)(2,1)S(1)}, u32[]{:S(2)}, u32[]{:S(2)}) %collective-permute-start.26) | collective-permute-done | bytes 294944 | tf_op jit(solution)/shard_map/ppermute | solution.py:32
  46.2 3.5 %collective-permute-start.28 = (bf16[2,384,512]{2,1,0:T(8,128)(2,1)}, bf16[2,384,512]{2,1,0:T(8,128)(2,1)}, u32[]{:S(2)}, u32[]{:S(2)}) collective-permute-start(bf16[2,384,512]{2,1,0:T(8,128)(2,1)} %get-tuple-element.80.ka.va), channel_id=1, source_target_pairs={{0,8},{1,9},{2,10},{3,11},{4,12},{5,13},{6,14},{7,15},{8,16},{9,17... | collective-permute-start | bytes 2359304 | tf_op jit(solution)/shard_map/ppermute | solution.py:32
  52.5 3.9 %collective-permute-start.6 = (bf16[2,384,128]{2,1,0:T(8,128)(2,1)S(1)}, bf16[2,384,128]{2,1,0:T(8,128)(2,1)S(1)}, u32[]{:S(2)}, u32[]{:S(2)}) collective-permute-start(bf16[2,384,128]{2,1,0:T(8,128)(2,1)S(1)} %get-tuple-element.51.q), channel_id=1, source_target_pairs={{8,0},{9,1},{10,2},{11,3},{12,4},{13,5},{14,6},{15,7},{16,8},{17,9... | collective-permute-start | bytes 589832 | tf_op jit(solution)/shard_map/ppermute | solution.py:32
  57.1 13.2 %collective-permute-done.4.ua.xa.ka.va = bf16[2,384,256]{2,1,0:T(8,128)(2,1)S(1)} collective-permute-done((bf16[2,384,256]{2,1,0:T(8,128)(2,1)S(1)}, bf16[2,384,256]{2,1,0:T(8,128)(2,1)S(1)}, u32[]{:S(2)}, u32[]{:S(2)}) %collective-permute-start.4) | collective-permute-done | bytes 393248 | tf_op jit(solution)/shard_map/ppermute | solution.py:32
  70.9 1.9 %collective-permute-start.18 = (bf16[2,384,256]{2,1,0:T(8,128)(2,1)S(1)}, bf16[2,384,256]{2,1,0:T(8,128)(2,1)S(1)}, u32[]{:S(2)}, u32[]{:S(2)}) collective-permute-start(bf16[2,384,256]{2,1,0:T(8,128)(2,1)S(1)} %get-tuple-element.65.q), channel_id=1, source_target_pairs={{8,0},{9,1},{10,2},{11,3},{12,4},{13,5},{14,6},{15,7},{16,8},{17,9... | collective-permute-start | bytes 1179656 | tf_op jit(solution)/shard_map/ppermute | solution.py:32
  74.0 2.7 %remote.3 = (bf16[2,384,128]{2,1,0:T(8,128)(2,1)S(1)}, f32[1,1,768]{2,1,0:T(1,128)S(1)}) custom-call(bf16[2,384,128]{2,1,0:T(8,128)(2,1)S(1)} %collective-permute-done.6.q, bf16[2,384,256]{2,1,0:T(8,128)(2,1)S(1)} %collective-permute-done.4.ua.xa.ka.va, bf16[2,384,256]{2,1,0:T(8,128)(2,1)S(1)} %collective-permute-done.4.ua.xa.ka.va, ...), custom_call_target="tpu_custom_call" | custom-call | flops 452984832 | bytes 786432 | tf_op jit(solution)/shard_map/remote/pallas_call | solution.py:206
  79.0 4.8 %collective-permute-done.18.q = bf16[2,384,256]{2,1,0:T(8,128)(2,1)S(1)} collective-permute-done((bf16[2,384,256]{2,1,0:T(8,128)(2,1)S(1)}, bf16[2,384,256]{2,1,0:T(8,128)(2,1)S(1)}, u32[]{:S(2)}, u32[]{:S(2)}) %collective-permute-start.18) | collective-permute-done | bytes 393248 | tf_op jit(solution)/shard_map/ppermute | solution.py:32
  84.6 3.5 %collective-permute-start.8 = (f32[1,1,768]{2,1,0:T(1,128)S(1)}, f32[1,1,768]{2,1,0:T(1,128)S(1)}, u32[]{:S(2)}, u32[]{:S(2)}) collective-permute-start(f32[1,1,768]{2,1,0:T(1,128)S(1)} %get-tuple-element.56), channel_id=1, source_target_pairs={{0,8},{1,9},{2,10},{3,11},{4,12},{5,13},{6,14},{7,15},{8,16},{9,17... | collective-permute-start | bytes 9224 | tf_op jit(solution)/shard_map/ppermute | solution.py:32
  90.1 2.2 %collective-permute-start.30 = (bf16[2,384,256]{2,1,0:T(8,128)(2,1)}, bf16[2,384,256]{2,1,0:T(8,128)(2,1)S(1)}, u32[]{:S(2)}, u32[]{:S(2)}) collective-permute-start(bf16[2,384,256]{2,1,0:T(8,128)(2,1)} %copy-done.15), channel_id=1, source_target_pairs={{8,0},{9,1},{10,2},{11,3},{12,4},{13,5},{14,6},{15,7},{16,8},{17,9... | collective-permute-start | bytes 1179656 | tf_op jit(solution)/shard_map/ppermute | solution.py:32
  92.3 3.6 %collective-permute-start.7 = (bf16[2,384,128]{2,1,0:T(8,128)(2,1)}, bf16[2,384,128]{2,1,0:T(8,128)(2,1)S(1)}, u32[]{:S(2)}, u32[]{:S(2)}) collective-permute-start(bf16[2,384,128]{2,1,0:T(8,128)(2,1)} %copy-done.23), channel_id=1, source_target_pairs={{0,8},{1,9},{2,10},{3,11},{4,12},{5,13},{6,14},{7,15},{8,16},{9,17... | collective-permute-start | bytes 589832 | tf_op jit(solution)/shard_map/ppermute | solution.py:32
  97.0 6.7 %remote.4 = (bf16[2,384,256]{2,1,0:T(8,128)(2,1)S(1)}, f32[2,1,768]{2,1,0:T(1,128)S(1)}) custom-call(bf16[2,384,256]{2,1,0:T(8,128)(2,1)S(1)} %copy-done.12, bf16[2,384,512]{2,1,0:T(8,128)(2,1)S(1)} %collective-permute-done.16.ua.xa.ka.va, bf16[2,384,512]{2,1,0:T(8,128)(2,1)S(1)} %collective-permute-done.16.ua.xa.ka.va, ...), custom_call_target="tpu_custom_call" | custom-call | flops 905969664 | bytes 1572864 | tf_op jit(solution)/shard_map/remote/pallas_call | solution.py:206
  103.7 3.5 %collective-permute-start.19 = (bf16[2,384,256]{2,1,0:T(8,128)(2,1)S(1)}, bf16[2,384,256]{2,1,0:T(8,128)(2,1)S(1)}, u32[]{:S(2)}, u32[]{:S(2)}) collective-permute-start(bf16[2,384,256]{2,1,0:T(8,128)(2,1)S(1)} %get-tuple-element.69), channel_id=1, source_target_pairs={{0,8},{1,9},{2,10},{3,11},{4,12},{5,13},{6,14},{7,15},{8,16},{9,17... | collective-permute-start | bytes 1179656 | tf_op jit(solution)/shard_map/ppermute | solution.py:32
  107.3 5.3 %own.3 = (f32[2,384,128]{2,1,0:T(8,128)S(1)}, f32[1,1,768]{2,1,0:T(1,128)S(1)}) custom-call(s32[9]{0:T(128)S(1)} %stack.36.meta, bf16[2,384,128]{2,1,0:T(8,128)(2,1)S(1)} %copy-done.22, bf16[2,384,256]{2,1,0:T(8,128)(2,1)S(1)} %copy-done.18, bf16[2,384,256]{2,1,0:T(8,128)(2,1)S(1)} %copy-done.18, bf16[2,384,256]{2,1,0:T(8,128)(2,1)S(1)} %copy-done.20, ...), custom_call_target="tpu_custom_call" | custom-call | flops 1056964608 | bytes 786432 | tf_op jit(solution)/shard_map/own/pallas_call | solution.py:206
  113.3 1.9 %collective-permute-start.20 = (f32[2,1,768]{2,1,0:T(1,128)S(1)}, f32[2,1,768]{2,1,0:T(1,128)S(1)}, u32[]{:S(2)}, u32[]{:S(2)}) collective-permute-start(f32[2,1,768]{2,1,0:T(1,128)S(1)} %get-tuple-element.70), channel_id=1, source_target_pairs={{0,8},{1,9},{2,10},{3,11},{4,12},{5,13},{6,14},{7,15},{8,16},{9,17... | collective-permute-start | bytes 18440 | tf_op jit(solution)/shard_map/ppermute | solution.py:32
  115.3 6.8 %remote.5 = (bf16[2,384,256]{2,1,0:T(8,128)(2,1)S(1)}, f32[2,1,768]{2,1,0:T(1,128)S(1)}) custom-call(bf16[2,384,256]{2,1,0:T(8,128)(2,1)S(1)} %collective-permute-done.30.q, bf16[2,384,512]{2,1,0:T(8,128)(2,1)} %collective-permute-done.28.ua.xa.ka.va, bf16[2,384,512]{2,1,0:T(8,128)(2,1)} %collective-permute-done.28.ua.xa.ka.va, ...), custom_call_target="tpu_custom_call" | custom-call | flops 905969664 | bytes 1572864 | tf_op jit(solution)/shard_map/remote/pallas_call | solution.py:206
  124.0 2.1 %collective-permute-start.32 = (f32[2,1,768]{2,1,0:T(1,128)S(1)}, f32[2,1,768]{2,1,0:T(1,128)S(1)}, u32[]{:S(2)}, u32[]{:S(2)}) collective-permute-start(f32[2,1,768]{2,1,0:T(1,128)S(1)} %get-tuple-element.84), channel_id=1, source_target_pairs={{0,8},{1,9},{2,10},{3,11},{4,12},{5,13},{6,14},{7,15},{8,16},{9,17... | collective-permute-start | bytes 18440 | tf_op jit(solution)/shard_map/ppermute | solution.py:32
  126.1 10.6 %own.4 = (f32[2,384,256]{2,1,0:T(8,128)S(1)}, f32[2,1,768]{2,1,0:T(1,128)S(1)}) custom-call(s32[9]{0:T(128)S(1)} %stack.36.meta, bf16[2,384,256]{2,1,0:T(8,128)(2,1)S(1)} %copy-done.14, bf16[2,384,512]{2,1,0:T(8,128)(2,1)} %get-tuple-element.66.ka.va, bf16[2,384,512]{2,1,0:T(8,128)(2,1)} %get-tuple-element.66.ka.va, ...), custom_call_target="tpu_custom_call" | custom-call | flops 2113929216 | bytes 1572864 | tf_op jit(solution)/shard_map/own/pallas_call | solution.py:206
  143.0 11.0 %own.5 = (f32[2,384,256]{2,1,0:T(8,128)S(1)}, f32[2,1,768]{2,1,0:T(1,128)S(1)}) custom-call(s32[9]{0:T(128)S(1)} %stack.36.meta, bf16[2,384,256]{2,1,0:T(8,128)(2,1)S(1)} %copy-done.16, bf16[2,384,512]{2,1,0:T(8,128)(2,1)} %get-tuple-element.80.ka.va, bf16[2,384,512]{2,1,0:T(8,128)(2,1)} %get-tuple-element.80.ka.va, ...), custom_call_target="tpu_custom_call" | custom-call | flops 2113929216 | bytes 1572864 | tf_op jit(solution)/shard_map/own/pallas_call | solution.py:206
  163.4 2.4 %collective-permute-done.35.refs_11_ = bf16[192,256]{1,0:T(8,128)(2,1)S(1)} collective-permute-done((bf16[192,256]{1,0:T(8,128)(2,1)S(1)}, bf16[192,256]{1,0:T(8,128)(2,1)S(1)}, u32[]{:S(2)}, u32[]{:S(2)}) %collective-permute-start.35) | collective-permute-done | bytes 98336 | tf_op jit(solution)/shard_map/ppermute | solution.py:32
  (122 shorter events, 51.6 us)
Async XLA Ops:
  7.7 13.2 %collective-permute-start.14 = (bf16[192,768]{1,0:T(8,128)(2,1)S(1)}, bf16[192,768]{1,0:T(8,128)(2,1)S(1)}, u32[]{:S(2)}, u32[]{:S(2)}) collective-permute-start(bf16[192,768]{1,0:T(8,128)(2,1)S(1)} %get-tuple-element.64), channel_id=1, source_target_pairs={{0,6},{1,7},{2,4},{3,5},{4,2},{5,3},{6,0},{7,1},{8,14},{9,15},{10,... | collective-permute-start | bytes 884744 | tf_op jit(solution)/shard_map/ppermute | solution.py:32
  22.5 29.9 %collective-permute-start.16 = (bf16[2,384,512]{2,1,0:T(8,128)(2,1)}, bf16[2,384,512]{2,1,0:T(8,128)(2,1)S(1)}, u32[]{:S(2)}, u32[]{:S(2)}) collective-permute-start(bf16[2,384,512]{2,1,0:T(8,128)(2,1)} %get-tuple-element.66.ka.va), channel_id=1, source_target_pairs={{0,8},{1,9},{2,10},{3,11},{4,12},{5,13},{6,14},{7,15},{8,16},{9,17... | collective-permute-start | bytes 2359304 | tf_op jit(solution)/shard_map/ppermute | solution.py:32
  26.8 12.7 %collective-permute-start.24 = (bf16[192,768]{1,0:T(8,128)(2,1)S(1)}, bf16[192,768]{1,0:T(8,128)(2,1)S(1)}, u32[]{:S(2)}, u32[]{:S(2)}) collective-permute-start(bf16[192,768]{1,0:T(8,128)(2,1)S(1)} %get-tuple-element.76), channel_id=1, source_target_pairs={{0,4},{1,5},{2,6},{3,7},{4,0},{5,1},{6,2},{7,3},{8,12},{9,13},{10,... | collective-permute-start | bytes 884744 | tf_op jit(solution)/shard_map/ppermute | solution.py:32
  28.4 12.6 %collective-permute-start.25 = (bf16[192,768]{1,0:T(8,128)(2,1)S(1)}, bf16[192,768]{1,0:T(8,128)(2,1)S(1)}, u32[]{:S(2)}, u32[]{:S(2)}) collective-permute-start(bf16[192,768]{1,0:T(8,128)(2,1)S(1)} %get-tuple-element.77), channel_id=1, source_target_pairs={{0,2},{1,3},{2,0},{3,1},{4,6},{5,7},{6,4},{7,5},{8,10},{9,11},{10,... | collective-permute-start | bytes 884744 | tf_op jit(solution)/shard_map/ppermute | solution.py:32
  29.9 14.8 %collective-permute-start.26 = (bf16[192,768]{1,0:T(8,128)(2,1)S(1)}, bf16[192,768]{1,0:T(8,128)(2,1)S(1)}, u32[]{:S(2)}, u32[]{:S(2)}) collective-permute-start(bf16[192,768]{1,0:T(8,128)(2,1)S(1)} %get-tuple-element.78), channel_id=1, source_target_pairs={{0,6},{1,7},{2,4},{3,5},{4,2},{5,3},{6,0},{7,1},{8,14},{9,15},{10,... | collective-permute-start | bytes 884744 | tf_op jit(solution)/shard_map/ppermute | solution.py:32
  31.2 18.5 %collective-permute-start = (bf16[192,384]{1,0:T(8,128)(2,1)S(1)}, bf16[192,384]{1,0:T(8,128)(2,1)S(1)}, u32[]{:S(2)}, u32[]{:S(2)}) collective-permute-start(bf16[192,384]{1,0:T(8,128)(2,1)S(1)} %get-tuple-element.48), channel_id=1, source_target_pairs={{0,4},{1,5},{2,6},{3,7},{4,0},{5,1},{6,2},{7,3},{8,12},{9,13},{10,... | collective-permute-start | bytes 442376 | tf_op jit(solution)/shard_map/ppermute | solution.py:32
  46.2 26.6 %collective-permute-start.28 = (bf16[2,384,512]{2,1,0:T(8,128)(2,1)}, bf16[2,384,512]{2,1,0:T(8,128)(2,1)}, u32[]{:S(2)}, u32[]{:S(2)}) collective-permute-start(bf16[2,384,512]{2,1,0:T(8,128)(2,1)} %get-tuple-element.80.ka.va), channel_id=1, source_target_pairs={{0,8},{1,9},{2,10},{3,11},{4,12},{5,13},{6,14},{7,15},{8,16},{9,17... | collective-permute-start | bytes 2359304 | tf_op jit(solution)/shard_map/ppermute | solution.py:32
  50.5 19.9 %collective-permute-start.4 = (bf16[2,384,256]{2,1,0:T(8,128)(2,1)S(1)}, bf16[2,384,256]{2,1,0:T(8,128)(2,1)S(1)}, u32[]{:S(2)}, u32[]{:S(2)}) collective-permute-start(bf16[2,384,256]{2,1,0:T(8,128)(2,1)S(1)} %get-tuple-element.52.ka.va), channel_id=1, source_target_pairs={{0,8},{1,9},{2,10},{3,11},{4,12},{5,13},{6,14},{7,15},{8,16},{9,17... | collective-permute-start | bytes 1179656 | tf_op jit(solution)/shard_map/ppermute | solution.py:32
  52.4 39.9 %collective-permute-start.17 = (bf16[2,384,512]{2,1,0:T(8,128)(2,1)S(1)}, bf16[2,384,512]{2,1,0:T(8,128)(2,1)}, u32[]{:S(2)}, u32[]{:S(2)}) collective-permute-start(bf16[2,384,512]{2,1,0:T(8,128)(2,1)S(1)} %collective-permute-done.16.ua.xa.ka.va), channel_id=1, source_target_pairs={{0,1},{1,0},{2,3},{3,2},{4,5},{5,4},{6,7},{7,6},{8,9},{9,8},{10,11... | collective-permute-start | bytes 2359304 | tf_op jit(solution)/shard_map/ppermute | solution.py:32
  52.5 18.4 %collective-permute-start.6 = (bf16[2,384,128]{2,1,0:T(8,128)(2,1)S(1)}, bf16[2,384,128]{2,1,0:T(8,128)(2,1)S(1)}, u32[]{:S(2)}, u32[]{:S(2)}) collective-permute-start(bf16[2,384,128]{2,1,0:T(8,128)(2,1)S(1)} %get-tuple-element.51.q), channel_id=1, source_target_pairs={{8,0},{9,1},{10,2},{11,3},{12,4},{13,5},{14,6},{15,7},{16,8},{17,9... | collective-permute-start | bytes 589832 | tf_op jit(solution)/shard_map/ppermute | solution.py:32
  70.9 12.9 %collective-permute-start.18 = (bf16[2,384,256]{2,1,0:T(8,128)(2,1)S(1)}, bf16[2,384,256]{2,1,0:T(8,128)(2,1)S(1)}, u32[]{:S(2)}, u32[]{:S(2)}) collective-permute-start(bf16[2,384,256]{2,1,0:T(8,128)(2,1)S(1)} %get-tuple-element.65.q), channel_id=1, source_target_pairs={{8,0},{9,1},{10,2},{11,3},{12,4},{13,5},{14,6},{15,7},{16,8},{17,9... | collective-permute-start | bytes 1179656 | tf_op jit(solution)/shard_map/ppermute | solution.py:32
  72.8 42.5 %collective-permute-start.29 = (bf16[2,384,512]{2,1,0:T(8,128)(2,1)}, bf16[2,384,512]{2,1,0:T(8,128)(2,1)}, u32[]{:S(2)}, u32[]{:S(2)}) collective-permute-start(bf16[2,384,512]{2,1,0:T(8,128)(2,1)} %collective-permute-done.28.ua.xa.ka.va), channel_id=1, source_target_pairs={{0,1},{1,0},{2,3},{3,2},{4,5},{5,4},{6,7},{7,6},{8,9},{9,8},{10,11... | collective-permute-start | bytes 2359304 | tf_op jit(solution)/shard_map/ppermute | solution.py:32
  72.9 51.1 %collective-permute-start.15 = (bf16[2,384,512]{2,1,0:T(8,128)(2,1)}, bf16[2,384,512]{2,1,0:T(8,128)(2,1)}, u32[]{:S(2)}, u32[]{:S(2)}) collective-permute-start(bf16[2,384,512]{2,1,0:T(8,128)(2,1)} %get-tuple-element.66.ka.va), channel_id=1, source_target_pairs={{0,1},{1,0},{2,3},{3,2},{4,5},{5,4},{6,7},{7,6},{8,9},{9,8},{10,11... | collective-permute-start | bytes 2359304 | tf_op jit(solution)/shard_map/ppermute | solution.py:32
  78.9 62.0 %collective-permute-start.27 = (bf16[2,384,512]{2,1,0:T(8,128)(2,1)}, bf16[2,384,512]{2,1,0:T(8,128)(2,1)}, u32[]{:S(2)}, u32[]{:S(2)}) collective-permute-start(bf16[2,384,512]{2,1,0:T(8,128)(2,1)} %get-tuple-element.80.ka.va), channel_id=1, source_target_pairs={{0,1},{1,0},{2,3},{3,2},{4,5},{5,4},{6,7},{7,6},{8,9},{9,8},{10,11... | collective-permute-start | bytes 2359304 | tf_op jit(solution)/shard_map/ppermute | solution.py:32
  90.1 23.2 %collective-permute-start.30 = (bf16[2,384,256]{2,1,0:T(8,128)(2,1)}, bf16[2,384,256]{2,1,0:T(8,128)(2,1)S(1)}, u32[]{:S(2)}, u32[]{:S(2)}) collective-permute-start(bf16[2,384,256]{2,1,0:T(8,128)(2,1)} %copy-done.15), channel_id=1, source_target_pairs={{8,0},{9,1},{10,2},{11,3},{12,4},{13,5},{14,6},{15,7},{16,8},{17,9... | collective-permute-start | bytes 1179656 | tf_op jit(solution)/shard_map/ppermute | solution.py:32
  92.3 11.4 %collective-permute-start.7 = (bf16[2,384,128]{2,1,0:T(8,128)(2,1)}, bf16[2,384,128]{2,1,0:T(8,128)(2,1)S(1)}, u32[]{:S(2)}, u32[]{:S(2)}) collective-permute-start(bf16[2,384,128]{2,1,0:T(8,128)(2,1)} %copy-done.23), channel_id=1, source_target_pairs={{0,8},{1,9},{2,10},{3,11},{4,12},{5,13},{6,14},{7,15},{8,16},{9,17... | collective-permute-start | bytes 589832 | tf_op jit(solution)/shard_map/ppermute | solution.py:32
  103.7 34.6 %collective-permute-start.19 = (bf16[2,384,256]{2,1,0:T(8,128)(2,1)S(1)}, bf16[2,384,256]{2,1,0:T(8,128)(2,1)S(1)}, u32[]{:S(2)}, u32[]{:S(2)}) collective-permute-start(bf16[2,384,256]{2,1,0:T(8,128)(2,1)S(1)} %get-tuple-element.69), channel_id=1, source_target_pairs={{0,8},{1,9},{2,10},{3,11},{4,12},{5,13},{6,14},{7,15},{8,16},{9,17... | collective-permute-start | bytes 1179656 | tf_op jit(solution)/shard_map/ppermute | solution.py:32
  113.3 23.4 %collective-permute-start.20 = (f32[2,1,768]{2,1,0:T(1,128)S(1)}, f32[2,1,768]{2,1,0:T(1,128)S(1)}, u32[]{:S(2)}, u32[]{:S(2)}) collective-permute-start(f32[2,1,768]{2,1,0:T(1,128)S(1)} %get-tuple-element.70), channel_id=1, source_target_pairs={{0,8},{1,9},{2,10},{3,11},{4,12},{5,13},{6,14},{7,15},{8,16},{9,17... | collective-permute-start | bytes 18440 | tf_op jit(solution)/shard_map/ppermute | solution.py:32
  122.0 32.0 %collective-permute-start.31 = (bf16[2,384,256]{2,1,0:T(8,128)(2,1)S(1)}, bf16[2,384,256]{2,1,0:T(8,128)(2,1)S(1)}, u32[]{:S(2)}, u32[]{:S(2)}) collective-permute-start(bf16[2,384,256]{2,1,0:T(8,128)(2,1)S(1)} %get-tuple-element.83), channel_id=1, source_target_pairs={{0,8},{1,9},{2,10},{3,11},{4,12},{5,13},{6,14},{7,15},{8,16},{9,17... | collective-permute-start | bytes 1179656 | tf_op jit(solution)/shard_map/ppermute | solution.py:32
  124.0 17.5 %collective-permute-start.32 = (f32[2,1,768]{2,1,0:T(1,128)S(1)}, f32[2,1,768]{2,1,0:T(1,128)S(1)}, u32[]{:S(2)}, u32[]{:S(2)}) collective-permute-start(f32[2,1,768]{2,1,0:T(1,128)S(1)} %get-tuple-element.84), channel_id=1, source_target_pairs={{0,8},{1,9},{2,10},{3,11},{4,12},{5,13},{6,14},{7,15},{8,16},{9,17... | collective-permute-start | bytes 18440 | tf_op jit(solution)/shard_map/ppermute | solution.py:32
  136.7 20.0 %collective-permute-start.9 = (bf16[192,128]{1,0:T(8,128)(2,1)S(1)}, bf16[192,128]{1,0:T(8,128)(2,1)S(1)}, u32[]{:S(2)}, u32[]{:S(2)}) collective-permute-start(bf16[192,128]{1,0:T(8,128)(2,1)S(1)} %get-tuple-element.58), channel_id=1, source_target_pairs={{0,4},{1,5},{2,6},{3,7},{4,0},{5,1},{6,2},{7,3},{8,12},{9,13},{10,... | collective-permute-start | bytes 147464 | tf_op jit(solution)/shard_map/ppermute | solution.py:32
  138.3 19.0 %collective-permute-start.10 = (bf16[192,128]{1,0:T(8,128)(2,1)S(1)}, bf16[192,128]{1,0:T(8,128)(2,1)S(1)}, u32[]{:S(2)}, u32[]{:S(2)}) collective-permute-start(bf16[192,128]{1,0:T(8,128)(2,1)S(1)} %get-tuple-element.59), channel_id=1, source_target_pairs={{0,2},{1,3},{2,0},{3,1},{4,6},{5,7},{6,4},{7,5},{8,10},{9,11},{10,... | collective-permute-start | bytes 147464 | tf_op jit(solution)/shard_map/ppermute | solution.py:32
  141.0 17.9 %collective-permute-start.11 = (bf16[192,128]{1,0:T(8,128)(2,1)S(1)}, bf16[192,128]{1,0:T(8,128)(2,1)S(1)}, u32[]{:S(2)}, u32[]{:S(2)}) collective-permute-start(bf16[192,128]{1,0:T(8,128)(2,1)S(1)} %get-tuple-element.60), channel_id=1, source_target_pairs={{0,6},{1,7},{2,4},{3,5},{4,2},{5,3},{6,0},{7,1},{8,14},{9,15},{10,... | collective-permute-start | bytes 147464 | tf_op jit(solution)/shard_map/ppermute | solution.py:32
  141.5 18.8 %collective-permute-start.21 = (bf16[192,256]{1,0:T(8,128)(2,1)S(1)}, bf16[192,256]{1,0:T(8,128)(2,1)S(1)}, u32[]{:S(2)}, u32[]{:S(2)}) collective-permute-start(bf16[192,256]{1,0:T(8,128)(2,1)S(1)} %get-tuple-element.72), channel_id=1, source_target_pairs={{0,4},{1,5},{2,6},{3,7},{4,0},{5,1},{6,2},{7,3},{8,12},{9,13},{10,... | collective-permute-start | bytes 294920 | tf_op jit(solution)/shard_map/ppermute | solution.py:32
  (38 other events, 632.3 us)

commit v2 on v1

v2 whole, which is shorter than its diff:
```python
import functools
import math

import jax
import jax.numpy as jnp
from jax import lax
from jax.experimental import pallas as pl
from jax.experimental.pallas import tpu as pltpu
from jax.sharding import PartitionSpec as P

HEAD_DIM = 128
AXES = ("span", "seq")
ANY = pl.BlockSpec(memory_space=pl.ANY)
SMEM = pl.BlockSpec(memory_space=pltpu.SMEM)
MIB = 1024 * 1024
TILE = 128
NT = (((1,), (1,)), ((), ()))
NN = (((1,), (0,)), ((), ()))


def params(mib):
    return pltpu.CompilerParams(vmem_limit_bytes=mib * MIB)


def move(block, target):
    spans, members = lax.axis_size("span"), lax.axis_size("seq")
    route = []
    for device in range(spans * members):
        span, member = divmod(device, members)
        to_span, to_member = target(span, member)
        if 0 <= to_span < spans:
            route.append((device, to_span * members + to_member))
    return lax.ppermute(block, AXES, route)


def within_level(dx, dy):
    return lambda span, member: (span ^ dy, member ^ (2 * dx))


def other_core(span, member):
    return span, member ^ 1


def one_up(span, member):
    return span + 2, member


def one_down(span, member):
    return span - 2, member


PLACES = ((0, 0), (0, 1), (1, 0), (1, 1))


def timestep_gate(level_index, plan, gate_weight, span_number):
    noise_level = jnp.sum(
        jnp.where(jnp.arange(level_index.shape[0], dtype=jnp.int32) == span_number, level_index, 0)
    )
    timestep = jnp.sum(
        jnp.where(jnp.arange(plan.shape[0], dtype=jnp.int32) == noise_level, plan, 0)
    )
    half_freq = gate_weight.shape[0] // 2
    frequencies = jnp.exp(-math.log(10000.0) * jnp.arange(half_freq, dtype=jnp.float32) / half_freq)
    angles = timestep.astype(jnp.float32) * frequencies
    embedding = jnp.concatenate([jnp.cos(angles), jnp.sin(angles)])[None, :]
    return jnp.dot(
        embedding, gate_weight, precision=lax.Precision.HIGHEST, preferred_element_type=jnp.float32
    )


def pack_kernel(first, heads, group_width, count, meta, q, k, v, *rest):
    outs, sems = rest[count : count + 4], rest[count + 4]
    copies = []
    for j in range(4):
        for t, ref in enumerate((q, k, v)):
            for h in range(heads):
                column = pl.multiple_of(meta[j] * group_width + (first + h) * HEAD_DIM, HEAD_DIM)
                copy = pltpu.make_async_copy(
                    ref.at[:, pl.ds(column, HEAD_DIM)], outs[j].at[t * heads + h], sems.at[j, t * heads + h]
                )
                copy.start()
                copies.append(copy)
    for copy in copies:
        copy.wait()


def pack(meta, q, k, v, first, heads, group_width, after):
    rows = q.shape[0]
    return pl.pallas_call(
        functools.partial(pack_kernel, first, heads, group_width, len(after)),
        out_shape=[jax.ShapeDtypeStruct((3 * heads, rows, HEAD_DIM), q.dtype)] * 4,
        in_specs=[SMEM] + [ANY] * (3 + len(after)),
        out_specs=[ANY] * 4,
        scratch_shapes=[pltpu.SemaphoreType.DMA((4, 3 * heads))],
        compiler_params=params(60),
        cost_estimate=pl.CostEstimate(
            flops=0, bytes_accessed=48 * rows * heads * HEAD_DIM, transcendentals=0
        ),
        name="pack",
    )(meta, q, k, v, *after)


def stack_kernel(heads, count, meta, *refs):
    pieces, (q_out, kv_out, sems) = refs[:4], refs[4 + count :]
    rows = pieces[0].shape[1]
    copies = []
    for j, (dx, _) in enumerate(PLACES):
        parity = meta[4 + j]
        at = pl.ds(dx * rows, rows)
        for t, (source, target) in enumerate(
            (
                (pieces[j].at[pl.ds(heads, 2 * heads)], kv_out.at[:, parity, at]),
                (pieces[j].at[pl.ds(0, heads)], q_out.at[:, parity, at]),
            )
        ):
            copy = pltpu.make_async_copy(source, target, sems.at[j, t])
            copy.start()
            copies.append(copy)
    for copy in copies:
        copy.wait()


def stack(meta, pieces, after):
    triple, rows, _ = pieces[0].shape
    heads = triple // 3
    dtype = pieces[0].dtype
    return pl.pallas_call(
        functools.partial(stack_kernel, heads, len(after)),
        out_shape=[
            jax.ShapeDtypeStruct((heads, 2, 2 * rows, HEAD_DIM), dtype),
            jax.ShapeDtypeStruct((2 * heads, 2, 2 * rows, HEAD_DIM), dtype),
        ],
        in_specs=[SMEM] + [ANY] * (4 + len(after)),
        out_specs=[ANY] * 2,
        scratch_shapes=[pltpu.SemaphoreType.DMA((4, 2))],
        compiler_params=params(8),
        cost_estimate=pl.CostEstimate(
            flops=0, bytes_accessed=48 * rows * heads * HEAD_DIM, transcendentals=0
        ),
        name="stack",
    )(meta, *pieces, *after)


def softmax_part(q, keys, values):
    scale = math.log2(math.e) / math.sqrt(HEAD_DIM)
    scores = [lax.dot_general(q, k, NT, preferred_element_type=jnp.float32) for k in keys]
    peak = functools.reduce(jnp.maximum, scores).max(axis=1, keepdims=True)
    peak = peak * scale
    weights = [jnp.exp2(s * scale - peak) for s in scores]
    total = functools.reduce(jnp.add, weights).sum(axis=1, keepdims=True)
    out = functools.reduce(
        jnp.add,
        [
            lax.dot_general(w.astype(jnp.bfloat16), v, NN, preferred_element_type=jnp.float32)
            for w, v in zip(weights, values)
        ],
    )
    return out / total, peak + jnp.log2(total)


def attend_rows(q_ref, p, blocks, o_ref, lse_ref):
    rows = q_ref.shape[2]
    for t in range(rows // TILE):
        out, lse = softmax_part(
            q_ref[0, p, pl.ds(t * TILE, TILE)],
            [kv[0][0, i] for kv, i in blocks],
            [kv[1][0, i] for kv, i in blocks],
        )
        row = p * (rows // TILE) + t
        o_ref[0, pl.ds(row * TILE, TILE)] = out.astype(o_ref.dtype)
        lse_ref[pl.ds(row, 1)] = jnp.broadcast_to(lse, (TILE, TILE)).T[:1]


def remote_kernel(count, q, ka, va, kb, vb, *rest):
    o, lse = rest[count:]
    a, b = (ka, va), (kb, vb)
    every = [(a, 0), (b, 0), (a, 1), (b, 1)]
    attend_rows(q, 0, every, o, lse)
    attend_rows(q, 1, every[2:], o, lse)
    left, terms = lse[...], []
    for _ in range(3):
        terms.append(left.astype(jnp.bfloat16))
        left = left - terms[-1].astype(jnp.float32)
    terms.append(jnp.zeros_like(terms[0]))
    last = 2 * q.shape[2]
    o[0, pl.ds(last, 4 * lse.shape[0])] = jnp.concatenate(
        [term.astype(jnp.float32) for term in terms], axis=0
    ).astype(jnp.bfloat16)


def own_kernel(count, meta, q, ka, va, kb, vb, ua, xa, ub, xb, *rest):
    o, lse = rest[count:]
    a, b, c, d = (ka, va), (kb, vb), (ua, xa), (ub, xb)
    own = [(a, 0), (b, 0), (a, 1), (b, 1)]
    below = [(c, 0), (d, 0), (c, 1), (d, 1)]

    @pl.when(meta[8] >= 1)
    def _():
        attend_rows(q, 0, own[:2] + below, o, lse.at[0])
        attend_rows(q, 1, own + below, o, lse.at[0])

    @pl.when(meta[8] < 1)
    def _():
        attend_rows(q, 0, own[:2], o, lse.at[0])
        attend_rows(q, 1, own, o, lse.at[0])


def lse_rows(rows):
    return -(-2 * rows // TILE // 8) * 8


def attend(far, meta, q, kvs, after):
    heads, _, rows, _ = q.shape
    block = (1, 2, rows, HEAD_DIM)
    head = pl.BlockSpec(block, lambda h: (h, 0, 0, 0))
    value = pl.BlockSpec(block, lambda h: (heads + h, 0, 0, 0))
    operands, specs = ([], []) if far else ([meta], [SMEM])
    operands.append(q)
    specs.append(head)
    for kv in kvs:
        operands += [kv, kv]
        specs += [head, value]
    extra = lse_rows(rows)
    if far:
        length = 2 * rows + 4 * extra
        out_shape = jax.ShapeDtypeStruct((heads, length, HEAD_DIM), jnp.bfloat16)
        out_specs = pl.BlockSpec((1, length, HEAD_DIM), lambda h: (h, 0, 0))
        scratch = [pltpu.VMEM((extra, TILE), jnp.float32)]
    else:
        out_shape = [
            jax.ShapeDtypeStruct((heads, 2 * rows, HEAD_DIM), jnp.float32),
            jax.ShapeDtypeStruct((heads, extra, TILE), jnp.float32),
        ]
        out_specs = [
            pl.BlockSpec((1, 2 * rows, HEAD_DIM), lambda h: (h, 0, 0)),
            pl.BlockSpec((1, extra, TILE), lambda h: (h, 0, 0)),
        ]
        scratch = []
    scores = heads * (3 if far else 7) * rows * 2 * rows
    return pl.pallas_call(
        functools.partial(remote_kernel if far else own_kernel, len(after)),
        grid=(heads,),
        out_shape=out_shape,
        in_specs=specs + [ANY] * len(after),
        out_specs=out_specs,
        scratch_shapes=scratch,
        compiler_params=params(20),
        cost_estimate=pl.CostEstimate(
            flops=scores * HEAD_DIM * 4,
            bytes_accessed=(len(kvs) + 1) * heads * rows * 8 * HEAD_DIM,
            transcendentals=scores,
        ),
        name="remote" if far else "own",
    )(*operands, *after)


def merge_kernel(count, meta, o, lse, o_far, *rest):
    outs, scratch = rest[count : count + 4], rest[count + 4]
    rows = o.shape[1] // 2
    half = rows // 2
    extra = lse.shape[1]
    terms = o_far[0, pl.ds(2 * rows, 4 * extra)].astype(jnp.float32)
    lse_far = terms[:extra] + terms[extra : 2 * extra] + terms[2 * extra : 3 * extra]
    far = jnp.where(meta[8] >= 2, 1.0, 0.0)
    share = far / (1.0 + jnp.exp2(lse[0] - lse_far))
    for row in range(2 * rows // TILE):
        at = pl.ds(row * TILE, TILE)
        weight = jnp.broadcast_to(share[row : row + 1], (HEAD_DIM, TILE)).T
        near = o[0, at]
        scratch[at] = near + weight * (o_far[0, at].astype(jnp.float32) - near)
    for j, (dx, _) in enumerate(PLACES):
        at = pl.ds(pl.multiple_of(meta[4 + j] * rows + dx * half, half), half)
        outs[j][0] = scratch[at].astype(outs[j].dtype)


def merge(meta, o, lse, o_far, after):
    heads, both, _ = o.shape
    by_head = lambda h: (h, 0, 0)
    return pl.pallas_call(
        functools.partial(merge_kernel, len(after)),
        grid=(heads,),
        out_shape=[jax.ShapeDtypeStruct((heads, both // 4, HEAD_DIM), jnp.bfloat16)] * 4,
        in_specs=[SMEM]
        + [pl.BlockSpec((1,) + a.shape[1:], by_head) for a in (o, lse, o_far)]
        + [ANY] * len(after),
        out_specs=[pl.BlockSpec((1, both // 4, HEAD_DIM), by_head)] * 4,
        scratch_shapes=[pltpu.VMEM((both, HEAD_DIM), jnp.float32)],
        compiler_params=params(12),
        cost_estimate=pl.CostEstimate(
            flops=4 * both * HEAD_DIM * heads,
            bytes_accessed=8 * both * HEAD_DIM * heads,
            transcendentals=0,
        ),
        name="merge",
    )(meta, o, lse, o_far, *after)


def finish_kernel(firsts, group_width, meta, gate, *refs):
    pieces, out = refs[:-1], refs[-1]
    for i, piece in enumerate(pieces):
        chunk, j = divmod(i, 4)
        for h in range(piece.shape[0]):
            column = meta[j] * group_width + (firsts[chunk] + h) * HEAD_DIM
            at = pl.ds(pl.multiple_of(column, HEAD_DIM), HEAD_DIM)
            out[:, at] = (gate[:, at] * piece[h].astype(jnp.float32)).astype(out.dtype)


def finish(meta, gate, pieces, firsts, group_width):
    rows = pieces[0].shape[1]
    whole = pl.BlockSpec(memory_space=pltpu.VMEM)
    return pl.pallas_call(
        functools.partial(finish_kernel, firsts, group_width),
        out_shape=jax.ShapeDtypeStruct((rows, 4 * group_width), jnp.bfloat16),
        in_specs=[SMEM] + [whole] * (1 + len(pieces)),
        out_specs=whole,
        compiler_params=params(16),
        cost_estimate=pl.CostEstimate(
            flops=rows * group_width * 4, bytes_accessed=rows * group_width * 16, transcendentals=0
        ),
        name="finish",
    )(meta, gate, *pieces)


def shards(queries, keys, values, level_index, plan, gate_weight):
    span = lax.axis_index("span")
    member = lax.axis_index("seq")
    x, y = member // 2, span % 2
    group_width = queries.shape[1] // 4
    group_heads = group_width // HEAD_DIM
    meta = jnp.stack(
        [2 * (x ^ dx) + (y ^ dy) for dx, dy in PLACES]
        + [y ^ dy for _, dy in PLACES]
        + [span // 2]
    ).astype(jnp.int32)
    gate = timestep_gate(level_index, plan, gate_weight, span)

    sizes = []
    while sum(sizes) < group_heads:
        sizes.append(min(2 if sizes else 1, group_heads - sum(sizes)))
    firsts = [sum(sizes[:i]) for i in range(len(sizes))]
    chunks = range(len(sizes))

    received, last = [], []
    for i in chunks:
        sent = pack(meta, queries, keys, values, firsts[i], sizes[i], group_width, last)
        last = [sent[0]]
        received.append([sent[0]] + [move(sent[j], within_level(*PLACES[j])) for j in (1, 2, 3)])
    last.append(gate)

    q, kv, kv_up, q_down = {}, {}, {}, {}

    def spread(i, after):
        q[i], kv[i] = stack(meta, received[i], after)
        kv_up[i] = move(kv[i], one_up)
        q_down[i] = move(q[i], one_down)
        kv[i] = (kv[i], move(kv[i], other_core))
        return [q[i]]

    far, near, results = {}, {}, {}

    def remote(i, after):
        kv_up[i] = (kv_up[i], move(kv_up[i], other_core))
        far[i] = attend(True, meta, q_down[i], kv_up[i], after)
        kept = [far[i]]
        far[i] = move(far[i], one_up)
        return kept

    def own(i, after):
        near[i] = attend(False, meta, q[i], kv[i] + kv_up[i], after)
        return [near[i][1]]

    def close(i, after):
        merged = merge(meta, *near[i], far[i], after)
        results[i] = [merged[0]] + [move(merged[j], within_level(*PLACES[j])) for j in (1, 2, 3)]
        return [merged[0]]

    steps = []
    for i in chunks:
        steps.append((2 * i, spread, i))
        steps.append((2 * i + 3, remote, i))
        steps.append((2 * i + 4.5, own, i))
        steps.append((2 * i + 6.7, close, i))
    for _, step, i in sorted(steps, key=lambda item: item[0]):
        last = step(i, last)
    return finish(meta, gate, sum((results[i] for i in chunks), []), firsts, group_width)


def solution(mesh):
    rows = P(AXES, None)
    return jax.shard_map(
        shards,
        mesh=mesh,
        in_specs=(rows, rows, rows, P(), P(), P()),
        out_specs=rows,
        check_vma=False,
    )
```

time: 168 us -> 233 us (1.39)
  Pallas kernels: 53.9 us -> 143 us
  waiting for transfers between devices: 43.6 us -> 35.3 us
  local copies, waits for them, and re-layouts: 8.57 us -> 0.65 us
  starting transfers between devices: 57.1 us -> 49.8 us
    pallas_call x16, Pallas kernels: 53.9 us -> 143 us  [the longest x3 95.4 us: pack(): pl.pallas_call(functools.partial(pack_kernel, first, heads, group_width,...]
    unnamed x52 -> x26, local copies, waits for them, and re-layouts: 8.49 us -> 0.06 us
    ppermute x36 -> x33, waiting for transfers between devices: 43.6 us -> 35.3 us  [move(): return lax.ppermute(block, AXES, route)]
    ppermute x36 -> x33, starting transfers between devices: 57.1 us -> 49.8 us  [move(): return lax.ppermute(block, AXES, route)]
  transfers between devices with their start and end apart: 36 -> 33, of which waited for: 12 -> 12; matrix products, arithmetic and copies ran while one was open for 2% -> 1% of each run, Pallas kernels for 30% -> 52%
where the time goes in v2:
time: 233 us
  Pallas kernels  143 us (61%)
  starting transfers between devices  49.8 us (21%)
  waiting for transfers between devices  35.3 us (15%)
    pallas_call x3, Pallas kernels, pack(): pl.pallas_call(functools.partial(pack_kernel, first, heads, group_width,...  95.4 us
    ppermute x33, starting transfers between devices, move(): return lax.ppermute(block, AXES, route)  49.8 us
    pallas_call x6, Pallas kernels, attend(): pl.pallas_call(functools.partial(remote_kernel if far else own_kernel, le...  39.3 us
    ppermute x33, waiting for transfers between devices, move(): return lax.ppermute(block, AXES, route)  35.3 us
  transfers between devices with their start and end apart: 33, of which 12 were waited for; matrix products, arithmetic and copies ran while one was open for 1% of the time, Pallas kernels for 52%

profile of v2, /device:TPU:8, one launch (start us, length us, event | category | flops | bytes accessed | tf_op | source)
XLA Modules:
  0.0 232.8 jit_solution(7671481512886358645)
XLA Ops:
  0.6 19.9 %pack.3 = (bf16[3,192,128]{2,1,0:T(8,128)(2,1)}, bf16[3,192,128]{2,1,0:T(8,128)(2,1)}, bf16[3,192,128]{2,1,0:T(8,128)(2,1)}, bf16[3,192,128]{2,1,0:T(8,128)(2,1)}) custom-call(s32[9]{0:T(128)} %stack.36.meta, bf16[192,2560]{1,0:T(8,128)(2,1)} %q.5, bf16[192,2560]{1,0:T(8,128)(2,1)} %k.5, bf16[192,2560]{1,0:T(8,128)(2,1)} %v.5), custom_call_target="tpu_custom_call" | custom-call | bytes 1179648 | tf_op jit(solution)/shard_map/pack/pallas_call | solution.py:89
  26.6 37.7 %pack.4 = (bf16[6,192,128]{2,1,0:T(8,128)(2,1)}, bf16[6,192,128]{2,1,0:T(8,128)(2,1)}, bf16[6,192,128]{2,1,0:T(8,128)(2,1)}, bf16[6,192,128]{2,1,0:T(8,128)(2,1)}) custom-call(s32[9]{0:T(128)} %stack.36.meta, bf16[192,2560]{1,0:T(8,128)(2,1)} %q.5, bf16[192,2560]{1,0:T(8,128)(2,1)} %k.5, bf16[192,2560]{1,0:T(8,128)(2,1)} %v.5, ...), custom_call_target="tpu_custom_call" | custom-call | bytes 2359296 | tf_op jit(solution)/shard_map/pack/pallas_call | solution.py:89
  64.4 37.9 %pack.5 = (bf16[6,192,128]{2,1,0:T(8,128)(2,1)}, bf16[6,192,128]{2,1,0:T(8,128)(2,1)}, bf16[6,192,128]{2,1,0:T(8,128)(2,1)}, bf16[6,192,128]{2,1,0:T(8,128)(2,1)}) custom-call(s32[9]{0:T(128)} %stack.36.meta, bf16[192,2560]{1,0:T(8,128)(2,1)} %q.5, bf16[192,2560]{1,0:T(8,128)(2,1)} %k.5, bf16[192,2560]{1,0:T(8,128)(2,1)} %v.5, ...), custom_call_target="tpu_custom_call" | custom-call | bytes 2359296 | tf_op jit(solution)/shard_map/pack/pallas_call | solution.py:89
  104.9 3.5 %collective-permute-start.4 = (bf16[2,2,384,128]{3,2,1,0:T(8,128)(2,1)S(1)}, bf16[2,2,384,128]{3,2,1,0:T(8,128)(2,1)S(1)}, u32[]{:S(2)}, u32[]{:S(2)}) collective-permute-start(bf16[2,2,384,128]{3,2,1,0:T(8,128)(2,1)S(1)} %get-tuple-element.48.ka.va), channel_id=1, source_target_pairs={{0,8},{1,9},{2,10},{3,11},{4,12},{5,13},{6,14},{7,15},{8,16},{9,17... | collective-permute-start | bytes 1179656 | tf_op jit(solution)/shard_map/ppermute | solution.py:33
  111.9 2.4 %collective-permute-start.9 = (bf16[1,2,384,128]{3,2,1,0:T(8,128)(2,1)S(1)}, bf16[1,2,384,128]{3,2,1,0:T(8,128)(2,1)S(1)}, u32[]{:S(2)}, u32[]{:S(2)}) collective-permute-start(bf16[1,2,384,128]{3,2,1,0:T(8,128)(2,1)S(1)} %get-tuple-element.47.refs_4_.q), channel_id=1, source_target_pairs={{8,0},{9,1},{10,2},{11,3},{12,4},{13,5},{14,6},{15,7},{16,8},{17,9... | collective-permute-start | bytes 589832 | tf_op jit(solution)/shard_map/ppermute | solution.py:33
  114.3 2.5 %collective-permute-done.4.ka.va.ua.xa = bf16[2,2,384,128]{3,2,1,0:T(8,128)(2,1)S(1)} collective-permute-done((bf16[2,2,384,128]{3,2,1,0:T(8,128)(2,1)S(1)}, bf16[2,2,384,128]{3,2,1,0:T(8,128)(2,1)S(1)}, u32[]{:S(2)}, u32[]{:S(2)}) %collective-permute-start.4) | collective-permute-done | bytes 393248 | tf_op jit(solution)/shard_map/ppermute | solution.py:33
  121.4 4.6 %collective-permute-done.12.refs_3_ = bf16[6,192,128]{2,1,0:T(8,128)(2,1)S(1)} collective-permute-done((bf16[6,192,128]{2,1,0:T(8,128)(2,1)S(1)}, bf16[6,192,128]{2,1,0:T(8,128)(2,1)S(1)}, u32[]{:S(2)}, u32[]{:S(2)}) %collective-permute-start.12) | collective-permute-done | bytes 294944 | tf_op jit(solution)/shard_map/ppermute | solution.py:33
  126.0 2.4 %collective-permute-start.8 = (bf16[6,192,128]{2,1,0:T(8,128)(2,1)S(1)}, bf16[6,192,128]{2,1,0:T(8,128)(2,1)S(1)}, u32[]{:S(2)}, u32[]{:S(2)}) collective-permute-start(bf16[6,192,128]{2,1,0:T(8,128)(2,1)S(1)} %copy-done.5), channel_id=1, source_target_pairs={{0,6},{1,7},{2,4},{3,5},{4,2},{5,3},{6,0},{7,1},{8,14},{9,15},{10,... | collective-permute-start | bytes 884744 | tf_op jit(solution)/shard_map/ppermute | solution.py:33
  129.6 3.5 %collective-permute-start.15 = (bf16[4,2,384,128]{3,2,1,0:T(8,128)(2,1)S(1)}, bf16[4,2,384,128]{3,2,1,0:T(8,128)(2,1)S(1)}, u32[]{:S(2)}, u32[]{:S(2)}) collective-permute-start(bf16[4,2,384,128]{3,2,1,0:T(8,128)(2,1)S(1)} %get-tuple-element.59.ka.va), channel_id=1, source_target_pairs={{0,8},{1,9},{2,10},{3,11},{4,12},{5,13},{6,14},{7,15},{8,16},{9,17... | collective-permute-start | bytes 2359304 | tf_op jit(solution)/shard_map/ppermute | solution.py:33
  133.1 2.8 %remote.3.refs_4_ = bf16[1,800,128]{2,1,0:T(8,128)(2,1)S(1)} custom-call(bf16[1,2,384,128]{3,2,1,0:T(8,128)(2,1)S(1)} %collective-permute-done.9.q, bf16[2,2,384,128]{3,2,1,0:T(8,128)(2,1)S(1)} %collective-permute-done.4.ka.va.ua.xa, bf16[2,2,384,128]{3,2,1,0:T(8,128)(2,1)S(1)} %collective-permute-done.4.ka.va.ua.xa, ...), custom_call_target="tpu_custom_call" | custom-call | flops 452984832 | bytes 1179648 | tf_op jit(solution)/shard_map/remote/pallas_call | solution.py:240
  137.4 3.5 %collective-permute-start.23 = (bf16[4,2,384,128]{3,2,1,0:T(8,128)(2,1)S(1)}, bf16[4,2,384,128]{3,2,1,0:T(8,128)(2,1)S(1)}, u32[]{:S(2)}, u32[]{:S(2)}) collective-permute-start(bf16[4,2,384,128]{3,2,1,0:T(8,128)(2,1)S(1)} %get-tuple-element.66.ka.va), channel_id=1, source_target_pairs={{0,8},{1,9},{2,10},{3,11},{4,12},{5,13},{6,14},{7,15},{8,16},{9,17... | collective-permute-start | bytes 2359304 | tf_op jit(solution)/shard_map/ppermute | solution.py:33
  140.9 11.1 %collective-permute-done.15.ka.va.ua.xa = bf16[4,2,384,128]{3,2,1,0:T(8,128)(2,1)S(1)} collective-permute-done((bf16[4,2,384,128]{3,2,1,0:T(8,128)(2,1)S(1)}, bf16[4,2,384,128]{3,2,1,0:T(8,128)(2,1)S(1)}, u32[]{:S(2)}, u32[]{:S(2)}) %collective-permute-start.15) | collective-permute-done | bytes 786464 | tf_op jit(solution)/shard_map/ppermute | solution.py:33
  154.3 8.3 %collective-permute-done.23.ka.va.ua.xa = bf16[4,2,384,128]{3,2,1,0:T(8,128)(2,1)S(1)} collective-permute-done((bf16[4,2,384,128]{3,2,1,0:T(8,128)(2,1)S(1)}, bf16[4,2,384,128]{3,2,1,0:T(8,128)(2,1)S(1)}, u32[]{:S(2)}, u32[]{:S(2)}) %collective-permute-start.23) | collective-permute-done | bytes 786464 | tf_op jit(solution)/shard_map/ppermute | solution.py:33
  163.1 2.7 %collective-permute-done.17.q = bf16[2,2,384,128]{3,2,1,0:T(8,128)(2,1)S(1)} collective-permute-done((bf16[2,2,384,128]{3,2,1,0:T(8,128)(2,1)S(1)}, bf16[2,2,384,128]{3,2,1,0:T(8,128)(2,1)S(1)}, u32[]{:S(2)}, u32[]{:S(2)}) %collective-permute-start.17) | collective-permute-done | bytes 393248 | tf_op jit(solution)/shard_map/ppermute | solution.py:33
  165.8 2.2 collective-permute-start.25
  168.0 5.4 %own.3 = (f32[1,768,128]{2,1,0:T(8,128)S(1)}, f32[1,8,128]{2,1,0:T(8,128)S(1)}) custom-call(s32[9]{0:T(128)S(1)} %copy-done.4, bf16[1,2,384,128]{3,2,1,0:T(8,128)(2,1)S(1)} %get-tuple-element.47.refs_4_.q, bf16[2,2,384,128]{3,2,1,0:T(8,128)(2,1)S(1)} %get-tuple-element.48.ka.va, bf16[2,2,384,128]{3,2,1,0:T(8,128)(2,1)S(1)} %get-tuple-element.48.ka.va, ...), custom_call_target="tpu_custom_call" | custom-call | flops 1056964608 | bytes 1966080 | tf_op jit(solution)/shard_map/own/pallas_call | solution.py:240
  173.4 3.7 %collective-permute-start.13 = (bf16[1,800,128]{2,1,0:T(8,128)(2,1)S(1)}, bf16[1,800,128]{2,1,0:T(8,128)(2,1)S(1)}, u32[]{:S(2)}, u32[]{:S(2)}) collective-permute-start(bf16[1,800,128]{2,1,0:T(8,128)(2,1)S(1)} %remote.3.refs_4_), channel_id=1, source_target_pairs={{0,8},{1,9},{2,10},{3,11},{4,12},{5,13},{6,14},{7,15},{8,16},{9,17... | collective-permute-start | bytes 614408 | tf_op jit(solution)/shard_map/ppermute | solution.py:33
  177.1 5.6 %remote.4.rest_0_ = bf16[2,800,128]{2,1,0:T(8,128)(2,1)S(1)} custom-call(bf16[2,2,384,128]{3,2,1,0:T(8,128)(2,1)S(1)} %collective-permute-done.17.q, bf16[4,2,384,128]{3,2,1,0:T(8,128)(2,1)S(1)} %collective-permute-done.15.ka.va.ua.xa, bf16[4,2,384,128]{3,2,1,0:T(8,128)(2,1)S(1)} %collective-permute-done.15.ka.va.ua.xa, ...), custom_call_target="tpu_custom_call" | custom-call | flops 905969664 | bytes 2359296 | tf_op jit(solution)/shard_map/remote/pallas_call | solution.py:240
  182.7 3.5 %collective-permute-start.21 = (bf16[2,800,128]{2,1,0:T(8,128)(2,1)S(1)}, bf16[2,800,128]{2,1,0:T(8,128)(2,1)S(1)}, u32[]{:S(2)}, u32[]{:S(2)}) collective-permute-start(bf16[2,800,128]{2,1,0:T(8,128)(2,1)S(1)} %remote.4.rest_0_), channel_id=1, source_target_pairs={{0,8},{1,9},{2,10},{3,11},{4,12},{5,13},{6,14},{7,15},{8,16},{9,17... | collective-permute-start | bytes 1228808 | tf_op jit(solution)/shard_map/ppermute | solution.py:33
  186.2 10.0 %own.4 = (f32[2,768,128]{2,1,0:T(8,128)S(1)}, f32[2,8,128]{2,1,0:T(8,128)S(1)}) custom-call(s32[9]{0:T(128)S(1)} %copy-done.4, bf16[2,2,384,128]{3,2,1,0:T(8,128)(2,1)S(1)} %get-tuple-element.55.rest_0_.q, bf16[4,2,384,128]{3,2,1,0:T(8,128)(2,1)S(1)} %get-tuple-element.59.ka.va, bf16[4,2,384,128]{3,2,1,0:T(8,128)(2,1)S(1)} %get-tuple-element.59.ka.va, ...), custom_call_target="tpu_custom_call" | custom-call | flops 2113929216 | bytes 3932160 | tf_op jit(solution)/shard_map/own/pallas_call | solution.py:240
  197.0 5.6 %remote.5.rest_0_ = bf16[2,800,128]{2,1,0:T(8,128)(2,1)S(1)} custom-call(bf16[2,2,384,128]{3,2,1,0:T(8,128)(2,1)S(1)} %collective-permute-done.25.q, bf16[4,2,384,128]{3,2,1,0:T(8,128)(2,1)S(1)} %collective-permute-done.23.ka.va.ua.xa, bf16[4,2,384,128]{3,2,1,0:T(8,128)(2,1)S(1)} %collective-permute-done.23.ka.va.ua.xa, ...), custom_call_target="tpu_custom_call" | custom-call | flops 905969664 | bytes 2359296 | tf_op jit(solution)/shard_map/remote/pallas_call | solution.py:240
  202.6 2.1 collective-permute-start.29
  204.7 10.0 %own.5 = (f32[2,768,128]{2,1,0:T(8,128)S(1)}, f32[2,8,128]{2,1,0:T(8,128)S(1)}) custom-call(s32[9]{0:T(128)S(1)} %copy-done.4, bf16[2,2,384,128]{3,2,1,0:T(8,128)(2,1)S(1)} %get-tuple-element.56.rest_0_.q, bf16[4,2,384,128]{3,2,1,0:T(8,128)(2,1)S(1)} %get-tuple-element.66.ka.va, bf16[4,2,384,128]{3,2,1,0:T(8,128)(2,1)S(1)} %get-tuple-element.66.ka.va, ...), custom_call_target="tpu_custom_call" | custom-call | flops 2113929216 | bytes 3932160 | tf_op jit(solution)/shard_map/own/pallas_call | solution.py:240
  221.5 2.4 %collective-permute-start.28 = (bf16[2,192,128]{2,1,0:T(8,128)(2,1)S(1)}, bf16[2,192,128]{2,1,0:T(8,128)(2,1)S(1)}, u32[]{:S(2)}, u32[]{:S(2)}) collective-permute-start(bf16[2,192,128]{2,1,0:T(8,128)(2,1)S(1)} %get-tuple-element.71), channel_id=1, source_target_pairs={{0,6},{1,7},{2,4},{3,5},{4,2},{5,3},{6,0},{7,1},{8,14},{9,15},{10,... | collective-permute-start | bytes 294920 | tf_op jit(solution)/shard_map/ppermute | solution.py:33
  (90 shorter events, 38.7 us)
Async XLA Ops:
  20.5 83.1 %collective-permute-start = (bf16[3,192,128]{2,1,0:T(8,128)(2,1)}, bf16[3,192,128]{2,1,0:T(8,128)(2,1)S(1)}, u32[]{:S(2)}, u32[]{:S(2)}) collective-permute-start(bf16[3,192,128]{2,1,0:T(8,128)(2,1)} %get-tuple-element.42), channel_id=1, source_target_pairs={{0,4},{1,5},{2,6},{3,7},{4,0},{5,1},{6,2},{7,3},{8,12},{9,13},{10,... | collective-permute-start | bytes 442376 | tf_op jit(solution)/shard_map/ppermute | solution.py:33
  22.1 81.6 %collective-permute-start.1 = (bf16[3,192,128]{2,1,0:T(8,128)(2,1)}, bf16[3,192,128]{2,1,0:T(8,128)(2,1)S(1)}, u32[]{:S(2)}, u32[]{:S(2)}) collective-permute-start(bf16[3,192,128]{2,1,0:T(8,128)(2,1)} %get-tuple-element.43), channel_id=1, source_target_pairs={{0,2},{1,3},{2,0},{3,1},{4,6},{5,7},{6,4},{7,5},{8,10},{9,11},{10,... | collective-permute-start | bytes 442376 | tf_op jit(solution)/shard_map/ppermute | solution.py:33
  23.6 80.1 %collective-permute-start.2 = (bf16[3,192,128]{2,1,0:T(8,128)(2,1)}, bf16[3,192,128]{2,1,0:T(8,128)(2,1)S(1)}, u32[]{:S(2)}, u32[]{:S(2)}) collective-permute-start(bf16[3,192,128]{2,1,0:T(8,128)(2,1)} %get-tuple-element.44), channel_id=1, source_target_pairs={{0,6},{1,7},{2,4},{3,5},{4,2},{5,3},{6,0},{7,1},{8,14},{9,15},{10,... | collective-permute-start | bytes 442376 | tf_op jit(solution)/shard_map/ppermute | solution.py:33
  104.9 11.9 %collective-permute-start.4 = (bf16[2,2,384,128]{3,2,1,0:T(8,128)(2,1)S(1)}, bf16[2,2,384,128]{3,2,1,0:T(8,128)(2,1)S(1)}, u32[]{:S(2)}, u32[]{:S(2)}) collective-permute-start(bf16[2,2,384,128]{3,2,1,0:T(8,128)(2,1)S(1)} %get-tuple-element.48.ka.va), channel_id=1, source_target_pairs={{0,8},{1,9},{2,10},{3,11},{4,12},{5,13},{6,14},{7,15},{8,16},{9,17... | collective-permute-start | bytes 1179656 | tf_op jit(solution)/shard_map/ppermute | solution.py:33
  110.0 9.9 %collective-permute-start.11 = (bf16[6,192,128]{2,1,0:T(8,128)(2,1)S(1)}, bf16[6,192,128]{2,1,0:T(8,128)(2,1)S(1)}, u32[]{:S(2)}, u32[]{:S(2)}) collective-permute-start(bf16[6,192,128]{2,1,0:T(8,128)(2,1)S(1)} %copy-done.9), channel_id=1, source_target_pairs={{0,2},{1,3},{2,0},{3,1},{4,6},{5,7},{6,4},{7,5},{8,10},{9,11},{10,... | collective-permute-start | bytes 884744 | tf_op jit(solution)/shard_map/ppermute | solution.py:33
  111.5 14.5 %collective-permute-start.12 = (bf16[6,192,128]{2,1,0:T(8,128)(2,1)S(1)}, bf16[6,192,128]{2,1,0:T(8,128)(2,1)S(1)}, u32[]{:S(2)}, u32[]{:S(2)}) collective-permute-start(bf16[6,192,128]{2,1,0:T(8,128)(2,1)S(1)} %copy-done.8), channel_id=1, source_target_pairs={{0,6},{1,7},{2,4},{3,5},{4,2},{5,3},{6,0},{7,1},{8,14},{9,15},{10,... | collective-permute-start | bytes 884744 | tf_op jit(solution)/shard_map/ppermute | solution.py:33
  111.9 17.7 %collective-permute-start.9 = (bf16[1,2,384,128]{3,2,1,0:T(8,128)(2,1)S(1)}, bf16[1,2,384,128]{3,2,1,0:T(8,128)(2,1)S(1)}, u32[]{:S(2)}, u32[]{:S(2)}) collective-permute-start(bf16[1,2,384,128]{3,2,1,0:T(8,128)(2,1)S(1)} %get-tuple-element.47.refs_4_.q), channel_id=1, source_target_pairs={{8,0},{9,1},{10,2},{11,3},{12,4},{13,5},{14,6},{15,7},{16,8},{17,9... | collective-permute-start | bytes 589832 | tf_op jit(solution)/shard_map/ppermute | solution.py:33
  116.8 16.3 %collective-permute-start.5 = (bf16[2,2,384,128]{3,2,1,0:T(8,128)(2,1)S(1)}, bf16[2,2,384,128]{3,2,1,0:T(8,128)(2,1)S(1)}, u32[]{:S(2)}, u32[]{:S(2)}) collective-permute-start(bf16[2,2,384,128]{3,2,1,0:T(8,128)(2,1)S(1)} %collective-permute-done.4.ka.va.ua.xa), channel_id=1, source_target_pairs={{0,1},{1,0},{2,3},{3,2},{4,5},{5,4},{6,7},{7,6},{8,9},{9,8},{10,11... | collective-permute-start | bytes 1179656 | tf_op jit(solution)/shard_map/ppermute | solution.py:33
  117.5 18.4 %collective-permute-start.6 = (bf16[6,192,128]{2,1,0:T(8,128)(2,1)S(1)}, bf16[6,192,128]{2,1,0:T(8,128)(2,1)S(1)}, u32[]{:S(2)}, u32[]{:S(2)}) collective-permute-start(bf16[6,192,128]{2,1,0:T(8,128)(2,1)S(1)} %copy-done.7), channel_id=1, source_target_pairs={{0,4},{1,5},{2,6},{3,7},{4,0},{5,1},{6,2},{7,3},{8,12},{9,13},{10,... | collective-permute-start | bytes 884744 | tf_op jit(solution)/shard_map/ppermute | solution.py:33
  119.9 16.0 %collective-permute-start.7 = (bf16[6,192,128]{2,1,0:T(8,128)(2,1)S(1)}, bf16[6,192,128]{2,1,0:T(8,128)(2,1)S(1)}, u32[]{:S(2)}, u32[]{:S(2)}) collective-permute-start(bf16[6,192,128]{2,1,0:T(8,128)(2,1)S(1)} %copy-done.6), channel_id=1, source_target_pairs={{0,2},{1,3},{2,0},{3,1},{4,6},{5,7},{6,4},{7,5},{8,10},{9,11},{10,... | collective-permute-start | bytes 884744 | tf_op jit(solution)/shard_map/ppermute | solution.py:33
  126.0 10.2 %collective-permute-start.8 = (bf16[6,192,128]{2,1,0:T(8,128)(2,1)S(1)}, bf16[6,192,128]{2,1,0:T(8,128)(2,1)S(1)}, u32[]{:S(2)}, u32[]{:S(2)}) collective-permute-start(bf16[6,192,128]{2,1,0:T(8,128)(2,1)S(1)} %copy-done.5), channel_id=1, source_target_pairs={{0,6},{1,7},{2,4},{3,5},{4,2},{5,3},{6,0},{7,1},{8,14},{9,15},{10,... | collective-permute-start | bytes 884744 | tf_op jit(solution)/shard_map/ppermute | solution.py:33
  129.6 22.3 %collective-permute-start.15 = (bf16[4,2,384,128]{3,2,1,0:T(8,128)(2,1)S(1)}, bf16[4,2,384,128]{3,2,1,0:T(8,128)(2,1)S(1)}, u32[]{:S(2)}, u32[]{:S(2)}) collective-permute-start(bf16[4,2,384,128]{3,2,1,0:T(8,128)(2,1)S(1)} %get-tuple-element.59.ka.va), channel_id=1, source_target_pairs={{0,8},{1,9},{2,10},{3,11},{4,12},{5,13},{6,14},{7,15},{8,16},{9,17... | collective-permute-start | bytes 2359304 | tf_op jit(solution)/shard_map/ppermute | solution.py:33
  137.4 25.2 %collective-permute-start.23 = (bf16[4,2,384,128]{3,2,1,0:T(8,128)(2,1)S(1)}, bf16[4,2,384,128]{3,2,1,0:T(8,128)(2,1)S(1)}, u32[]{:S(2)}, u32[]{:S(2)}) collective-permute-start(bf16[4,2,384,128]{3,2,1,0:T(8,128)(2,1)S(1)} %get-tuple-element.66.ka.va), channel_id=1, source_target_pairs={{0,8},{1,9},{2,10},{3,11},{4,12},{5,13},{6,14},{7,15},{8,16},{9,17... | collective-permute-start | bytes 2359304 | tf_op jit(solution)/shard_map/ppermute | solution.py:33
  151.9 21.5 %collective-permute-start.16 = (bf16[4,2,384,128]{3,2,1,0:T(8,128)(2,1)S(1)}, bf16[4,2,384,128]{3,2,1,0:T(8,128)(2,1)S(1)}, u32[]{:S(2)}, u32[]{:S(2)}) collective-permute-start(bf16[4,2,384,128]{3,2,1,0:T(8,128)(2,1)S(1)} %collective-permute-done.15.ka.va.ua.xa), channel_id=1, source_target_pairs={{0,1},{1,0},{2,3},{3,2},{4,5},{5,4},{6,7},{7,6},{8,9},{9,8},{10,11... | collective-permute-start | bytes 2359304 | tf_op jit(solution)/shard_map/ppermute | solution.py:33
  151.9 30.8 %collective-permute-start.14 = (bf16[4,2,384,128]{3,2,1,0:T(8,128)(2,1)S(1)}, bf16[4,2,384,128]{3,2,1,0:T(8,128)(2,1)S(1)}, u32[]{:S(2)}, u32[]{:S(2)}) collective-permute-start(bf16[4,2,384,128]{3,2,1,0:T(8,128)(2,1)S(1)} %get-tuple-element.59.ka.va), channel_id=1, source_target_pairs={{0,1},{1,0},{2,3},{3,2},{4,5},{5,4},{6,7},{7,6},{8,9},{9,8},{10,11... | collective-permute-start | bytes 2359304 | tf_op jit(solution)/shard_map/ppermute | solution.py:33
  152.4 10.2 %collective-permute-start.3 = (bf16[2,2,384,128]{3,2,1,0:T(8,128)(2,1)S(1)}, bf16[2,2,384,128]{3,2,1,0:T(8,128)(2,1)S(1)}, u32[]{:S(2)}, u32[]{:S(2)}) collective-permute-start(bf16[2,2,384,128]{3,2,1,0:T(8,128)(2,1)S(1)} %get-tuple-element.48.ka.va), channel_id=1, source_target_pairs={{0,1},{1,0},{2,3},{3,2},{4,5},{5,4},{6,7},{7,6},{8,9},{9,8},{10,11... | collective-permute-start | bytes 1179656 | tf_op jit(solution)/shard_map/ppermute | solution.py:33
  152.4 13.4 %collective-permute-start.17 = (bf16[2,2,384,128]{3,2,1,0:T(8,128)(2,1)S(1)}, bf16[2,2,384,128]{3,2,1,0:T(8,128)(2,1)S(1)}, u32[]{:S(2)}, u32[]{:S(2)}) collective-permute-start(bf16[2,2,384,128]{3,2,1,0:T(8,128)(2,1)S(1)} %get-tuple-element.55.rest_0_.q), channel_id=1, source_target_pairs={{8,0},{9,1},{10,2},{11,3},{12,4},{13,5},{14,6},{15,7},{16,8},{17,9... | collective-permute-start | bytes 1179656 | tf_op jit(solution)/shard_map/ppermute | solution.py:33
  162.6 34.4 %collective-permute-start.24 = (bf16[4,2,384,128]{3,2,1,0:T(8,128)(2,1)S(1)}, bf16[4,2,384,128]{3,2,1,0:T(8,128)(2,1)S(1)}, u32[]{:S(2)}, u32[]{:S(2)}) collective-permute-start(bf16[4,2,384,128]{3,2,1,0:T(8,128)(2,1)S(1)} %collective-permute-done.23.ka.va.ua.xa), channel_id=1, source_target_pairs={{0,1},{1,0},{2,3},{3,2},{4,5},{5,4},{6,7},{7,6},{8,9},{9,8},{10,11... | collective-permute-start | bytes 2359304 | tf_op jit(solution)/shard_map/ppermute | solution.py:33
  162.6 42.1 %collective-permute-start.22 = (bf16[4,2,384,128]{3,2,1,0:T(8,128)(2,1)S(1)}, bf16[4,2,384,128]{3,2,1,0:T(8,128)(2,1)S(1)}, u32[]{:S(2)}, u32[]{:S(2)}) collective-permute-start(bf16[4,2,384,128]{3,2,1,0:T(8,128)(2,1)S(1)} %get-tuple-element.66.ka.va), channel_id=1, source_target_pairs={{0,1},{1,0},{2,3},{3,2},{4,5},{5,4},{6,7},{7,6},{8,9},{9,8},{10,11... | collective-permute-start | bytes 2359304 | tf_op jit(solution)/shard_map/ppermute | solution.py:33
  165.8 31.1 %collective-permute-start.25 = (bf16[2,2,384,128]{3,2,1,0:T(8,128)(2,1)S(1)}, bf16[2,2,384,128]{3,2,1,0:T(8,128)(2,1)S(1)}, u32[]{:S(2)}, u32[]{:S(2)}) collective-permute-start(bf16[2,2,384,128]{3,2,1,0:T(8,128)(2,1)S(1)} %get-tuple-element.56.rest_0_.q), channel_id=1, source_target_pairs={{8,0},{9,1},{10,2},{11,3},{12,4},{13,5},{14,6},{15,7},{16,8},{17,9... | collective-permute-start | bytes 1179656 | tf_op jit(solution)/shard_map/ppermute | solution.py:33
  173.4 22.8 %collective-permute-start.13 = (bf16[1,800,128]{2,1,0:T(8,128)(2,1)S(1)}, bf16[1,800,128]{2,1,0:T(8,128)(2,1)S(1)}, u32[]{:S(2)}, u32[]{:S(2)}) collective-permute-start(bf16[1,800,128]{2,1,0:T(8,128)(2,1)S(1)} %remote.3.refs_4_), channel_id=1, source_target_pairs={{0,8},{1,9},{2,10},{3,11},{4,12},{5,13},{6,14},{7,15},{8,16},{9,17... | collective-permute-start | bytes 614408 | tf_op jit(solution)/shard_map/ppermute | solution.py:33
  182.7 32.1 %collective-permute-start.21 = (bf16[2,800,128]{2,1,0:T(8,128)(2,1)S(1)}, bf16[2,800,128]{2,1,0:T(8,128)(2,1)S(1)}, u32[]{:S(2)}, u32[]{:S(2)}) collective-permute-start(bf16[2,800,128]{2,1,0:T(8,128)(2,1)S(1)} %remote.4.rest_0_), channel_id=1, source_target_pairs={{0,8},{1,9},{2,10},{3,11},{4,12},{5,13},{6,14},{7,15},{8,16},{9,17... | collective-permute-start | bytes 1228808 | tf_op jit(solution)/shard_map/ppermute | solution.py:33
  202.6 16.8 %collective-permute-start.29 = (bf16[2,800,128]{2,1,0:T(8,128)(2,1)S(1)}, bf16[2,800,128]{2,1,0:T(8,128)(2,1)S(1)}, u32[]{:S(2)}, u32[]{:S(2)}) collective-permute-start(bf16[2,800,128]{2,1,0:T(8,128)(2,1)S(1)} %remote.5.rest_0_), channel_id=1, source_target_pairs={{0,8},{1,9},{2,10},{3,11},{4,12},{5,13},{6,14},{7,15},{8,16},{9,17... | collective-permute-start | bytes 1228808 | tf_op jit(solution)/shard_map/ppermute | solution.py:33
  215.8 9.7 %collective-permute-start.26 = (bf16[2,192,128]{2,1,0:T(8,128)(2,1)S(1)}, bf16[2,192,128]{2,1,0:T(8,128)(2,1)S(1)}, u32[]{:S(2)}, u32[]{:S(2)}) collective-permute-start(bf16[2,192,128]{2,1,0:T(8,128)(2,1)S(1)} %get-tuple-element.69), channel_id=1, source_target_pairs={{0,4},{1,5},{2,6},{3,7},{4,0},{5,1},{6,2},{7,3},{8,12},{9,13},{10,... | collective-permute-start | bytes 294920 | tf_op jit(solution)/shard_map/ppermute | solution.py:33
  (22 other events, 471.5 us)

commit v3 on v2

v3 whole, which is shorter than its diff:
```python
import functools
import math

import jax
import jax.numpy as jnp
from jax import lax
from jax.experimental import pallas as pl
from jax.experimental.pallas import tpu as pltpu
from jax.sharding import PartitionSpec as P

HEAD_DIM = 128
AXES = ("span", "seq")
ANY = pl.BlockSpec(memory_space=pl.ANY)
SMEM = pl.BlockSpec(memory_space=pltpu.SMEM)
MIB = 1024 * 1024
TILE = 128
SIZES = (3, 2)
COST = 1000
ORDER = "s0 n0 s10 n1 r0 f01 r1 f1 c0 c1"
NT = (((1,), (1,)), ((), ()))
NN = (((1,), (0,)), ((), ()))


def params(mib):
    return pltpu.CompilerParams(vmem_limit_bytes=mib * MIB)


def move(block, target):
    spans, members = lax.axis_size("span"), lax.axis_size("seq")
    route = []
    for device in range(spans * members):
        span, member = divmod(device, members)
        to_span, to_member = target(span, member)
        if 0 <= to_span < spans:
            route.append((device, to_span * members + to_member))
    return lax.ppermute(block, AXES, route)


def within_level(dx, dy):
    return lambda span, member: (span ^ dy, member ^ (2 * dx))


def other_core(span, member):
    return span, member ^ 1


def one_up(span, member):
    return span + 2, member


def one_down(span, member):
    return span - 2, member


PLACES = ((0, 0), (0, 1), (1, 0), (1, 1))


def timestep_gate(level_index, plan, gate_weight, span_number):
    noise_level = jnp.sum(
        jnp.where(jnp.arange(level_index.shape[0], dtype=jnp.int32) == span_number, level_index, 0)
    )
    timestep = jnp.sum(
        jnp.where(jnp.arange(plan.shape[0], dtype=jnp.int32) == noise_level, plan, 0)
    )
    half_freq = gate_weight.shape[0] // 2
    frequencies = jnp.exp(-math.log(10000.0) * jnp.arange(half_freq, dtype=jnp.float32) / half_freq)
    angles = timestep.astype(jnp.float32) * frequencies
    embedding = jnp.concatenate([jnp.cos(angles), jnp.sin(angles)])[None, :]
    return jnp.dot(
        embedding, gate_weight, precision=lax.Precision.HIGHEST, preferred_element_type=jnp.float32
    )


def pack_kernel(firsts, sizes, group_width, meta, q, k, v, *outs):
    for i, (first, heads) in enumerate(zip(firsts, sizes)):
        for j in range(4):
            for t, ref in enumerate((q, k, v)):
                for h in range(heads):
                    column = meta[j] * group_width + (first + h) * HEAD_DIM
                    at = pl.ds(pl.multiple_of(column, HEAD_DIM), HEAD_DIM)
                    outs[4 * i + j][t * heads + h] = ref[:, at]


def pack(meta, q, k, v, firsts, sizes, group_width):
    rows = q.shape[0]
    whole = pl.BlockSpec(memory_space=pltpu.VMEM)
    outs = pl.pallas_call(
        functools.partial(pack_kernel, firsts, sizes, group_width),
        out_shape=[
            jax.ShapeDtypeStruct((3 * heads, rows, HEAD_DIM), q.dtype)
            for heads in sizes
            for _ in PLACES
        ],
        in_specs=[SMEM, whole, whole, whole],
        out_specs=[whole] * (4 * len(sizes)),
        compiler_params=params(60),
        cost_estimate=pl.CostEstimate(flops=COST, bytes_accessed=COST, transcendentals=0),
        name="pack",
    )(meta, q, k, v)
    return [outs[4 * i : 4 * i + 4] for i in range(len(sizes))]


def stack_kernel(heads, count, meta, *refs):
    pieces, outs = refs[:4], refs[4 + count :]
    (q_out, kv_out), sems = outs[:2], outs[-1]
    rows = pieces[0].shape[1]
    copies = []
    for j, (dx, _) in enumerate(PLACES):
        parity = meta[4 + j]
        at = pl.ds(dx * rows, rows)
        for t, (source, target) in enumerate(
            (
                (pieces[j].at[pl.ds(heads, 2 * heads)], kv_out.at[:, parity, at]),
                (pieces[j].at[pl.ds(0, heads)], q_out.at[:, parity, at]),
            )
        ):
            copy = pltpu.make_async_copy(source, target, sems.at[j, t])
            copy.start()
            copies.append(copy)
    for copy in copies:
        copy.wait()


def stack(meta, pieces, later, after):
    triple, rows, _ = pieces[0].shape
    heads = triple // 3
    dtype = pieces[0].dtype
    outs = pl.pallas_call(
        functools.partial(stack_kernel, heads, len(later) + len(after)),
        out_shape=[
            jax.ShapeDtypeStruct((heads, 2, 2 * rows, HEAD_DIM), dtype),
            jax.ShapeDtypeStruct((2 * heads, 2, 2 * rows, HEAD_DIM), dtype),
        ]
        + [jax.ShapeDtypeStruct(block.shape, block.dtype) for block in later],
        in_specs=[SMEM] + [ANY] * (4 + len(later) + len(after)),
        out_specs=[ANY] * (2 + len(later)),
        scratch_shapes=[pltpu.SemaphoreType.DMA((4, 2))],
        input_output_aliases={5 + n: 2 + n for n in range(len(later))},
        compiler_params=params(8),
        cost_estimate=pl.CostEstimate(flops=COST, bytes_accessed=COST, transcendentals=0),
        name="stack",
    )(meta, *pieces, *later, *after)
    return outs[0], outs[1], outs[2:]


def softmax_part(q, keys, values):
    scale = math.log2(math.e) / math.sqrt(HEAD_DIM)
    scores = [lax.dot_general(q, k, NT, preferred_element_type=jnp.float32) for k in keys]
    peak = functools.reduce(jnp.maximum, scores).max(axis=1, keepdims=True)
    peak = peak * scale
    weights = [jnp.exp2(s * scale - peak) for s in scores]
    total = functools.reduce(jnp.add, weights).sum(axis=1, keepdims=True)
    out = functools.reduce(
        jnp.add,
        [
            lax.dot_general(w.astype(jnp.bfloat16), v, NN, preferred_element_type=jnp.float32)
            for w, v in zip(weights, values)
        ],
    )
    return out / total, peak + jnp.log2(total)


def attend_rows(q_ref, p, blocks, o_ref, lse_ref):
    rows = q_ref.shape[2]
    out, lse = softmax_part(
        q_ref[0, p], [kv[0][0, i] for kv, i in blocks], [kv[1][0, i] for kv, i in blocks]
    )
    o_ref[0, pl.ds(p * rows, rows)] = out.astype(o_ref.dtype)
    for t in range(rows // TILE):
        column = jnp.broadcast_to(lse[t * TILE : (t + 1) * TILE], (TILE, TILE))
        lse_ref[pl.ds(p * (rows // TILE) + t, 1)] = column.T[:1]


def remote_kernel(count, q, ka, va, kb, vb, *rest):
    o, lse = rest[count:]
    a, b = (ka, va), (kb, vb)
    every = [(a, 0), (b, 0), (a, 1), (b, 1)]
    attend_rows(q, 0, every, o, lse)
    attend_rows(q, 1, every[2:], o, lse)
    left, terms = lse[...], []
    for _ in range(3):
        terms.append(left.astype(jnp.bfloat16))
        left = left - terms[-1].astype(jnp.float32)
    terms.append(jnp.zeros_like(terms[0]))
    last = 2 * q.shape[2]
    o[0, pl.ds(last, 4 * lse.shape[0])] = jnp.concatenate(
        [term.astype(jnp.float32) for term in terms], axis=0
    ).astype(jnp.bfloat16)


def near_kernel(count, q, ka, va, kb, vb, *rest):
    o, lse = rest[count:]
    a, b = (ka, va), (kb, vb)
    own = [(a, 0), (b, 0), (a, 1), (b, 1)]
    attend_rows(q, 0, own[:2], o, lse.at[0])
    attend_rows(q, 1, own, o, lse.at[0])


def blend(first, first_lse, other, other_lse, usable, store):
    share = jnp.where(usable, 1.0, 0.0) / (1.0 + jnp.exp2(first_lse - other_lse))
    for row in range(first.shape[1] // TILE):
        at = pl.ds(row * TILE, TILE)
        weight = jnp.broadcast_to(share[row : row + 1], (HEAD_DIM, TILE)).T
        start = first[0, at]
        store(at, start + weight * (other[0, at].astype(jnp.float32) - start))
    more = jnp.log2(1.0 + jnp.exp2(-jnp.abs(first_lse - other_lse)))
    return jnp.where(usable, jnp.maximum(first_lse, other_lse) + more, first_lse)


def far_kernel(count, meta, q, ka, va, kb, vb, o_near, lse_near, *rest):
    o, lse, part, part_lse = rest[count:]
    a, b = (ka, va), (kb, vb)
    every = [(a, 0), (b, 0), (a, 1), (b, 1)]

    def store(at, block):
        o[0, at] = block

    @pl.when(meta[8] >= 1)
    def _():
        attend_rows(q, 0, every, part, part_lse)
        attend_rows(q, 1, every, part, part_lse)
        lse[0] = blend(o_near, lse_near[0], part, part_lse[...], True, store)

    @pl.when(meta[8] < 1)
    def _():
        o[...] = o_near[...]
        lse[...] = lse_near[...]


def in_order_kernel(*refs):
    pass


def in_order(block, after):
    return pl.pallas_call(
        in_order_kernel,
        out_shape=jax.ShapeDtypeStruct(block.shape, block.dtype),
        in_specs=[ANY] * (1 + len(after)),
        out_specs=ANY,
        input_output_aliases={0: 0},
        compiler_params=params(1),
        cost_estimate=pl.CostEstimate(flops=COST, bytes_accessed=COST, transcendentals=0),
        name="in_order",
    )(block, *after)


def lse_rows(rows):
    return -(-2 * rows // TILE // 8) * 8


def attend(body, meta, q, kv, near, after):
    heads, _, rows, _ = q.shape
    block = (1, 2, rows, HEAD_DIM)
    head = pl.BlockSpec(block, lambda h: (h, 0, 0, 0))
    value = pl.BlockSpec(block, lambda h: (heads + h, 0, 0, 0))
    extra = lse_rows(rows)
    by_head = lambda h: (h, 0, 0)
    o_spec = pl.BlockSpec((1, 2 * rows, HEAD_DIM), by_head)
    lse_spec = pl.BlockSpec((1, extra, TILE), by_head)
    part_lse = pltpu.VMEM((extra, TILE), jnp.float32)
    operands = [q] + [half for half in kv for _ in range(2)]
    specs = [head] + [head, value] * 2
    out_shape = [
        jax.ShapeDtypeStruct((heads, 2 * rows, HEAD_DIM), jnp.float32),
        jax.ShapeDtypeStruct((heads, extra, TILE), jnp.float32),
    ]
    out_specs, scratch = [o_spec, lse_spec], []
    if body is remote_kernel:
        length = 2 * rows + 4 * extra
        out_shape = jax.ShapeDtypeStruct((heads, length, HEAD_DIM), jnp.bfloat16)
        out_specs = pl.BlockSpec((1, length, HEAD_DIM), by_head)
        scratch = [part_lse]
    if body is far_kernel:
        operands = [meta] + operands + list(near)
        specs = [SMEM] + specs + [o_spec, lse_spec]
        scratch = [pltpu.VMEM((1, 2 * rows, HEAD_DIM), jnp.float32), part_lse]
    return pl.pallas_call(
        functools.partial(body, len(after)),
        grid=(heads,),
        out_shape=out_shape,
        in_specs=specs + [ANY] * len(after),
        out_specs=out_specs,
        scratch_shapes=scratch,
        compiler_params=params(20),
        cost_estimate=pl.CostEstimate(flops=COST, bytes_accessed=COST, transcendentals=0),
        name=body.__name__[:-7],
    )(*operands, *after)


def merge_kernel(count, meta, o, lse, o_far, *rest):
    outs, scratch = rest[count : count + 4], rest[count + 4]
    rows = o.shape[1] // 2
    half = rows // 2
    extra = lse.shape[1]
    terms = o_far[0, pl.ds(2 * rows, 4 * extra)].astype(jnp.float32)
    lse_far = terms[:extra] + terms[extra : 2 * extra] + terms[2 * extra : 3 * extra]

    def store(at, block):
        scratch[at] = block

    blend(o, lse[0], o_far, lse_far, meta[8] >= 2, store)
    for j, (dx, _) in enumerate(PLACES):
        at = pl.ds(pl.multiple_of(meta[4 + j] * rows + dx * half, half), half)
        outs[j][0] = scratch[at].astype(outs[j].dtype)


def merge(meta, o, lse, o_far, after):
    heads, both, _ = o.shape
    by_head = lambda h: (h, 0, 0)
    return pl.pallas_call(
        functools.partial(merge_kernel, len(after)),
        grid=(heads,),
        out_shape=[jax.ShapeDtypeStruct((heads, both // 4, HEAD_DIM), jnp.bfloat16)] * 4,
        in_specs=[SMEM]
        + [pl.BlockSpec((1,) + a.shape[1:], by_head) for a in (o, lse, o_far)]
        + [ANY] * len(after),
        out_specs=[pl.BlockSpec((1, both // 4, HEAD_DIM), by_head)] * 4,
        scratch_shapes=[pltpu.VMEM((both, HEAD_DIM), jnp.float32)],
        compiler_params=params(12),
        cost_estimate=pl.CostEstimate(flops=COST, bytes_accessed=COST, transcendentals=0),
        name="merge",
    )(meta, o, lse, o_far, *after)


def finish_kernel(firsts, group_width, meta, gate, *refs):
    pieces, out = refs[:-1], refs[-1]
    for i, piece in enumerate(pieces):
        chunk, j = divmod(i, 4)
        for h in range(piece.shape[0]):
            column = meta[j] * group_width + (firsts[chunk] + h) * HEAD_DIM
            at = pl.ds(pl.multiple_of(column, HEAD_DIM), HEAD_DIM)
            out[:, at] = (gate[:, at] * piece[h].astype(jnp.float32)).astype(out.dtype)


def finish(meta, gate, pieces, firsts, group_width):
    rows = pieces[0].shape[1]
    whole = pl.BlockSpec(memory_space=pltpu.VMEM)
    return pl.pallas_call(
        functools.partial(finish_kernel, firsts, group_width),
        out_shape=jax.ShapeDtypeStruct((rows, 4 * group_width), jnp.bfloat16),
        in_specs=[SMEM] + [whole] * (1 + len(pieces)),
        out_specs=whole,
        compiler_params=params(16),
        cost_estimate=pl.CostEstimate(flops=COST, bytes_accessed=COST, transcendentals=0),
        name="finish",
    )(meta, gate, *pieces)


def chunk_sizes(heads):
    sizes = []
    for size in SIZES:
        if sum(sizes) + size <= heads:
            sizes.append(size)
    return sizes + [1] * (heads - sum(sizes))


def shards(queries, keys, values, level_index, plan, gate_weight):
    span = lax.axis_index("span")
    member = lax.axis_index("seq")
    x, y = member // 2, span % 2
    group_width = queries.shape[1] // 4
    group_heads = group_width // HEAD_DIM
    meta = jnp.stack(
        [2 * (x ^ dx) + (y ^ dy) for dx, dy in PLACES]
        + [y ^ dy for _, dy in PLACES]
        + [span // 2]
    ).astype(jnp.int32)
    gate = timestep_gate(level_index, plan, gate_weight, span)

    sizes = chunk_sizes(group_heads)
    firsts = [sum(sizes[:i]) for i in range(len(sizes))]
    chunks = range(len(sizes))

    sent = pack(meta, queries, keys, values, firsts, sizes, group_width)
    last = [gate]

    q, kv, kv_up, q_down = {}, {}, {}, {}
    far, own, results = {}, {}, {}

    def exchange(blocks):
        return [blocks[0]] + [move(blocks[j], within_level(*PLACES[j])) for j in (1, 2, 3)]

    exchanged = {0: exchange(sent[0])}

    def spread(i, after):
        pieces = exchanged.pop(i)
        later = sent[i + 1] if i + 1 < len(sizes) else []
        q[i], kv[i], later = stack(meta, pieces, later[1:], after)
        if later:
            exchanged[i + 1] = exchange([sent[i + 1][0], *later])
        kv_up[i] = move(kv[i], one_up)
        q_down[i] = move(q[i], one_down)
        kv[i] = (kv[i], move(kv[i], other_core))
        return [q[i]]

    def near(i, after):
        own[i] = attend(near_kernel, meta, q[i], kv[i], None, after)
        return [own[i][1]]

    def remote(i, after):
        held = in_order(kv_up[i], after)
        kv_up[i] = (held, move(held, other_core))
        part = attend(remote_kernel, meta, q_down[i], kv_up[i], None, [])
        far[i] = move(part, one_up)
        return [part]

    def own_far(i, after):
        own[i] = attend(far_kernel, meta, q[i], kv_up[i], own[i], after)
        return [own[i][1]]

    def close(i, after):
        merged = merge(meta, *own[i], far[i], after)
        results[i] = exchange(merged)
        return [merged[0]]

    steps = {"s": spread, "n": near, "r": remote, "f": own_far, "c": close}
    for step in ORDER.split():
        kind, i = step[0], int(step[1])
        extra = [q_down[int(j)] for j in step[2:]]
        last = steps[kind](i, last + extra)
    return finish(meta, gate, sum((results[i] for i in chunks), []), firsts, group_width)


def solution(mesh):
    rows = P(AXES, None)
    return jax.shard_map(
        shards,
        mesh=mesh,
        in_specs=(rows, rows, rows, P(), P(), P()),
        out_specs=rows,
        check_vma=False,
    )
```

time: 233 us -> 125 us (0.54)
  Pallas kernels: 143 us -> 42.2 us
  starting transfers between devices: 49.8 us -> 31.9 us
  waiting for transfers between devices: 35.3 us -> 45.8 us
    pallas_call x12 -> x11, Pallas kernels: 138 us -> 38.3 us  [the longest x6 31.2 us: attend(): pl.pallas_call(functools.partial(body, len(after)), grid=(heads,), out_sh...]
    ppermute x33 -> x22, starting transfers between devices: 49.8 us -> 31.9 us  [move(): return lax.ppermute(block, AXES, route)]
    ppermute x33 -> x22, waiting for transfers between devices: 35.3 us -> 45.8 us  [move(): return lax.ppermute(block, AXES, route)]
  transfers between devices with their start and end apart: 33 -> 22, of which waited for: 12 -> 14; matrix products, arithmetic and copies ran while one was open for 1% -> 3% of each run, Pallas kernels for 52% -> 28%
where the time goes in v3:
time: 125 us
  waiting for transfers between devices  45.8 us (37%)
  Pallas kernels  42.2 us (34%)
  starting transfers between devices  31.9 us (26%)
  other arithmetic  1.82 us (1%)
  matrix products  1.34 us (1%)
    ppermute x22, waiting for transfers between devices, move(): return lax.ppermute(block, AXES, route)  45.8 us
    ppermute x22, starting transfers between devices, move(): return lax.ppermute(block, AXES, route)  31.9 us
    pallas_call x6, Pallas kernels, attend(): pl.pallas_call(functools.partial(body, len(after)), grid=(heads,), out_sh...  31.2 us
    pallas_call x1, Pallas kernels, pack(): pl.pallas_call(functools.partial(pack_kernel, firsts, sizes, group_width)...  4.11 us
    pallas_call x2, Pallas kernels, stack(): pl.pallas_call(functools.partial(stack_kernel, heads, len(later) + len(af...  3.03 us
  transfers between devices with their start and end apart: 22, of which 14 were waited for; matrix products, arithmetic and copies ran while one was open for 3% of the time, Pallas kernels for 28%

profile of v3, /device:TPU:8, one launch (start us, length us, event | category | flops | bytes accessed | tf_op | source)
XLA Modules:
  0.0 124.5 jit_solution(4043559479820675746)
XLA Ops:
  0.6 4.1 %pack.1 = (bf16[9,192,128]{2,1,0:T(8,128)(2,1)}, bf16[9,192,128]{2,1,0:T(8,128)(2,1)}, bf16[9,192,128]{2,1,0:T(8,128)(2,1)}, bf16[9,192,128]{2,1,0:T(8,128)(2,1)...) custom-call(s32[9]{0:T(128)} %stack.35.meta, ...), custom_call_target="tpu_custom_call" | custom-call | flops 1000 | bytes 1000 | tf_op jit(solution)/shard_map/pack/pallas_call | solution.py:87
  12.0 5.1 %collective-permute-done.refs_1_ = bf16[9,192,128]{2,1,0:T(8,128)(2,1)S(1)} collective-permute-done((bf16[9,192,128]{2,1,0:T(8,128)(2,1)}, bf16[9,192,128]{2,1,0:T(8,128)(2,1)S(1)}, u32[]{:S(2)}, u32[]{:S(2)}) %collective-permute-start) | collective-permute-done | bytes 442400 | tf_op jit(solution)/shard_map/ppermute | solution.py:36
  17.1 2.4 %collective-permute-done.1.refs_2_ = bf16[9,192,128]{2,1,0:T(8,128)(2,1)S(1)} collective-permute-done((bf16[9,192,128]{2,1,0:T(8,128)(2,1)}, bf16[9,192,128]{2,1,0:T(8,128)(2,1)S(1)}, u32[]{:S(2)}, u32[]{:S(2)}) %collective-permute-start.1) | collective-permute-done | bytes 442400 | tf_op jit(solution)/shard_map/ppermute | solution.py:36
  19.5 8.1 %collective-permute-done.2.refs_3_ = bf16[9,192,128]{2,1,0:T(8,128)(2,1)} collective-permute-done((bf16[9,192,128]{2,1,0:T(8,128)(2,1)}, bf16[9,192,128]{2,1,0:T(8,128)(2,1)}, u32[]{:S(2)}, u32[]{:S(2)}) %collective-permute-start.2) | collective-permute-done | bytes 442400 | tf_op jit(solution)/shard_map/ppermute | solution.py:36
  29.6 2.2 %collective-permute-start.8 = (bf16[3,2,384,128]{3,2,1,0:T(8,128)(2,1)S(1)}, bf16[3,2,384,128]{3,2,1,0:T(8,128)(2,1)S(1)}, u32[]{:S(2)}, u32[]{:S(2)}) collective-permute-start(bf16[3,2,384,128]{3,2,1,0:T(8,128)(2,1)S(1)} %get-tuple-element.43.q.rest_0_), channel_id=1, source_target_pairs={{8,0},{9,1},{10,2},{11,3},{12,4},{13,5},{14,6},{15,7},{16,8},{17,9... | collective-permute-start | bytes 1769480 | tf_op jit(solution)/shard_map/ppermute | solution.py:36
  31.8 3.7 %collective-permute-start.3 = (bf16[6,2,384,128]{3,2,1,0:T(8,128)(2,1)S(1)}, bf16[6,2,384,128]{3,2,1,0:T(8,128)(2,1)S(1)}, u32[]{:S(2)}, u32[]{:S(2)}) collective-permute-start(bf16[6,2,384,128]{3,2,1,0:T(8,128)(2,1)S(1)} %get-tuple-element.44.ka.va), channel_id=1, source_target_pairs={{0,8},{1,9},{2,10},{3,11},{4,12},{5,13},{6,14},{7,15},{8,16},{9,17... | collective-permute-start | bytes 3538952 | tf_op jit(solution)/shard_map/ppermute | solution.py:36
  39.0 5.2 %near.2 = (f32[3,768,128]{2,1,0:T(8,128)S(1)}, f32[3,8,128]{2,1,0:T(8,128)S(1)}) custom-call(bf16[3,2,384,128]{3,2,1,0:T(8,128)(2,1)S(1)} %get-tuple-element.43.q.rest_0_, bf16[6,2,384,128]{3,2,1,0:T(8,128)(2,1)S(1)} %get-tuple-element.44.ka.va, bf16[6,2,384,128]{3,2,1,0:T(8,128)(2,1)S(1)} %get-tuple-element.44.ka.va, ...), custom_call_target="tpu_custom_call" | custom-call | flops 1000 | bytes 1000 | tf_op jit(solution)/shard_map/near/pallas_call | solution.py:277
  44.5 2.4 %collective-permute-done.5.refs_2_ = bf16[6,192,128]{2,1,0:T(8,128)(2,1)S(1)} collective-permute-done((bf16[6,192,128]{2,1,0:T(8,128)(2,1)S(1)}, bf16[6,192,128]{2,1,0:T(8,128)(2,1)S(1)}, u32[]{:S(2)}, u32[]{:S(2)}) %collective-permute-start.5) | collective-permute-done | bytes 294944 | tf_op jit(solution)/shard_map/ppermute | solution.py:36
  47.0 4.9 %collective-permute-done.6.refs_3_ = bf16[6,192,128]{2,1,0:T(8,128)(2,1)S(1)} collective-permute-done((bf16[6,192,128]{2,1,0:T(8,128)(2,1)S(1)}, bf16[6,192,128]{2,1,0:T(8,128)(2,1)S(1)}, u32[]{:S(2)}, u32[]{:S(2)}) %collective-permute-start.6) | collective-permute-done | bytes 294944 | tf_op jit(solution)/shard_map/ppermute | solution.py:36
  53.1 2.3 %collective-permute-done.9.kb.vb = bf16[4,2,384,128]{3,2,1,0:T(8,128)(2,1)S(1)} collective-permute-done((bf16[4,2,384,128]{3,2,1,0:T(8,128)(2,1)S(1)}, bf16[4,2,384,128]{3,2,1,0:T(8,128)(2,1)S(1)}, u32[]{:S(2)}, u32[]{:S(2)}) %collective-permute-start.9) | collective-permute-done | bytes 786464 | tf_op jit(solution)/shard_map/ppermute | solution.py:36
  55.4 3.5 %near.3 = (f32[2,768,128]{2,1,0:T(8,128)S(1)}, f32[2,8,128]{2,1,0:T(8,128)S(1)}) custom-call(bf16[2,2,384,128]{3,2,1,0:T(8,128)(2,1)S(1)} %get-tuple-element.50.q.rest_0_, bf16[4,2,384,128]{3,2,1,0:T(8,128)(2,1)S(1)} %get-tuple-element.51.ka.va, bf16[4,2,384,128]{3,2,1,0:T(8,128)(2,1)S(1)} %get-tuple-element.51.ka.va, ...), custom_call_target="tpu_custom_call" | custom-call | flops 1000 | bytes 1000 | tf_op jit(solution)/shard_map/near/pallas_call | solution.py:277
  58.9 2.9 %collective-permute-done.3.refs_0_ = bf16[6,2,384,128]{3,2,1,0:T(8,128)(2,1)S(1)} collective-permute-done((bf16[6,2,384,128]{3,2,1,0:T(8,128)(2,1)S(1)}, bf16[6,2,384,128]{3,2,1,0:T(8,128)(2,1)S(1)}, u32[]{:S(2)}, u32[]{:S(2)}) %collective-permute-start.3) | collective-permute-done | bytes 1179680 | tf_op jit(solution)/shard_map/ppermute | solution.py:36
  61.8 3.6 %collective-permute-start.13 = (bf16[4,2,384,128]{3,2,1,0:T(8,128)(2,1)S(1)}, bf16[4,2,384,128]{3,2,1,0:T(8,128)(2,1)S(1)}, u32[]{:S(2)}, u32[]{:S(2)}) collective-permute-start(bf16[4,2,384,128]{3,2,1,0:T(8,128)(2,1)S(1)} %get-tuple-element.51.ka.va), channel_id=1, source_target_pairs={{0,8},{1,9},{2,10},{3,11},{4,12},{5,13},{6,14},{7,15},{8,16},{9,17... | collective-permute-start | bytes 2359304 | tf_op jit(solution)/shard_map/ppermute | solution.py:36
  65.4 2.2 %collective-permute-start.11 = (bf16[2,2,384,128]{3,2,1,0:T(8,128)(2,1)S(1)}, bf16[2,2,384,128]{3,2,1,0:T(8,128)(2,1)S(1)}, u32[]{:S(2)}, u32[]{:S(2)}) collective-permute-start(bf16[2,2,384,128]{3,2,1,0:T(8,128)(2,1)S(1)} %get-tuple-element.50.q.rest_0_), channel_id=1, source_target_pairs={{8,0},{9,1},{10,2},{11,3},{12,4},{13,5},{14,6},{15,7},{16,8},{17,9... | collective-permute-start | bytes 1179656 | tf_op jit(solution)/shard_map/ppermute | solution.py:36
  67.7 5.7 %remote.2.rest_0_ = bf16[3,800,128]{2,1,0:T(8,128)(2,1)S(1)} custom-call(bf16[3,2,384,128]{3,2,1,0:T(8,128)(2,1)S(1)} %collective-permute-done.8.refs_5_.q, bf16[6,2,384,128]{3,2,1,0:T(8,128)(2,1)S(1)} %in_order.2.ka.va, bf16[6,2,384,128]{3,2,1,0:T(8,128)(2,1)S(1)} %in_order.2.ka.va, bf16[6,2,384,128]{3,2,1,0:T(8,128)(2,1)S(1)} %collective-permute-done.10.kb.vb, ...), custom_call_target="tpu_custom_call" | custom-call | flops 1000 | bytes 1000 | tf_op jit(solution)/shard_map/remote/pallas_call | solution.py:277
  73.4 5.2 %collective-permute-done.11.rest_1_.q = bf16[2,2,384,128]{3,2,1,0:T(8,128)(2,1)S(1)} collective-permute-done((bf16[2,2,384,128]{3,2,1,0:T(8,128)(2,1)S(1)}, bf16[2,2,384,128]{3,2,1,0:T(8,128)(2,1)S(1)}, u32[]{:S(2)}, u32[]{:S(2)}) %collective-permute-start.11) | collective-permute-done | bytes 393248 | tf_op jit(solution)/shard_map/ppermute | solution.py:36
  78.6 7.7 %far.2 = (f32[3,768,128]{2,1,0:T(8,128)S(1)}, f32[3,8,128]{2,1,0:T(8,128)S(1)}) custom-call(s32[9]{0:T(128)S(1)} %copy-done.6, bf16[3,2,384,128]{3,2,1,0:T(8,128)(2,1)S(1)} %get-tuple-element.43.q.rest_0_, bf16[6,2,384,128]{3,2,1,0:T(8,128)(2,1)S(1)} %in_order.2.ka.va, bf16[6,2,384,128]{3,2,1,0:T(8,128)(2,1)S(1)} %in_order.2.ka.va, ...), custom_call_target="tpu_custom_call" | custom-call | flops 1000 | bytes 1000 | tf_op jit(solution)/shard_map/far/pallas_call | solution.py:277
  86.3 3.7 %collective-permute-start.12 = (bf16[3,800,128]{2,1,0:T(8,128)(2,1)S(1)}, bf16[3,800,128]{2,1,0:T(8,128)(2,1)S(1)}, u32[]{:S(2)}, u32[]{:S(2)}) collective-permute-start(bf16[3,800,128]{2,1,0:T(8,128)(2,1)S(1)} %remote.2.rest_0_), channel_id=1, source_target_pairs={{0,8},{1,9},{2,10},{3,11},{4,12},{5,13},{6,14},{7,15},{8,16},{9,17... | collective-permute-start | bytes 1843208 | tf_op jit(solution)/shard_map/ppermute | solution.py:36
  90.1 3.8 %remote.3.rest_0_ = bf16[2,800,128]{2,1,0:T(8,128)(2,1)S(1)} custom-call(bf16[2,2,384,128]{3,2,1,0:T(8,128)(2,1)S(1)} %collective-permute-done.11.rest_1_.q, bf16[4,2,384,128]{3,2,1,0:T(8,128)(2,1)S(1)} %in_order.3.ka.va, bf16[4,2,384,128]{3,2,1,0:T(8,128)(2,1)S(1)} %in_order.3.ka.va, bf16[4,2,384,128]{3,2,1,0:T(8,128)(2,1)S(1)} %collective-permute-done.14.kb.vb, ...), custom_call_target="tpu_custom_call" | custom-call | flops 1000 | bytes 1000 | tf_op jit(solution)/shard_map/remote/pallas_call | solution.py:277
  93.9 2.1 %collective-permute-start.18 = (bf16[2,800,128]{2,1,0:T(8,128)(2,1)S(1)}, bf16[2,800,128]{2,1,0:T(8,128)(2,1)S(1)}, u32[]{:S(2)}, u32[]{:S(2)}) collective-permute-start(bf16[2,800,128]{2,1,0:T(8,128)(2,1)S(1)} %remote.3.rest_0_), channel_id=1, source_target_pairs={{0,8},{1,9},{2,10},{3,11},{4,12},{5,13},{6,14},{7,15},{8,16},{9,17... | collective-permute-start | bytes 1228808 | tf_op jit(solution)/shard_map/ppermute | solution.py:36
  95.9 5.3 %far.3 = (f32[2,768,128]{2,1,0:T(8,128)S(1)}, f32[2,8,128]{2,1,0:T(8,128)S(1)}) custom-call(s32[9]{0:T(128)S(1)} %copy-done.6, bf16[2,2,384,128]{3,2,1,0:T(8,128)(2,1)S(1)} %get-tuple-element.50.q.rest_0_, bf16[4,2,384,128]{3,2,1,0:T(8,128)(2,1)S(1)} %in_order.3.ka.va, bf16[4,2,384,128]{3,2,1,0:T(8,128)(2,1)S(1)} %in_order.3.ka.va, ...), custom_call_target="tpu_custom_call" | custom-call | flops 1000 | bytes 1000 | tf_op jit(solution)/shard_map/far/pallas_call | solution.py:277
  101.3 3.6 %collective-permute-done.12.o_far = bf16[3,800,128]{2,1,0:T(8,128)(2,1)S(1)} collective-permute-done((bf16[3,800,128]{2,1,0:T(8,128)(2,1)S(1)}, bf16[3,800,128]{2,1,0:T(8,128)(2,1)S(1)}, u32[]{:S(2)}, u32[]{:S(2)}) %collective-permute-start.12) | collective-permute-done | bytes 614432 | tf_op jit(solution)/shard_map/ppermute | solution.py:36
  109.7 3.6 %collective-permute-done.18.o_far = bf16[2,800,128]{2,1,0:T(8,128)(2,1)S(1)} collective-permute-done((bf16[2,800,128]{2,1,0:T(8,128)(2,1)S(1)}, bf16[2,800,128]{2,1,0:T(8,128)(2,1)S(1)}, u32[]{:S(2)}, u32[]{:S(2)}) %collective-permute-start.18) | collective-permute-done | bytes 409632 | tf_op jit(solution)/shard_map/ppermute | solution.py:36
  119.0 2.2 %collective-permute-done.20.refs_6_ = bf16[2,192,128]{2,1,0:T(8,128)(2,1)S(1)} collective-permute-done((bf16[2,192,128]{2,1,0:T(8,128)(2,1)S(1)}, bf16[2,192,128]{2,1,0:T(8,128)(2,1)S(1)}, u32[]{:S(2)}, u32[]{:S(2)}) %collective-permute-start.20) | collective-permute-done | bytes 98336 | tf_op jit(solution)/shard_map/ppermute | solution.py:36
  (58 shorter events, 28.3 us)
Async XLA Ops:
  4.7 12.4 %collective-permute-start = (bf16[9,192,128]{2,1,0:T(8,128)(2,1)}, bf16[9,192,128]{2,1,0:T(8,128)(2,1)S(1)}, u32[]{:S(2)}, u32[]{:S(2)}) collective-permute-start(bf16[9,192,128]{2,1,0:T(8,128)(2,1)} %get-tuple-element.37), channel_id=1, source_target_pairs={{0,4},{1,5},{2,6},{3,7},{4,0},{5,1},{6,2},{7,3},{8,12},{9,13},{10,... | collective-permute-start | bytes 1327112 | tf_op jit(solution)/shard_map/ppermute | solution.py:36
  6.2 13.3 %collective-permute-start.1 = (bf16[9,192,128]{2,1,0:T(8,128)(2,1)}, bf16[9,192,128]{2,1,0:T(8,128)(2,1)S(1)}, u32[]{:S(2)}, u32[]{:S(2)}) collective-permute-start(bf16[9,192,128]{2,1,0:T(8,128)(2,1)} %get-tuple-element.38), channel_id=1, source_target_pairs={{0,2},{1,3},{2,0},{3,1},{4,6},{5,7},{6,4},{7,5},{8,10},{9,11},{10,... | collective-permute-start | bytes 1327112 | tf_op jit(solution)/shard_map/ppermute | solution.py:36
  7.7 19.9 %collective-permute-start.2 = (bf16[9,192,128]{2,1,0:T(8,128)(2,1)}, bf16[9,192,128]{2,1,0:T(8,128)(2,1)}, u32[]{:S(2)}, u32[]{:S(2)}) collective-permute-start(bf16[9,192,128]{2,1,0:T(8,128)(2,1)} %get-tuple-element.39), channel_id=1, source_target_pairs={{0,6},{1,7},{2,4},{3,5},{4,2},{5,3},{6,0},{7,1},{8,14},{9,15},{10,... | collective-permute-start | bytes 1327112 | tf_op jit(solution)/shard_map/ppermute | solution.py:36
  10.6 17.0 %copy-start.1 = (bf16[9,192,128]{2,1,0:T(8,128)(2,1)S(1)}, bf16[9,192,128]{2,1,0:T(8,128)(2,1)}, u32[]{:S(2)}) copy-start(bf16[9,192,128]{2,1,0:T(8,128)(2,1)} %get-tuple-element.36.refs_0_) | copy-start | bytes 1327108
  10.6 17.0 %copy-start.2 = (bf16[6,192,128]{2,1,0:T(8,128)(2,1)S(1)}, bf16[6,192,128]{2,1,0:T(8,128)(2,1)}, u32[]{:S(2)}) copy-start(bf16[6,192,128]{2,1,0:T(8,128)(2,1)} %get-tuple-element.40.refs_4_) | copy-start | bytes 884740
  29.5 9.0 %collective-permute-start.7 = (bf16[6,2,384,128]{3,2,1,0:T(8,128)(2,1)S(1)}, bf16[6,2,384,128]{3,2,1,0:T(8,128)(2,1)S(1)}, u32[]{:S(2)}, u32[]{:S(2)}) collective-permute-start(bf16[6,2,384,128]{3,2,1,0:T(8,128)(2,1)S(1)} %get-tuple-element.44.ka.va), channel_id=1, source_target_pairs={{0,1},{1,0},{2,3},{3,2},{4,5},{5,4},{6,7},{7,6},{8,9},{9,8},{10,11... | collective-permute-start | bytes 3538952 | tf_op jit(solution)/shard_map/ppermute | solution.py:36
  29.6 22.3 %collective-permute-start.8 = (bf16[3,2,384,128]{3,2,1,0:T(8,128)(2,1)S(1)}, bf16[3,2,384,128]{3,2,1,0:T(8,128)(2,1)S(1)}, u32[]{:S(2)}, u32[]{:S(2)}) collective-permute-start(bf16[3,2,384,128]{3,2,1,0:T(8,128)(2,1)S(1)} %get-tuple-element.43.q.rest_0_), channel_id=1, source_target_pairs={{8,0},{9,1},{10,2},{11,3},{12,4},{13,5},{14,6},{15,7},{16,8},{17,9... | collective-permute-start | bytes 1769480 | tf_op jit(solution)/shard_map/ppermute | solution.py:36
  31.8 30.0 %collective-permute-start.3 = (bf16[6,2,384,128]{3,2,1,0:T(8,128)(2,1)S(1)}, bf16[6,2,384,128]{3,2,1,0:T(8,128)(2,1)S(1)}, u32[]{:S(2)}, u32[]{:S(2)}) collective-permute-start(bf16[6,2,384,128]{3,2,1,0:T(8,128)(2,1)S(1)} %get-tuple-element.44.ka.va), channel_id=1, source_target_pairs={{0,8},{1,9},{2,10},{3,11},{4,12},{5,13},{6,14},{7,15},{8,16},{9,17... | collective-permute-start | bytes 3538952 | tf_op jit(solution)/shard_map/ppermute | solution.py:36
  35.5 9.1 %collective-permute-start.4 = (bf16[6,192,128]{2,1,0:T(8,128)(2,1)S(1)}, bf16[6,192,128]{2,1,0:T(8,128)(2,1)S(1)}, u32[]{:S(2)}, u32[]{:S(2)}) collective-permute-start(bf16[6,192,128]{2,1,0:T(8,128)(2,1)S(1)} %get-tuple-element.46), channel_id=1, source_target_pairs={{0,4},{1,5},{2,6},{3,7},{4,0},{5,1},{6,2},{7,3},{8,12},{9,13},{10,... | collective-permute-start | bytes 884744 | tf_op jit(solution)/shard_map/ppermute | solution.py:36
  37.0 9.9 %collective-permute-start.5 = (bf16[6,192,128]{2,1,0:T(8,128)(2,1)S(1)}, bf16[6,192,128]{2,1,0:T(8,128)(2,1)S(1)}, u32[]{:S(2)}, u32[]{:S(2)}) collective-permute-start(bf16[6,192,128]{2,1,0:T(8,128)(2,1)S(1)} %get-tuple-element.47), channel_id=1, source_target_pairs={{0,2},{1,3},{2,0},{3,1},{4,6},{5,7},{6,4},{7,5},{8,10},{9,11},{10,... | collective-permute-start | bytes 884744 | tf_op jit(solution)/shard_map/ppermute | solution.py:36
  38.5 13.3 %collective-permute-start.6 = (bf16[6,192,128]{2,1,0:T(8,128)(2,1)S(1)}, bf16[6,192,128]{2,1,0:T(8,128)(2,1)S(1)}, u32[]{:S(2)}, u32[]{:S(2)}) collective-permute-start(bf16[6,192,128]{2,1,0:T(8,128)(2,1)S(1)} %get-tuple-element.48), channel_id=1, source_target_pairs={{0,6},{1,7},{2,4},{3,5},{4,2},{5,3},{6,0},{7,1},{8,14},{9,15},{10,... | collective-permute-start | bytes 884744 | tf_op jit(solution)/shard_map/ppermute | solution.py:36
  53.0 2.4 %collective-permute-start.9 = (bf16[4,2,384,128]{3,2,1,0:T(8,128)(2,1)S(1)}, bf16[4,2,384,128]{3,2,1,0:T(8,128)(2,1)S(1)}, u32[]{:S(2)}, u32[]{:S(2)}) collective-permute-start(bf16[4,2,384,128]{3,2,1,0:T(8,128)(2,1)S(1)} %get-tuple-element.51.ka.va), channel_id=1, source_target_pairs={{0,1},{1,0},{2,3},{3,2},{4,5},{5,4},{6,7},{7,6},{8,9},{9,8},{10,11... | collective-permute-start | bytes 2359304 | tf_op jit(solution)/shard_map/ppermute | solution.py:36
  61.8 5.9 %collective-permute-start.10 = (bf16[6,2,384,128]{3,2,1,0:T(8,128)(2,1)S(1)}, bf16[6,2,384,128]{3,2,1,0:T(8,128)(2,1)S(1)}, u32[]{:S(2)}, u32[]{:S(2)}) collective-permute-start(bf16[6,2,384,128]{3,2,1,0:T(8,128)(2,1)S(1)} %in_order.2.ka.va), channel_id=1, source_target_pairs={{0,1},{1,0},{2,3},{3,2},{4,5},{5,4},{6,7},{7,6},{8,9},{9,8},{10,11... | collective-permute-start | bytes 3538952 | tf_op jit(solution)/shard_map/ppermute | solution.py:36
  61.8 24.5 %collective-permute-start.13 = (bf16[4,2,384,128]{3,2,1,0:T(8,128)(2,1)S(1)}, bf16[4,2,384,128]{3,2,1,0:T(8,128)(2,1)S(1)}, u32[]{:S(2)}, u32[]{:S(2)}) collective-permute-start(bf16[4,2,384,128]{3,2,1,0:T(8,128)(2,1)S(1)} %get-tuple-element.51.ka.va), channel_id=1, source_target_pairs={{0,8},{1,9},{2,10},{3,11},{4,12},{5,13},{6,14},{7,15},{8,16},{9,17... | collective-permute-start | bytes 2359304 | tf_op jit(solution)/shard_map/ppermute | solution.py:36
  65.4 13.1 %collective-permute-start.11 = (bf16[2,2,384,128]{3,2,1,0:T(8,128)(2,1)S(1)}, bf16[2,2,384,128]{3,2,1,0:T(8,128)(2,1)S(1)}, u32[]{:S(2)}, u32[]{:S(2)}) collective-permute-start(bf16[2,2,384,128]{3,2,1,0:T(8,128)(2,1)S(1)} %get-tuple-element.50.q.rest_0_), channel_id=1, source_target_pairs={{8,0},{9,1},{10,2},{11,3},{12,4},{13,5},{14,6},{15,7},{16,8},{17,9... | collective-permute-start | bytes 1179656 | tf_op jit(solution)/shard_map/ppermute | solution.py:36
  86.3 3.8 %collective-permute-start.14 = (bf16[4,2,384,128]{3,2,1,0:T(8,128)(2,1)S(1)}, bf16[4,2,384,128]{3,2,1,0:T(8,128)(2,1)S(1)}, u32[]{:S(2)}, u32[]{:S(2)}) collective-permute-start(bf16[4,2,384,128]{3,2,1,0:T(8,128)(2,1)S(1)} %in_order.3.ka.va), channel_id=1, source_target_pairs={{0,1},{1,0},{2,3},{3,2},{4,5},{5,4},{6,7},{7,6},{8,9},{9,8},{10,11... | collective-permute-start | bytes 2359304 | tf_op jit(solution)/shard_map/ppermute | solution.py:36
  86.3 18.5 %collective-permute-start.12 = (bf16[3,800,128]{2,1,0:T(8,128)(2,1)S(1)}, bf16[3,800,128]{2,1,0:T(8,128)(2,1)S(1)}, u32[]{:S(2)}, u32[]{:S(2)}) collective-permute-start(bf16[3,800,128]{2,1,0:T(8,128)(2,1)S(1)} %remote.2.rest_0_), channel_id=1, source_target_pairs={{0,8},{1,9},{2,10},{3,11},{4,12},{5,13},{6,14},{7,15},{8,16},{9,17... | collective-permute-start | bytes 1843208 | tf_op jit(solution)/shard_map/ppermute | solution.py:36
  93.9 19.4 %collective-permute-start.18 = (bf16[2,800,128]{2,1,0:T(8,128)(2,1)S(1)}, bf16[2,800,128]{2,1,0:T(8,128)(2,1)S(1)}, u32[]{:S(2)}, u32[]{:S(2)}) collective-permute-start(bf16[2,800,128]{2,1,0:T(8,128)(2,1)S(1)} %remote.3.rest_0_), channel_id=1, source_target_pairs={{0,8},{1,9},{2,10},{3,11},{4,12},{5,13},{6,14},{7,15},{8,16},{9,17... | collective-permute-start | bytes 1228808 | tf_op jit(solution)/shard_map/ppermute | solution.py:36
  106.1 11.2 %collective-permute-start.15 = (bf16[3,192,128]{2,1,0:T(8,128)(2,1)S(1)}, bf16[3,192,128]{2,1,0:T(8,128)(2,1)S(1)}, u32[]{:S(2)}, u32[]{:S(2)}) collective-permute-start(bf16[3,192,128]{2,1,0:T(8,128)(2,1)S(1)} %get-tuple-element.59), channel_id=1, source_target_pairs={{0,4},{1,5},{2,6},{3,7},{4,0},{5,1},{6,2},{7,3},{8,12},{9,13},{10,... | collective-permute-start | bytes 442376 | tf_op jit(solution)/shard_map/ppermute | solution.py:36
  107.7 10.1 %collective-permute-start.16 = (bf16[3,192,128]{2,1,0:T(8,128)(2,1)S(1)}, bf16[3,192,128]{2,1,0:T(8,128)(2,1)S(1)}, u32[]{:S(2)}, u32[]{:S(2)}) collective-permute-start(bf16[3,192,128]{2,1,0:T(8,128)(2,1)S(1)} %get-tuple-element.60), channel_id=1, source_target_pairs={{0,2},{1,3},{2,0},{3,1},{4,6},{5,7},{6,4},{7,5},{8,10},{9,11},{10,... | collective-permute-start | bytes 442376 | tf_op jit(solution)/shard_map/ppermute | solution.py:36
  109.2 8.7 %collective-permute-start.17 = (bf16[3,192,128]{2,1,0:T(8,128)(2,1)S(1)}, bf16[3,192,128]{2,1,0:T(8,128)(2,1)S(1)}, u32[]{:S(2)}, u32[]{:S(2)}) collective-permute-start(bf16[3,192,128]{2,1,0:T(8,128)(2,1)S(1)} %get-tuple-element.61), channel_id=1, source_target_pairs={{0,6},{1,7},{2,4},{3,5},{4,2},{5,3},{6,0},{7,1},{8,14},{9,15},{10,... | collective-permute-start | bytes 442376 | tf_op jit(solution)/shard_map/ppermute | solution.py:36
  114.3 4.7 %collective-permute-start.19 = (bf16[2,192,128]{2,1,0:T(8,128)(2,1)S(1)}, bf16[2,192,128]{2,1,0:T(8,128)(2,1)S(1)}, u32[]{:S(2)}, u32[]{:S(2)}) collective-permute-start(bf16[2,192,128]{2,1,0:T(8,128)(2,1)S(1)} %get-tuple-element.64), channel_id=1, source_target_pairs={{0,4},{1,5},{2,6},{3,7},{4,0},{5,1},{6,2},{7,3},{8,12},{9,13},{10,... | collective-permute-start | bytes 294920 | tf_op jit(solution)/shard_map/ppermute | solution.py:36
  115.9 5.3 %collective-permute-start.20 = (bf16[2,192,128]{2,1,0:T(8,128)(2,1)S(1)}, bf16[2,192,128]{2,1,0:T(8,128)(2,1)S(1)}, u32[]{:S(2)}, u32[]{:S(2)}) collective-permute-start(bf16[2,192,128]{2,1,0:T(8,128)(2,1)S(1)} %get-tuple-element.65), channel_id=1, source_target_pairs={{0,2},{1,3},{2,0},{3,1},{4,6},{5,7},{6,4},{7,5},{8,10},{9,11},{10,... | collective-permute-start | bytes 294920 | tf_op jit(solution)/shard_map/ppermute | solution.py:36
  117.3 5.5 %collective-permute-start.21 = (bf16[2,192,128]{2,1,0:T(8,128)(2,1)S(1)}, bf16[2,192,128]{2,1,0:T(8,128)(2,1)S(1)}, u32[]{:S(2)}, u32[]{:S(2)}) collective-permute-start(bf16[2,192,128]{2,1,0:T(8,128)(2,1)S(1)} %get-tuple-element.66), channel_id=1, source_target_pairs={{0,6},{1,7},{2,4},{3,5},{4,2},{5,3},{6,0},{7,1},{8,14},{9,15},{10,... | collective-permute-start | bytes 294920 | tf_op jit(solution)/shard_map/ppermute | solution.py:36
  (7 other events, 90.7 us)

commit v4 on v3

--- a/solution.py
+++ b/solution.py
@@ -15,14 +15,22 @@
 MIB = 1024 * 1024
 TILE = 128
 SIZES = (3, 2)
-COST = 1000
-ORDER = "s0 n0 s10 n1 r0 f01 r1 f1 c0 c1"
+APART = (0,)
+COSTS = {}
+EARLY = False
+ORDER = "s0 n0 s1+q0 r0 n1+q1 r1 f0 f1 c0 c1"
 NT = (((1,), (1,)), ((), ()))
 NN = (((1,), (0,)), ((), ()))
 
 
 def params(mib):
     return pltpu.CompilerParams(vmem_limit_bytes=mib * MIB)
+
+
+def estimate(microseconds):
+    return pl.CostEstimate(
+        flops=0, bytes_accessed=int(microseconds * 3.6e6) + 1000, transcendentals=0
+    )
 
 
 def move(block, target):
@@ -81,7 +89,7 @@
                     outs[4 * i + j][t * heads + h] = ref[:, at]
 
 
-def pack(meta, q, k, v, firsts, sizes, group_width):
+def pack(meta, q, k, v, firsts, sizes, group_width, cost=0):
     rows = q.shape[0]
     whole = pl.BlockSpec(memory_space=pltpu.VMEM)
     outs = pl.pallas_call(
@@ -94,7 +102,7 @@
         in_specs=[SMEM, whole, whole, whole],
         out_specs=[whole] * (4 * len(sizes)),
         compiler_params=params(60),
-        cost_estimate=pl.CostEstimate(flops=COST, bytes_accessed=COST, transcendentals=0),
+        cost_estimate=estimate(cost),
         name="pack",
     )(meta, q, k, v)
     return [outs[4 * i : 4 * i + 4] for i in range(len(sizes))]
@@ -121,7 +129,7 @@
         copy.wait()
 
 
-def stack(meta, pieces, later, after):
+def stack(meta, pieces, later, after, cost):
     triple, rows, _ = pieces[0].shape
     heads = triple // 3
     dtype = pieces[0].dtype
@@ -137,7 +145,7 @@
         scratch_shapes=[pltpu.SemaphoreType.DMA((4, 2))],
         input_output_aliases={5 + n: 2 + n for n in range(len(later))},
         compiler_params=params(8),
-        cost_estimate=pl.CostEstimate(flops=COST, bytes_accessed=COST, transcendentals=0),
+        cost_estimate=estimate(cost),
         name="stack",
     )(meta, *pieces, *later, *after)
     return outs[0], outs[1], outs[2:]
@@ -231,24 +239,51 @@
     pass
 
 
-def in_order(block, after):
+def in_order(blocks, after):
     return pl.pallas_call(
         in_order_kernel,
-        out_shape=jax.ShapeDtypeStruct(block.shape, block.dtype),
+        out_shape=[jax.ShapeDtypeStruct(block.shape, block.dtype) for block in blocks],
+        in_specs=[ANY] * (len(blocks) + len(after)),
+        out_specs=[ANY] * len(blocks),
+        input_output_aliases={n: n for n in range(len(blocks))},
+        compiler_params=params(1),
+        cost_estimate=pl.CostEstimate(flops=0, bytes_accessed=0, transcendentals=0),
+        name="in_order",
+    )(*blocks, *after)
+
+
+def halves_kernel(count, kv, *rest):
+    k, v, sems = rest[count:]
+    heads = k.shape[0]
+    copies = [
+        pltpu.make_async_copy(kv.at[pl.ds(n * heads, heads)], out, sems.at[n])
+        for n, out in enumerate((k, v))
+    ]
+    for copy in copies:
+        copy.start()
+    for copy in copies:
+        copy.wait()
+
+
+def halves(kv, after):
+    half = jax.ShapeDtypeStruct((kv.shape[0] // 2,) + kv.shape[1:], kv.dtype)
+    return pl.pallas_call(
+        functools.partial(halves_kernel, len(after)),
+        out_shape=[half, half],
         in_specs=[ANY] * (1 + len(after)),
-        out_specs=ANY,
-        input_output_aliases={0: 0},
+        out_specs=[ANY] * 2,
+        scratch_shapes=[pltpu.SemaphoreType.DMA((2,))],
         compiler_params=params(1),
-        cost_estimate=pl.CostEstimate(flops=COST, bytes_accessed=COST, transcendentals=0),
-        name="in_order",
-    )(block, *after)
+        cost_estimate=estimate(0),
+        name="halves",
+    )(kv, *after)
 
 
 def lse_rows(rows):
     return -(-2 * rows // TILE // 8) * 8
 
 
-def attend(body, meta, q, kv, near, after):
+def attend(body, meta, q, kv, near, after, cost):
     heads, _, rows, _ = q.shape
     block = (1, 2, rows, HEAD_DIM)
     head = pl.BlockSpec(block, lambda h: (h, 0, 0, 0))
@@ -258,8 +293,11 @@
     o_spec = pl.BlockSpec((1, 2 * rows, HEAD_DIM), by_head)
     lse_spec = pl.BlockSpec((1, extra, TILE), by_head)
     part_lse = pltpu.VMEM((extra, TILE), jnp.float32)
-    operands = [q] + [half for half in kv for _ in range(2)]
-    specs = [head] + [head, value] * 2
+    operands, specs = [q], [head]
+    for half in kv:
+        apart = isinstance(half, tuple)
+        operands += half if apart else [half, half]
+        specs += [head, head if apart else value]
     out_shape = [
         jax.ShapeDtypeStruct((heads, 2 * rows, HEAD_DIM), jnp.float32),
         jax.ShapeDtypeStruct((heads, extra, TILE), jnp.float32),
@@ -282,7 +320,7 @@
         out_specs=out_specs,
         scratch_shapes=scratch,
         compiler_params=params(20),
-        cost_estimate=pl.CostEstimate(flops=COST, bytes_accessed=COST, transcendentals=0),
+        cost_estimate=estimate(cost),
         name=body.__name__[:-7],
     )(*operands, *after)
 
@@ -304,7 +342,7 @@
         outs[j][0] = scratch[at].astype(outs[j].dtype)
 
 
-def merge(meta, o, lse, o_far, after):
+def merge(meta, o, lse, o_far, after, cost):
     heads, both, _ = o.shape
     by_head = lambda h: (h, 0, 0)
     return pl.pallas_call(
@@ -317,7 +355,7 @@
         out_specs=[pl.BlockSpec((1, both // 4, HEAD_DIM), by_head)] * 4,
         scratch_shapes=[pltpu.VMEM((both, HEAD_DIM), jnp.float32)],
         compiler_params=params(12),
-        cost_estimate=pl.CostEstimate(flops=COST, bytes_accessed=COST, transcendentals=0),
+        cost_estimate=estimate(cost),
         name="merge",
     )(meta, o, lse, o_far, *after)
 
@@ -332,7 +370,7 @@
             out[:, at] = (gate[:, at] * piece[h].astype(jnp.float32)).astype(out.dtype)
 
 
-def finish(meta, gate, pieces, firsts, group_width):
+def finish(meta, gate, pieces, firsts, group_width, cost=0):
     rows = pieces[0].shape[1]
     whole = pl.BlockSpec(memory_space=pltpu.VMEM)
     return pl.pallas_call(
@@ -341,7 +379,7 @@
         in_specs=[SMEM] + [whole] * (1 + len(pieces)),
         out_specs=whole,
         compiler_params=params(16),
-        cost_estimate=pl.CostEstimate(flops=COST, bytes_accessed=COST, transcendentals=0),
+        cost_estimate=estimate(cost),
         name="finish",
     )(meta, gate, *pieces)
 
@@ -381,11 +419,13 @@
         return [blocks[0]] + [move(blocks[j], within_level(*PLACES[j])) for j in (1, 2, 3)]
 
     exchanged = {0: exchange(sent[0])}
-
-    def spread(i, after):
+    if EARLY and len(sizes) > 1:
+        exchanged[1] = exchange([sent[1][0], *in_order(sent[1][1:], last)])
+
+    def spread(i, after, cost):
         pieces = exchanged.pop(i)
-        later = sent[i + 1] if i + 1 < len(sizes) else []
-        q[i], kv[i], later = stack(meta, pieces, later[1:], after)
+        later = sent[i + 1] if i + 1 < len(sizes) and i + 1 not in exchanged else []
+        q[i], kv[i], later = stack(meta, pieces, later[1:], after, cost)
         if later:
             exchanged[i + 1] = exchange([sent[i + 1][0], *later])
         kv_up[i] = move(kv[i], one_up)
@@ -393,31 +433,35 @@
         kv[i] = (kv[i], move(kv[i], other_core))
         return [q[i]]
 
-    def near(i, after):
-        own[i] = attend(near_kernel, meta, q[i], kv[i], None, after)
+    def near(i, after, cost):
+        own[i] = attend(near_kernel, meta, q[i], kv[i], None, after, cost)
         return [own[i][1]]
 
-    def remote(i, after):
-        held = in_order(kv_up[i], after)
-        kv_up[i] = (held, move(held, other_core))
-        part = attend(remote_kernel, meta, q_down[i], kv_up[i], None, [])
+    def remote(i, after, cost):
+        if i in APART:
+            held = tuple(halves(kv_up[i], after))
+            kv_up[i] = (held, tuple(move(half, other_core) for half in held))
+        else:
+            held = in_order([kv_up[i]], after)[0]
+            kv_up[i] = (held, move(held, other_core))
+        part = attend(remote_kernel, meta, q_down[i], kv_up[i], None, [], cost)
         far[i] = move(part, one_up)
         return [part]
 
-    def own_far(i, after):
-        own[i] = attend(far_kernel, meta, q[i], kv_up[i], own[i], after)
+    def own_far(i, after, cost):
+        own[i] = attend(far_kernel, meta, q[i], kv_up[i], own[i], after, cost)
         return [own[i][1]]
 
-    def close(i, after):
-        merged = merge(meta, *own[i], far[i], after)
+    def close(i, after, cost):
+        merged = merge(meta, *own[i], far[i], after, cost)
         results[i] = exchange(merged)
         return [merged[0]]
 
     steps = {"s": spread, "n": near, "r": remote, "f": own_far, "c": close}
     for step in ORDER.split():
-        kind, i = step[0], int(step[1])
-        extra = [q_down[int(j)] for j in step[2:]]
-        last = steps[kind](i, last + extra)
+        name, *extra = step.split("+")
+        extra = [{"q": q_down, "o": far}[e[0]][int(e[1])] for e in extra]
+        last = steps[name[0]](int(name[1]), last + extra, COSTS.get(name, 0))
     return finish(meta, gate, sum((results[i] for i in chunks), []), firsts, group_width)
 
 

time: 125 us -> 118 us (0.944)
  waiting for transfers between devices: 45.8 us -> 38.1 us
    ppermute x22 -> x23, waiting for transfers between devices: 45.8 us -> 38.1 us  [move(): return lax.ppermute(block, AXES, route)]
    ppermute x22 -> x23, starting transfers between devices: 31.9 us -> 32.6 us  [move(): return lax.ppermute(block, AXES, route)]
  transfers between devices with their start and end apart: 22 -> 23, of which waited for: 14 -> 13; matrix products, arithmetic and copies ran while one was open for 3% -> 3% of each run, Pallas kernels for 28% -> 30%
where the time goes in v4:
time: 118 us
  Pallas kernels  42.5 us (36%)
  waiting for transfers between devices  38.1 us (32%)
  starting transfers between devices  32.6 us (28%)
  other arithmetic  1.97 us (2%)
  matrix products  1.34 us (1%)
    ppermute x23, waiting for transfers between devices, move(): return lax.ppermute(block, AXES, route)  38.1 us
    ppermute x23, starting transfers between devices, move(): return lax.ppermute(block, AXES, route)  32.6 us
    pallas_call x6, Pallas kernels, attend(): pl.pallas_call(functools.partial(body, len(after)), grid=(heads,), out_sh...  31.2 us
    pallas_call x1, Pallas kernels, pack(): pl.pallas_call(functools.partial(pack_kernel, firsts, sizes, group_width)...  4.13 us
    pallas_call x2, Pallas kernels, stack(): pl.pallas_call(functools.partial(stack_kernel, heads, len(later) + len(af...  3.03 us
  transfers between devices with their start and end apart: 23, of which 13 were waited for; matrix products, arithmetic and copies ran while one was open for 3% of the time, Pallas kernels for 30%

profile of v4, /device:TPU:8, one launch (start us, length us, event | category | flops | bytes accessed | tf_op | source)
XLA Modules:
  0.0 118.0 jit_solution(15398422432605082110)
XLA Ops:
  0.6 4.1 %pack.1 = (bf16[9,192,128]{2,1,0:T(8,128)(2,1)}, bf16[9,192,128]{2,1,0:T(8,128)(2,1)}, bf16[9,192,128]{2,1,0:T(8,128)(2,1)}, bf16[9,192,128]{2,1,0:T(8,128)(2,1)...) custom-call(s32[9]{0:T(128)} %stack.35.meta, ...), custom_call_target="tpu_custom_call" | custom-call | bytes 1000 | tf_op jit(solution)/shard_map/pack/pallas_call | solution.py:95
  12.2 4.9 %collective-permute-done.refs_1_ = bf16[9,192,128]{2,1,0:T(8,128)(2,1)S(1)} collective-permute-done((bf16[9,192,128]{2,1,0:T(8,128)(2,1)}, bf16[9,192,128]{2,1,0:T(8,128)(2,1)S(1)}, u32[]{:S(2)}, u32[]{:S(2)}) %collective-permute-start) | collective-permute-done | bytes 442400 | tf_op jit(solution)/shard_map/ppermute | solution.py:44
  17.1 2.4 %collective-permute-done.1.refs_2_ = bf16[9,192,128]{2,1,0:T(8,128)(2,1)S(1)} collective-permute-done((bf16[9,192,128]{2,1,0:T(8,128)(2,1)}, bf16[9,192,128]{2,1,0:T(8,128)(2,1)S(1)}, u32[]{:S(2)}, u32[]{:S(2)}) %collective-permute-start.1) | collective-permute-done | bytes 442400 | tf_op jit(solution)/shard_map/ppermute | solution.py:44
  19.5 8.1 %collective-permute-done.2.refs_3_ = bf16[9,192,128]{2,1,0:T(8,128)(2,1)} collective-permute-done((bf16[9,192,128]{2,1,0:T(8,128)(2,1)}, bf16[9,192,128]{2,1,0:T(8,128)(2,1)}, u32[]{:S(2)}, u32[]{:S(2)}) %collective-permute-start.2) | collective-permute-done | bytes 442400 | tf_op jit(solution)/shard_map/ppermute | solution.py:44
  27.6 1.9 %stack.36 = (bf16[3,2,384,128]{3,2,1,0:T(8,128)(2,1)S(1)}, bf16[6,2,384,128]{3,2,1,0:T(8,128)(2,1)S(1)}, bf16[6,192,128]{2,1,0:T(8,128)(2,1)S(1)}, bf16[6,192,12...) custom-call(s32[9]{0:T(128)S(1)} %copy-done.6, ...), custom_call_target="tpu_custom_call", output_to_operand_aliasing={{2}: (5, {}), {3}: (6, {}), {4}: (7, {})} | custom-call | bytes 1000 | tf_op jit(solution)/shard_map/stack/pallas_call | solution.py:136
  29.6 3.5 %collective-permute-start.3 = (bf16[6,2,384,128]{3,2,1,0:T(8,128)(2,1)S(1)}, bf16[6,2,384,128]{3,2,1,0:T(8,128)(2,1)S(1)}, u32[]{:S(2)}, u32[]{:S(2)}) collective-permute-start(bf16[6,2,384,128]{3,2,1,0:T(8,128)(2,1)S(1)} %get-tuple-element.46.ka.va), channel_id=1, source_target_pairs={{0,8},{1,9},{2,10},{3,11},{4,12},{5,13},{6,14},{7,15},{8,16},{9,17... | collective-permute-start | bytes 3538952 | tf_op jit(solution)/shard_map/ppermute | solution.py:44
  33.1 2.4 %collective-permute-start.8 = (bf16[3,2,384,128]{3,2,1,0:T(8,128)(2,1)S(1)}, bf16[3,2,384,128]{3,2,1,0:T(8,128)(2,1)S(1)}, u32[]{:S(2)}, u32[]{:S(2)}) collective-permute-start(bf16[3,2,384,128]{3,2,1,0:T(8,128)(2,1)S(1)} %get-tuple-element.45.q.rest_0_), channel_id=1, source_target_pairs={{8,0},{9,1},{10,2},{11,3},{12,4},{13,5},{14,6},{15,7},{16,8},{17,9... | collective-permute-start | bytes 1769480 | tf_op jit(solution)/shard_map/ppermute | solution.py:44
  39.1 5.2 %near.2 = (f32[3,768,128]{2,1,0:T(8,128)S(1)}, f32[3,8,128]{2,1,0:T(8,128)S(1)}) custom-call(bf16[3,2,384,128]{3,2,1,0:T(8,128)(2,1)S(1)} %get-tuple-element.45.q.rest_0_, bf16[6,2,384,128]{3,2,1,0:T(8,128)(2,1)S(1)} %get-tuple-element.46.ka.va, bf16[6,2,384,128]{3,2,1,0:T(8,128)(2,1)S(1)} %get-tuple-element.46.ka.va, ...), custom_call_target="tpu_custom_call" | custom-call | bytes 1000 | tf_op jit(solution)/shard_map/near/pallas_call | solution.py:315
  44.6 2.4 %collective-permute-done.5.refs_2_ = bf16[6,192,128]{2,1,0:T(8,128)(2,1)S(1)} collective-permute-done((bf16[6,192,128]{2,1,0:T(8,128)(2,1)S(1)}, bf16[6,192,128]{2,1,0:T(8,128)(2,1)S(1)}, u32[]{:S(2)}, u32[]{:S(2)}) %collective-permute-start.5) | collective-permute-done | bytes 294944 | tf_op jit(solution)/shard_map/ppermute | solution.py:44
  47.0 4.9 %collective-permute-done.6.refs_3_ = bf16[6,192,128]{2,1,0:T(8,128)(2,1)S(1)} collective-permute-done((bf16[6,192,128]{2,1,0:T(8,128)(2,1)S(1)}, bf16[6,192,128]{2,1,0:T(8,128)(2,1)S(1)}, u32[]{:S(2)}, u32[]{:S(2)}) %collective-permute-start.6) | collective-permute-done | bytes 294944 | tf_op jit(solution)/shard_map/ppermute | solution.py:44
  53.2 3.4 %collective-permute-start.12 = (bf16[4,2,384,128]{3,2,1,0:T(8,128)(2,1)S(1)}, bf16[4,2,384,128]{3,2,1,0:T(8,128)(2,1)S(1)}, u32[]{:S(2)}, u32[]{:S(2)}) collective-permute-start(bf16[4,2,384,128]{3,2,1,0:T(8,128)(2,1)S(1)} %get-tuple-element.56.ka.va), channel_id=1, source_target_pairs={{0,8},{1,9},{2,10},{3,11},{4,12},{5,13},{6,14},{7,15},{8,16},{9,17... | collective-permute-start | bytes 2359304 | tf_op jit(solution)/shard_map/ppermute | solution.py:44
  56.6 3.7 %collective-permute-done.3.kv = bf16[6,2,384,128]{3,2,1,0:T(8,128)(2,1)S(1)} collective-permute-done((bf16[6,2,384,128]{3,2,1,0:T(8,128)(2,1)S(1)}, bf16[6,2,384,128]{3,2,1,0:T(8,128)(2,1)S(1)}, u32[]{:S(2)}, u32[]{:S(2)}) %collective-permute-start.3) | collective-permute-done | bytes 1179680 | tf_op jit(solution)/shard_map/ppermute | solution.py:44
  61.1 1.9 %collective-permute-start.11 = (bf16[2,2,384,128]{3,2,1,0:T(8,128)(2,1)S(1)}, bf16[2,2,384,128]{3,2,1,0:T(8,128)(2,1)S(1)}, u32[]{:S(2)}, u32[]{:S(2)}) collective-permute-start(bf16[2,2,384,128]{3,2,1,0:T(8,128)(2,1)S(1)} %get-tuple-element.52.rest_0_.q), channel_id=1, source_target_pairs={{8,0},{9,1},{10,2},{11,3},{12,4},{13,5},{14,6},{15,7},{16,8},{17,9... | collective-permute-start | bytes 1179656 | tf_op jit(solution)/shard_map/ppermute | solution.py:44
  63.4 5.7 %remote.2.rest_0_ = bf16[3,800,128]{2,1,0:T(8,128)(2,1)S(1)} custom-call(bf16[3,2,384,128]{3,2,1,0:T(8,128)(2,1)S(1)} %collective-permute-done.8.refs_5_.q, bf16[3,2,384,128]{3,2,1,0:T(8,128)(2,1)S(1)} %get-tuple-element.53.ka, bf16[3,2,384,128]{3,2,1,0:T(8,128)(2,1)S(1)} %get-tuple-element.54.va, bf16[3,2,384,128]{3,2,1,0:T(8,128)(2,1)S(1)} %collective-permute-done.9.kb, ...), custom_call_target="tpu_custom_call" | custom-call | bytes 1000 | tf_op jit(solution)/shard_map/remote/pallas_call | solution.py:315
  69.1 5.0 %collective-permute-done.11.rest_1_.q = bf16[2,2,384,128]{3,2,1,0:T(8,128)(2,1)S(1)} collective-permute-done((bf16[2,2,384,128]{3,2,1,0:T(8,128)(2,1)S(1)}, bf16[2,2,384,128]{3,2,1,0:T(8,128)(2,1)S(1)}, u32[]{:S(2)}, u32[]{:S(2)}) %collective-permute-start.11) | collective-permute-done | bytes 393248 | tf_op jit(solution)/shard_map/ppermute | solution.py:44
  74.1 3.5 %near.3 = (f32[2,768,128]{2,1,0:T(8,128)S(1)}, f32[2,8,128]{2,1,0:T(8,128)S(1)}) custom-call(bf16[2,2,384,128]{3,2,1,0:T(8,128)(2,1)S(1)} %get-tuple-element.52.rest_0_.q, bf16[4,2,384,128]{3,2,1,0:T(8,128)(2,1)S(1)} %get-tuple-element.56.ka.va, bf16[4,2,384,128]{3,2,1,0:T(8,128)(2,1)S(1)} %get-tuple-element.56.ka.va, ...), custom_call_target="tpu_custom_call" | custom-call | bytes 1000 | tf_op jit(solution)/shard_map/near/pallas_call | solution.py:315
  77.7 3.5 %collective-permute-start.15 = (bf16[3,800,128]{2,1,0:T(8,128)(2,1)S(1)}, bf16[3,800,128]{2,1,0:T(8,128)(2,1)S(1)}, u32[]{:S(2)}, u32[]{:S(2)}) collective-permute-start(bf16[3,800,128]{2,1,0:T(8,128)(2,1)S(1)} %remote.2.rest_0_), channel_id=1, source_target_pairs={{0,8},{1,9},{2,10},{3,11},{4,12},{5,13},{6,14},{7,15},{8,16},{9,17... | collective-permute-start | bytes 1843208 | tf_op jit(solution)/shard_map/ppermute | solution.py:44
  81.2 3.8 %remote.3.rest_0_ = bf16[2,800,128]{2,1,0:T(8,128)(2,1)S(1)} custom-call(bf16[2,2,384,128]{3,2,1,0:T(8,128)(2,1)S(1)} %collective-permute-done.11.rest_1_.q, bf16[4,2,384,128]{3,2,1,0:T(8,128)(2,1)S(1)} %in_order.1.ka.va, bf16[4,2,384,128]{3,2,1,0:T(8,128)(2,1)S(1)} %in_order.1.ka.va, bf16[4,2,384,128]{3,2,1,0:T(8,128)(2,1)S(1)} %collective-permute-done.14.kb.vb, ...), custom_call_target="tpu_custom_call" | custom-call | bytes 1000 | tf_op jit(solution)/shard_map/remote/pallas_call | solution.py:315
  85.0 2.7 %collective-permute-start.19 = (bf16[2,800,128]{2,1,0:T(8,128)(2,1)S(1)}, bf16[2,800,128]{2,1,0:T(8,128)(2,1)S(1)}, u32[]{:S(2)}, u32[]{:S(2)}) collective-permute-start(bf16[2,800,128]{2,1,0:T(8,128)(2,1)S(1)} %remote.3.rest_0_), channel_id=1, source_target_pairs={{0,8},{1,9},{2,10},{3,11},{4,12},{5,13},{6,14},{7,15},{8,16},{9,17... | collective-permute-start | bytes 1228808 | tf_op jit(solution)/shard_map/ppermute | solution.py:44
  87.7 7.7 %far.2 = (f32[3,768,128]{2,1,0:T(8,128)S(1)}, f32[3,8,128]{2,1,0:T(8,128)S(1)}) custom-call(s32[9]{0:T(128)S(1)} %copy-done.6, bf16[3,2,384,128]{3,2,1,0:T(8,128)(2,1)S(1)} %get-tuple-element.45.q.rest_0_, bf16[3,2,384,128]{3,2,1,0:T(8,128)(2,1)S(1)} %get-tuple-element.53.ka, bf16[3,2,384,128]{3,2,1,0:T(8,128)(2,1)S(1)} %get-tuple-element.54.va, ...), custom_call_target="tpu_custom_call" | custom-call | bytes 1000 | tf_op jit(solution)/shard_map/far/pallas_call | solution.py:315
  95.4 5.3 %far.3 = (f32[2,768,128]{2,1,0:T(8,128)S(1)}, f32[2,8,128]{2,1,0:T(8,128)S(1)}) custom-call(s32[9]{0:T(128)S(1)} %copy-done.6, bf16[2,2,384,128]{3,2,1,0:T(8,128)(2,1)S(1)} %get-tuple-element.52.rest_0_.q, bf16[4,2,384,128]{3,2,1,0:T(8,128)(2,1)S(1)} %in_order.1.ka.va, bf16[4,2,384,128]{3,2,1,0:T(8,128)(2,1)S(1)} %in_order.1.ka.va, ...), custom_call_target="tpu_custom_call" | custom-call | bytes 1000 | tf_op jit(solution)/shard_map/far/pallas_call | solution.py:315
  110.3 2.8 %collective-permute-done.18.refs_3_ = bf16[3,192,128]{2,1,0:T(8,128)(2,1)S(1)} collective-permute-done((bf16[3,192,128]{2,1,0:T(8,128)(2,1)S(1)}, bf16[3,192,128]{2,1,0:T(8,128)(2,1)S(1)}, u32[]{:S(2)}, u32[]{:S(2)}) %collective-permute-start.18) | collective-permute-done | bytes 147488 | tf_op jit(solution)/shard_map/ppermute | solution.py:44
  113.5 1.8 %collective-permute-done.21.refs_6_ = bf16[2,192,128]{2,1,0:T(8,128)(2,1)S(1)} collective-permute-done((bf16[2,192,128]{2,1,0:T(8,128)(2,1)S(1)}, bf16[2,192,128]{2,1,0:T(8,128)(2,1)S(1)}, u32[]{:S(2)}, u32[]{:S(2)}) %collective-permute-start.21) | collective-permute-done | bytes 98336 | tf_op jit(solution)/shard_map/ppermute | solution.py:44
  116.3 1.7 %finish.1 = bf16[192,2560]{1,0:T(8,128)(2,1)} custom-call(s32[9]{0:T(128)S(1)} %copy-done.6, f32[1,2560]{1,0:T(1,128)S(1)} %fusion.4.refs_7_.gate, bf16[3,192,128]{2,1,0:T(8,128)(2,1)S(1)} %get-tuple-element.62.rest_0_.refs_0_, bf16[3,192,128]{2,1,0:T(8,128)(2,1)S(1)} %collective-permute-done.16.refs_1_, ...), custom_call_target="tpu_custom_call" | custom-call | bytes 1000 | tf_op jit(solution)/shard_map/finish/pallas_call | solution.py:376
  (60 shorter events, 24.9 us)
Async XLA Ops:
  4.7 12.4 %collective-permute-start = (bf16[9,192,128]{2,1,0:T(8,128)(2,1)}, bf16[9,192,128]{2,1,0:T(8,128)(2,1)S(1)}, u32[]{:S(2)}, u32[]{:S(2)}) collective-permute-start(bf16[9,192,128]{2,1,0:T(8,128)(2,1)} %get-tuple-element.39), channel_id=1, source_target_pairs={{0,4},{1,5},{2,6},{3,7},{4,0},{5,1},{6,2},{7,3},{8,12},{9,13},{10,... | collective-permute-start | bytes 1327112 | tf_op jit(solution)/shard_map/ppermute | solution.py:44
  6.2 13.3 %collective-permute-start.1 = (bf16[9,192,128]{2,1,0:T(8,128)(2,1)}, bf16[9,192,128]{2,1,0:T(8,128)(2,1)S(1)}, u32[]{:S(2)}, u32[]{:S(2)}) collective-permute-start(bf16[9,192,128]{2,1,0:T(8,128)(2,1)} %get-tuple-element.40), channel_id=1, source_target_pairs={{0,2},{1,3},{2,0},{3,1},{4,6},{5,7},{6,4},{7,5},{8,10},{9,11},{10,... | collective-permute-start | bytes 1327112 | tf_op jit(solution)/shard_map/ppermute | solution.py:44
  7.7 19.9 %collective-permute-start.2 = (bf16[9,192,128]{2,1,0:T(8,128)(2,1)}, bf16[9,192,128]{2,1,0:T(8,128)(2,1)}, u32[]{:S(2)}, u32[]{:S(2)}) collective-permute-start(bf16[9,192,128]{2,1,0:T(8,128)(2,1)} %get-tuple-element.41), channel_id=1, source_target_pairs={{0,6},{1,7},{2,4},{3,5},{4,2},{5,3},{6,0},{7,1},{8,14},{9,15},{10,... | collective-permute-start | bytes 1327112 | tf_op jit(solution)/shard_map/ppermute | solution.py:44
  10.8 16.8 %copy-start.1 = (bf16[9,192,128]{2,1,0:T(8,128)(2,1)S(1)}, bf16[9,192,128]{2,1,0:T(8,128)(2,1)}, u32[]{:S(2)}) copy-start(bf16[9,192,128]{2,1,0:T(8,128)(2,1)} %get-tuple-element.38.refs_0_) | copy-start | bytes 1327108
  29.5 9.1 %collective-permute-start.7 = (bf16[6,2,384,128]{3,2,1,0:T(8,128)(2,1)S(1)}, bf16[6,2,384,128]{3,2,1,0:T(8,128)(2,1)S(1)}, u32[]{:S(2)}, u32[]{:S(2)}) collective-permute-start(bf16[6,2,384,128]{3,2,1,0:T(8,128)(2,1)S(1)} %get-tuple-element.46.ka.va), channel_id=1, source_target_pairs={{0,1},{1,0},{2,3},{3,2},{4,5},{5,4},{6,7},{7,6},{8,9},{9,8},{10,11... | collective-permute-start | bytes 3538952 | tf_op jit(solution)/shard_map/ppermute | solution.py:44
  29.6 30.7 %collective-permute-start.3 = (bf16[6,2,384,128]{3,2,1,0:T(8,128)(2,1)S(1)}, bf16[6,2,384,128]{3,2,1,0:T(8,128)(2,1)S(1)}, u32[]{:S(2)}, u32[]{:S(2)}) collective-permute-start(bf16[6,2,384,128]{3,2,1,0:T(8,128)(2,1)S(1)} %get-tuple-element.46.ka.va), channel_id=1, source_target_pairs={{0,8},{1,9},{2,10},{3,11},{4,12},{5,13},{6,14},{7,15},{8,16},{9,17... | collective-permute-start | bytes 3538952 | tf_op jit(solution)/shard_map/ppermute | solution.py:44
  33.1 18.8 %collective-permute-start.8 = (bf16[3,2,384,128]{3,2,1,0:T(8,128)(2,1)S(1)}, bf16[3,2,384,128]{3,2,1,0:T(8,128)(2,1)S(1)}, u32[]{:S(2)}, u32[]{:S(2)}) collective-permute-start(bf16[3,2,384,128]{3,2,1,0:T(8,128)(2,1)S(1)} %get-tuple-element.45.q.rest_0_), channel_id=1, source_target_pairs={{8,0},{9,1},{10,2},{11,3},{12,4},{13,5},{14,6},{15,7},{16,8},{17,9... | collective-permute-start | bytes 1769480 | tf_op jit(solution)/shard_map/ppermute | solution.py:44
  35.5 9.1 %collective-permute-start.4 = (bf16[6,192,128]{2,1,0:T(8,128)(2,1)S(1)}, bf16[6,192,128]{2,1,0:T(8,128)(2,1)S(1)}, u32[]{:S(2)}, u32[]{:S(2)}) collective-permute-start(bf16[6,192,128]{2,1,0:T(8,128)(2,1)S(1)} %get-tuple-element.48), channel_id=1, source_target_pairs={{0,4},{1,5},{2,6},{3,7},{4,0},{5,1},{6,2},{7,3},{8,12},{9,13},{10,... | collective-permute-start | bytes 884744 | tf_op jit(solution)/shard_map/ppermute | solution.py:44
  37.1 9.9 %collective-permute-start.5 = (bf16[6,192,128]{2,1,0:T(8,128)(2,1)S(1)}, bf16[6,192,128]{2,1,0:T(8,128)(2,1)S(1)}, u32[]{:S(2)}, u32[]{:S(2)}) collective-permute-start(bf16[6,192,128]{2,1,0:T(8,128)(2,1)S(1)} %get-tuple-element.49), channel_id=1, source_target_pairs={{0,2},{1,3},{2,0},{3,1},{4,6},{5,7},{6,4},{7,5},{8,10},{9,11},{10,... | collective-permute-start | bytes 884744 | tf_op jit(solution)/shard_map/ppermute | solution.py:44
  38.6 13.3 %collective-permute-start.6 = (bf16[6,192,128]{2,1,0:T(8,128)(2,1)S(1)}, bf16[6,192,128]{2,1,0:T(8,128)(2,1)S(1)}, u32[]{:S(2)}, u32[]{:S(2)}) collective-permute-start(bf16[6,192,128]{2,1,0:T(8,128)(2,1)S(1)} %get-tuple-element.50), channel_id=1, source_target_pairs={{0,6},{1,7},{2,4},{3,5},{4,2},{5,3},{6,0},{7,1},{8,14},{9,15},{10,... | collective-permute-start | bytes 884744 | tf_op jit(solution)/shard_map/ppermute | solution.py:44
  53.1 21.0 %collective-permute-start.13 = (bf16[4,2,384,128]{3,2,1,0:T(8,128)(2,1)S(1)}, bf16[4,2,384,128]{3,2,1,0:T(8,128)(2,1)S(1)}, u32[]{:S(2)}, u32[]{:S(2)}) collective-permute-start(bf16[4,2,384,128]{3,2,1,0:T(8,128)(2,1)S(1)} %get-tuple-element.56.ka.va), channel_id=1, source_target_pairs={{0,1},{1,0},{2,3},{3,2},{4,5},{5,4},{6,7},{7,6},{8,9},{9,8},{10,11... | collective-permute-start | bytes 2359304 | tf_op jit(solution)/shard_map/ppermute | solution.py:44
  53.2 24.4 %collective-permute-start.12 = (bf16[4,2,384,128]{3,2,1,0:T(8,128)(2,1)S(1)}, bf16[4,2,384,128]{3,2,1,0:T(8,128)(2,1)S(1)}, u32[]{:S(2)}, u32[]{:S(2)}) collective-permute-start(bf16[4,2,384,128]{3,2,1,0:T(8,128)(2,1)S(1)} %get-tuple-element.56.ka.va), channel_id=1, source_target_pairs={{0,8},{1,9},{2,10},{3,11},{4,12},{5,13},{6,14},{7,15},{8,16},{9,17... | collective-permute-start | bytes 2359304 | tf_op jit(solution)/shard_map/ppermute | solution.py:44
  60.5 2.5 %collective-permute-start.9 = (bf16[3,2,384,128]{3,2,1,0:T(8,128)(2,1)S(1)}, bf16[3,2,384,128]{3,2,1,0:T(8,128)(2,1)S(1)}, u32[]{:S(2)}, u32[]{:S(2)}) collective-permute-start(bf16[3,2,384,128]{3,2,1,0:T(8,128)(2,1)S(1)} %get-tuple-element.53.ka), channel_id=1, source_target_pairs={{0,1},{1,0},{2,3},{3,2},{4,5},{5,4},{6,7},{7,6},{8,9},{9,8},{10,11... | collective-permute-start | bytes 1769480 | tf_op jit(solution)/shard_map/ppermute | solution.py:44
  60.6 2.8 %collective-permute-start.10 = (bf16[3,2,384,128]{3,2,1,0:T(8,128)(2,1)S(1)}, bf16[3,2,384,128]{3,2,1,0:T(8,128)(2,1)S(1)}, u32[]{:S(2)}, u32[]{:S(2)}) collective-permute-start(bf16[3,2,384,128]{3,2,1,0:T(8,128)(2,1)S(1)} %get-tuple-element.54.va), channel_id=1, source_target_pairs={{0,1},{1,0},{2,3},{3,2},{4,5},{5,4},{6,7},{7,6},{8,9},{9,8},{10,11... | collective-permute-start | bytes 1769480 | tf_op jit(solution)/shard_map/ppermute | solution.py:44
  61.1 13.0 %collective-permute-start.11 = (bf16[2,2,384,128]{3,2,1,0:T(8,128)(2,1)S(1)}, bf16[2,2,384,128]{3,2,1,0:T(8,128)(2,1)S(1)}, u32[]{:S(2)}, u32[]{:S(2)}) collective-permute-start(bf16[2,2,384,128]{3,2,1,0:T(8,128)(2,1)S(1)} %get-tuple-element.52.rest_0_.q), channel_id=1, source_target_pairs={{8,0},{9,1},{10,2},{11,3},{12,4},{13,5},{14,6},{15,7},{16,8},{17,9... | collective-permute-start | bytes 1179656 | tf_op jit(solution)/shard_map/ppermute | solution.py:44
  77.6 3.6 %collective-permute-start.14 = (bf16[4,2,384,128]{3,2,1,0:T(8,128)(2,1)S(1)}, bf16[4,2,384,128]{3,2,1,0:T(8,128)(2,1)S(1)}, u32[]{:S(2)}, u32[]{:S(2)}) collective-permute-start(bf16[4,2,384,128]{3,2,1,0:T(8,128)(2,1)S(1)} %in_order.1.ka.va), channel_id=1, source_target_pairs={{0,1},{1,0},{2,3},{3,2},{4,5},{5,4},{6,7},{7,6},{8,9},{9,8},{10,11... | collective-permute-start | bytes 2359304 | tf_op jit(solution)/shard_map/ppermute | solution.py:44
  77.7 23.0 %collective-permute-start.15 = (bf16[3,800,128]{2,1,0:T(8,128)(2,1)S(1)}, bf16[3,800,128]{2,1,0:T(8,128)(2,1)S(1)}, u32[]{:S(2)}, u32[]{:S(2)}) collective-permute-start(bf16[3,800,128]{2,1,0:T(8,128)(2,1)S(1)} %remote.2.rest_0_), channel_id=1, source_target_pairs={{0,8},{1,9},{2,10},{3,11},{4,12},{5,13},{6,14},{7,15},{8,16},{9,17... | collective-permute-start | bytes 1843208 | tf_op jit(solution)/shard_map/ppermute | solution.py:44
  85.0 20.5 %collective-permute-start.19 = (bf16[2,800,128]{2,1,0:T(8,128)(2,1)S(1)}, bf16[2,800,128]{2,1,0:T(8,128)(2,1)S(1)}, u32[]{:S(2)}, u32[]{:S(2)}) collective-permute-start(bf16[2,800,128]{2,1,0:T(8,128)(2,1)S(1)} %remote.3.rest_0_), channel_id=1, source_target_pairs={{0,8},{1,9},{2,10},{3,11},{4,12},{5,13},{6,14},{7,15},{8,16},{9,17... | collective-permute-start | bytes 1228808 | tf_op jit(solution)/shard_map/ppermute | solution.py:44
  102.0 7.6 %collective-permute-start.16 = (bf16[3,192,128]{2,1,0:T(8,128)(2,1)S(1)}, bf16[3,192,128]{2,1,0:T(8,128)(2,1)S(1)}, u32[]{:S(2)}, u32[]{:S(2)}) collective-permute-start(bf16[3,192,128]{2,1,0:T(8,128)(2,1)S(1)} %get-tuple-element.63), channel_id=1, source_target_pairs={{0,4},{1,5},{2,6},{3,7},{4,0},{5,1},{6,2},{7,3},{8,12},{9,13},{10,... | collective-permute-start | bytes 442376 | tf_op jit(solution)/shard_map/ppermute | solution.py:44
  103.5 6.8 %collective-permute-start.17 = (bf16[3,192,128]{2,1,0:T(8,128)(2,1)S(1)}, bf16[3,192,128]{2,1,0:T(8,128)(2,1)S(1)}, u32[]{:S(2)}, u32[]{:S(2)}) collective-permute-start(bf16[3,192,128]{2,1,0:T(8,128)(2,1)S(1)} %get-tuple-element.64), channel_id=1, source_target_pairs={{0,2},{1,3},{2,0},{3,1},{4,6},{5,7},{6,4},{7,5},{8,10},{9,11},{10,... | collective-permute-start | bytes 442376 | tf_op jit(solution)/shard_map/ppermute | solution.py:44
  105.0 8.1 %collective-permute-start.18 = (bf16[3,192,128]{2,1,0:T(8,128)(2,1)S(1)}, bf16[3,192,128]{2,1,0:T(8,128)(2,1)S(1)}, u32[]{:S(2)}, u32[]{:S(2)}) collective-permute-start(bf16[3,192,128]{2,1,0:T(8,128)(2,1)S(1)} %get-tuple-element.65), channel_id=1, source_target_pairs={{0,6},{1,7},{2,4},{3,5},{4,2},{5,3},{6,0},{7,1},{8,14},{9,15},{10,... | collective-permute-start | bytes 442376 | tf_op jit(solution)/shard_map/ppermute | solution.py:44
  106.5 7.0 %collective-permute-start.20 = (bf16[2,192,128]{2,1,0:T(8,128)(2,1)S(1)}, bf16[2,192,128]{2,1,0:T(8,128)(2,1)S(1)}, u32[]{:S(2)}, u32[]{:S(2)}) collective-permute-start(bf16[2,192,128]{2,1,0:T(8,128)(2,1)S(1)} %get-tuple-element.68), channel_id=1, source_target_pairs={{0,4},{1,5},{2,6},{3,7},{4,0},{5,1},{6,2},{7,3},{8,12},{9,13},{10,... | collective-permute-start | bytes 294920 | tf_op jit(solution)/shard_map/ppermute | solution.py:44
  108.1 7.2 %collective-permute-start.21 = (bf16[2,192,128]{2,1,0:T(8,128)(2,1)S(1)}, bf16[2,192,128]{2,1,0:T(8,128)(2,1)S(1)}, u32[]{:S(2)}, u32[]{:S(2)}) collective-permute-start(bf16[2,192,128]{2,1,0:T(8,128)(2,1)S(1)} %get-tuple-element.69), channel_id=1, source_target_pairs={{0,2},{1,3},{2,0},{3,1},{4,6},{5,7},{6,4},{7,5},{8,10},{9,11},{10,... | collective-permute-start | bytes 294920 | tf_op jit(solution)/shard_map/ppermute | solution.py:44
  109.6 6.7 %collective-permute-start.22 = (bf16[2,192,128]{2,1,0:T(8,128)(2,1)S(1)}, bf16[2,192,128]{2,1,0:T(8,128)(2,1)S(1)}, u32[]{:S(2)}, u32[]{:S(2)}) collective-permute-start(bf16[2,192,128]{2,1,0:T(8,128)(2,1)S(1)} %get-tuple-element.70), channel_id=1, source_target_pairs={{0,6},{1,7},{2,4},{3,5},{4,2},{5,3},{6,0},{7,1},{8,14},{9,15},{10,... | collective-permute-start | bytes 294920 | tf_op jit(solution)/shard_map/ppermute | solution.py:44
  (8 other events, 107.1 us)

commit v5 on v4

--- a/solution.py
+++ b/solution.py
@@ -79,33 +79,28 @@
     )
 
 
-def pack_kernel(firsts, sizes, group_width, meta, q, k, v, *outs):
-    for i, (first, heads) in enumerate(zip(firsts, sizes)):
-        for j in range(4):
-            for t, ref in enumerate((q, k, v)):
-                for h in range(heads):
-                    column = meta[j] * group_width + (first + h) * HEAD_DIM
-                    at = pl.ds(pl.multiple_of(column, HEAD_DIM), HEAD_DIM)
-                    outs[4 * i + j][t * heads + h] = ref[:, at]
-
-
-def pack(meta, q, k, v, firsts, sizes, group_width, cost=0):
+def pack_kernel(first, heads, group_width, count, meta, q, k, v, *rest):
+    outs = rest[count:]
+    for j in range(4):
+        for t, ref in enumerate((q, k, v)):
+            for h in range(heads):
+                column = meta[j] * group_width + (first + h) * HEAD_DIM
+                at = pl.ds(pl.multiple_of(column, HEAD_DIM), HEAD_DIM)
+                outs[j][t * heads + h] = ref[:, at]
+
+
+def pack(meta, q, k, v, first, heads, group_width, after):
     rows = q.shape[0]
     whole = pl.BlockSpec(memory_space=pltpu.VMEM)
-    outs = pl.pallas_call(
-        functools.partial(pack_kernel, firsts, sizes, group_width),
-        out_shape=[
-            jax.ShapeDtypeStruct((3 * heads, rows, HEAD_DIM), q.dtype)
-            for heads in sizes
-            for _ in PLACES
-        ],
-        in_specs=[SMEM, whole, whole, whole],
-        out_specs=[whole] * (4 * len(sizes)),
+    return pl.pallas_call(
+        functools.partial(pack_kernel, first, heads, group_width, len(after)),
+        out_shape=[jax.ShapeDtypeStruct((3 * heads, rows, HEAD_DIM), q.dtype)] * 4,
+        in_specs=[SMEM, whole, whole, whole] + [ANY] * len(after),
+        out_specs=[whole] * 4,
         compiler_params=params(60),
-        cost_estimate=estimate(cost),
+        cost_estimate=estimate(0),
         name="pack",
-    )(meta, q, k, v)
-    return [outs[4 * i : 4 * i + 4] for i in range(len(sizes))]
+    )(meta, q, k, v, *after)
 
 
 def stack_kernel(heads, count, meta, *refs):
@@ -169,9 +164,11 @@
 
 
 def attend_rows(q_ref, p, blocks, o_ref, lse_ref):
-    rows = q_ref.shape[2]
+    rows, q = q_ref.shape[2], q_ref[0, p or 0]
+    if p is None:
+        rows, p, q = 2 * rows, 0, q_ref[0].reshape(2 * rows, HEAD_DIM)
     out, lse = softmax_part(
-        q_ref[0, p], [kv[0][0, i] for kv, i in blocks], [kv[1][0, i] for kv, i in blocks]
+        q, [kv[0][0, i] for kv, i in blocks], [kv[1][0, i] for kv, i in blocks]
     )
     o_ref[0, pl.ds(p * rows, rows)] = out.astype(o_ref.dtype)
     for t in range(rows // TILE):
@@ -225,8 +222,7 @@
 
     @pl.when(meta[8] >= 1)
     def _():
-        attend_rows(q, 0, every, part, part_lse)
-        attend_rows(q, 1, every, part, part_lse)
+        attend_rows(q, None, every, part, part_lse)
         lse[0] = blend(o_near, lse_near[0], part, part_lse[...], True, store)
 
     @pl.when(meta[8] < 1)
@@ -409,7 +405,10 @@
     firsts = [sum(sizes[:i]) for i in range(len(sizes))]
     chunks = range(len(sizes))
 
-    sent = pack(meta, queries, keys, values, firsts, sizes, group_width)
+    sent, packed = [], []
+    for first, size in zip(firsts, sizes):
+        sent.append(pack(meta, queries, keys, values, first, size, group_width, packed))
+        packed = [sent[-1][0]]
     last = [gate]
 
     q, kv, kv_up, q_down = {}, {}, {}, {}

time: 118 us -> 117 us (level)
  waiting for transfers between devices: 38.1 us -> 35.1 us
  Pallas kernels: 42.5 us -> 43.9 us
    ppermute x23, waiting for transfers between devices: 38.1 us -> 35.1 us  [move(): return lax.ppermute(block, AXES, route)]
    pallas_call x1 -> x2, Pallas kernels: 4.13 us -> 6.57 us  [pack(): pl.pallas_call(functools.partial(pack_kernel, first, heads, group_width,...]
  transfers between devices with their start and end apart: 23 -> 23, of which waited for: 13 -> 14; matrix products, arithmetic and copies ran while one was open for 3% -> 3% of each run, Pallas kernels for 30% -> 32%
where the time goes in v5:
time: 117 us; the launch traced here: 116 us
  Pallas kernels  43.9 us (38%)
  waiting for transfers between devices  35.1 us (30%)
  starting transfers between devices  32.5 us (28%)
  other arithmetic  1.94 us (2%)
  matrix products  1.34 us (1%)
    ppermute x23, waiting for transfers between devices, move(): return lax.ppermute(block, AXES, route)  35.1 us
    ppermute x23, starting transfers between devices, move(): return lax.ppermute(block, AXES, route)  32.5 us
    pallas_call x6, Pallas kernels, attend(): pl.pallas_call(functools.partial(body, len(after)), grid=(heads,), out_sh...  30.1 us
    pallas_call x2, Pallas kernels, pack(): pl.pallas_call(functools.partial(pack_kernel, first, heads, group_width,...  6.57 us
    pallas_call x2, Pallas kernels, stack(): pl.pallas_call(functools.partial(stack_kernel, heads, len(later) + len(af...  3.03 us
  transfers between devices with their start and end apart: 23, of which 14 were waited for; matrix products, arithmetic and copies ran while one was open for 3% of the time, Pallas kernels for 32%

profile of v5, /device:TPU:8, one launch (start us, length us, event | category | flops | bytes accessed | tf_op | source)
XLA Modules:
  0.0 116.4 jit_solution(813387886682259968)
XLA Ops:
  0.6 3.5 %pack.2 = (bf16[9,192,128]{2,1,0:T(8,128)(2,1)}, bf16[9,192,128]{2,1,0:T(8,128)(2,1)}, bf16[9,192,128]{2,1,0:T(8,128)(2,1)}, bf16[9,192,128]{2,1,0:T(8,128)(2,1)}) custom-call(s32[9]{0:T(128)} %stack.35.meta, bf16[192,2560]{1,0:T(8,128)(2,1)} %q.3, bf16[192,2560]{1,0:T(8,128)(2,1)} %k.3, bf16[192,2560]{1,0:T(8,128)(2,1)} %v.3), custom_call_target="tpu_custom_call" | custom-call | bytes 1000 | tf_op jit(solution)/shard_map/pack/pallas_call | solution.py:95
  10.3 3.1 %pack.3 = (bf16[6,192,128]{2,1,0:T(8,128)(2,1)}, bf16[6,192,128]{2,1,0:T(8,128)(2,1)}, bf16[6,192,128]{2,1,0:T(8,128)(2,1)}, bf16[6,192,128]{2,1,0:T(8,128)(2,1)}) custom-call(s32[9]{0:T(128)} %stack.35.meta, bf16[192,2560]{1,0:T(8,128)(2,1)} %q.3, bf16[192,2560]{1,0:T(8,128)(2,1)} %k.3, bf16[192,2560]{1,0:T(8,128)(2,1)} %v.3, ...), custom_call_target="tpu_custom_call" | custom-call | bytes 1000 | tf_op jit(solution)/shard_map/pack/pallas_call | solution.py:95
  14.7 1.8 %collective-permute-done.refs_1_ = bf16[9,192,128]{2,1,0:T(8,128)(2,1)S(1)} collective-permute-done((bf16[9,192,128]{2,1,0:T(8,128)(2,1)}, bf16[9,192,128]{2,1,0:T(8,128)(2,1)S(1)}, u32[]{:S(2)}, u32[]{:S(2)}) %collective-permute-start) | collective-permute-done | bytes 442400 | tf_op jit(solution)/shard_map/ppermute | solution.py:44
  16.5 2.4 %collective-permute-done.1.refs_2_ = bf16[9,192,128]{2,1,0:T(8,128)(2,1)S(1)} collective-permute-done((bf16[9,192,128]{2,1,0:T(8,128)(2,1)}, bf16[9,192,128]{2,1,0:T(8,128)(2,1)S(1)}, u32[]{:S(2)}, u32[]{:S(2)}) %collective-permute-start.1) | collective-permute-done | bytes 442400 | tf_op jit(solution)/shard_map/ppermute | solution.py:44
  19.0 8.1 %collective-permute-done.2.refs_3_ = bf16[9,192,128]{2,1,0:T(8,128)(2,1)} collective-permute-done((bf16[9,192,128]{2,1,0:T(8,128)(2,1)}, bf16[9,192,128]{2,1,0:T(8,128)(2,1)}, u32[]{:S(2)}, u32[]{:S(2)}) %collective-permute-start.2) | collective-permute-done | bytes 442400 | tf_op jit(solution)/shard_map/ppermute | solution.py:44
  27.1 1.9 %stack.36 = (bf16[3,2,384,128]{3,2,1,0:T(8,128)(2,1)S(1)}, bf16[6,2,384,128]{3,2,1,0:T(8,128)(2,1)S(1)}, bf16[6,192,128]{2,1,0:T(8,128)(2,1)S(1)}, bf16[6,192,12...) custom-call(s32[9]{0:T(128)S(1)} %copy-done.6, ...), custom_call_target="tpu_custom_call", output_to_operand_aliasing={{2}: (5, {}), {3}: (6, {}), {4}: (7, {})} | custom-call | bytes 1000 | tf_op jit(solution)/shard_map/stack/pallas_call | solution.py:131
  29.0 3.5 %collective-permute-start.3 = (bf16[6,2,384,128]{3,2,1,0:T(8,128)(2,1)S(1)}, bf16[6,2,384,128]{3,2,1,0:T(8,128)(2,1)S(1)}, u32[]{:S(2)}, u32[]{:S(2)}) collective-permute-start(bf16[6,2,384,128]{3,2,1,0:T(8,128)(2,1)S(1)} %get-tuple-element.46.ka.va), channel_id=1, source_target_pairs={{0,8},{1,9},{2,10},{3,11},{4,12},{5,13},{6,14},{7,15},{8,16},{9,17... | collective-permute-start | bytes 3538952 | tf_op jit(solution)/shard_map/ppermute | solution.py:44
  32.5 2.4 %collective-permute-start.8 = (bf16[3,2,384,128]{3,2,1,0:T(8,128)(2,1)S(1)}, bf16[3,2,384,128]{3,2,1,0:T(8,128)(2,1)S(1)}, u32[]{:S(2)}, u32[]{:S(2)}) collective-permute-start(bf16[3,2,384,128]{3,2,1,0:T(8,128)(2,1)S(1)} %get-tuple-element.45.q.rest_0_), channel_id=1, source_target_pairs={{8,0},{9,1},{10,2},{11,3},{12,4},{13,5},{14,6},{15,7},{16,8},{17,9... | collective-permute-start | bytes 1769480 | tf_op jit(solution)/shard_map/ppermute | solution.py:44
  38.5 5.2 %near.2 = (f32[3,768,128]{2,1,0:T(8,128)S(1)}, f32[3,8,128]{2,1,0:T(8,128)S(1)}) custom-call(bf16[3,2,384,128]{3,2,1,0:T(8,128)(2,1)S(1)} %get-tuple-element.45.q.rest_0_, bf16[6,2,384,128]{3,2,1,0:T(8,128)(2,1)S(1)} %get-tuple-element.46.ka.va, bf16[6,2,384,128]{3,2,1,0:T(8,128)(2,1)S(1)} %get-tuple-element.46.ka.va, ...), custom_call_target="tpu_custom_call" | custom-call | bytes 1000 | tf_op jit(solution)/shard_map/near/pallas_call | solution.py:311
  44.0 2.4 %collective-permute-done.5.refs_2_ = bf16[6,192,128]{2,1,0:T(8,128)(2,1)S(1)} collective-permute-done((bf16[6,192,128]{2,1,0:T(8,128)(2,1)S(1)}, bf16[6,192,128]{2,1,0:T(8,128)(2,1)S(1)}, u32[]{:S(2)}, u32[]{:S(2)}) %collective-permute-start.5) | collective-permute-done | bytes 294944 | tf_op jit(solution)/shard_map/ppermute | solution.py:44
  46.5 4.9 %collective-permute-done.6.refs_3_ = bf16[6,192,128]{2,1,0:T(8,128)(2,1)S(1)} collective-permute-done((bf16[6,192,128]{2,1,0:T(8,128)(2,1)S(1)}, bf16[6,192,128]{2,1,0:T(8,128)(2,1)S(1)}, u32[]{:S(2)}, u32[]{:S(2)}) %collective-permute-start.6) | collective-permute-done | bytes 294944 | tf_op jit(solution)/shard_map/ppermute | solution.py:44
  52.6 3.4 %collective-permute-start.12 = (bf16[4,2,384,128]{3,2,1,0:T(8,128)(2,1)S(1)}, bf16[4,2,384,128]{3,2,1,0:T(8,128)(2,1)S(1)}, u32[]{:S(2)}, u32[]{:S(2)}) collective-permute-start(bf16[4,2,384,128]{3,2,1,0:T(8,128)(2,1)S(1)} %get-tuple-element.56.ka.va), channel_id=1, source_target_pairs={{0,8},{1,9},{2,10},{3,11},{4,12},{5,13},{6,14},{7,15},{8,16},{9,17... | collective-permute-start | bytes 2359304 | tf_op jit(solution)/shard_map/ppermute | solution.py:44
  56.0 3.7 %collective-permute-done.3.kv = bf16[6,2,384,128]{3,2,1,0:T(8,128)(2,1)S(1)} collective-permute-done((bf16[6,2,384,128]{3,2,1,0:T(8,128)(2,1)S(1)}, bf16[6,2,384,128]{3,2,1,0:T(8,128)(2,1)S(1)}, u32[]{:S(2)}, u32[]{:S(2)}) %collective-permute-start.3) | collective-permute-done | bytes 1179680 | tf_op jit(solution)/shard_map/ppermute | solution.py:44
  60.5 1.9 %collective-permute-start.11 = (bf16[2,2,384,128]{3,2,1,0:T(8,128)(2,1)S(1)}, bf16[2,2,384,128]{3,2,1,0:T(8,128)(2,1)S(1)}, u32[]{:S(2)}, u32[]{:S(2)}) collective-permute-start(bf16[2,2,384,128]{3,2,1,0:T(8,128)(2,1)S(1)} %get-tuple-element.52.rest_0_.q), channel_id=1, source_target_pairs={{8,0},{9,1},{10,2},{11,3},{12,4},{13,5},{14,6},{15,7},{16,8},{17,9... | collective-permute-start | bytes 1179656 | tf_op jit(solution)/shard_map/ppermute | solution.py:44
  62.9 5.7 %remote.2.rest_0_ = bf16[3,800,128]{2,1,0:T(8,128)(2,1)S(1)} custom-call(bf16[3,2,384,128]{3,2,1,0:T(8,128)(2,1)S(1)} %collective-permute-done.8.refs_5_.q, bf16[3,2,384,128]{3,2,1,0:T(8,128)(2,1)S(1)} %get-tuple-element.53.ka, bf16[3,2,384,128]{3,2,1,0:T(8,128)(2,1)S(1)} %get-tuple-element.54.va, bf16[3,2,384,128]{3,2,1,0:T(8,128)(2,1)S(1)} %collective-permute-done.9.kb, ...), custom_call_target="tpu_custom_call" | custom-call | bytes 1000 | tf_op jit(solution)/shard_map/remote/pallas_call | solution.py:311
  68.5 5.0 %collective-permute-done.11.rest_1_.q = bf16[2,2,384,128]{3,2,1,0:T(8,128)(2,1)S(1)} collective-permute-done((bf16[2,2,384,128]{3,2,1,0:T(8,128)(2,1)S(1)}, bf16[2,2,384,128]{3,2,1,0:T(8,128)(2,1)S(1)}, u32[]{:S(2)}, u32[]{:S(2)}) %collective-permute-start.11) | collective-permute-done | bytes 393248 | tf_op jit(solution)/shard_map/ppermute | solution.py:44
  73.5 3.5 %near.3 = (f32[2,768,128]{2,1,0:T(8,128)S(1)}, f32[2,8,128]{2,1,0:T(8,128)S(1)}) custom-call(bf16[2,2,384,128]{3,2,1,0:T(8,128)(2,1)S(1)} %get-tuple-element.52.rest_0_.q, bf16[4,2,384,128]{3,2,1,0:T(8,128)(2,1)S(1)} %get-tuple-element.56.ka.va, bf16[4,2,384,128]{3,2,1,0:T(8,128)(2,1)S(1)} %get-tuple-element.56.ka.va, ...), custom_call_target="tpu_custom_call" | custom-call | bytes 1000 | tf_op jit(solution)/shard_map/near/pallas_call | solution.py:311
  77.1 3.5 %collective-permute-start.15 = (bf16[3,800,128]{2,1,0:T(8,128)(2,1)S(1)}, bf16[3,800,128]{2,1,0:T(8,128)(2,1)S(1)}, u32[]{:S(2)}, u32[]{:S(2)}) collective-permute-start(bf16[3,800,128]{2,1,0:T(8,128)(2,1)S(1)} %remote.2.rest_0_), channel_id=1, source_target_pairs={{0,8},{1,9},{2,10},{3,11},{4,12},{5,13},{6,14},{7,15},{8,16},{9,17... | collective-permute-start | bytes 1843208 | tf_op jit(solution)/shard_map/ppermute | solution.py:44
  80.6 3.8 %remote.3.rest_0_ = bf16[2,800,128]{2,1,0:T(8,128)(2,1)S(1)} custom-call(bf16[2,2,384,128]{3,2,1,0:T(8,128)(2,1)S(1)} %collective-permute-done.11.rest_1_.q, bf16[4,2,384,128]{3,2,1,0:T(8,128)(2,1)S(1)} %in_order.1.ka.va, bf16[4,2,384,128]{3,2,1,0:T(8,128)(2,1)S(1)} %in_order.1.ka.va, bf16[4,2,384,128]{3,2,1,0:T(8,128)(2,1)S(1)} %collective-permute-done.14.kb.vb, ...), custom_call_target="tpu_custom_call" | custom-call | bytes 1000 | tf_op jit(solution)/shard_map/remote/pallas_call | solution.py:311
  84.4 2.7 %collective-permute-start.19 = (bf16[2,800,128]{2,1,0:T(8,128)(2,1)S(1)}, bf16[2,800,128]{2,1,0:T(8,128)(2,1)S(1)}, u32[]{:S(2)}, u32[]{:S(2)}) collective-permute-start(bf16[2,800,128]{2,1,0:T(8,128)(2,1)S(1)} %remote.3.rest_0_), channel_id=1, source_target_pairs={{0,8},{1,9},{2,10},{3,11},{4,12},{5,13},{6,14},{7,15},{8,16},{9,17... | collective-permute-start | bytes 1228808 | tf_op jit(solution)/shard_map/ppermute | solution.py:44
  87.1 7.1 %far.2 = (f32[3,768,128]{2,1,0:T(8,128)S(1)}, f32[3,8,128]{2,1,0:T(8,128)S(1)}) custom-call(s32[9]{0:T(128)S(1)} %copy-done.6, bf16[3,2,384,128]{3,2,1,0:T(8,128)(2,1)S(1)} %get-tuple-element.45.q.rest_0_, bf16[3,2,384,128]{3,2,1,0:T(8,128)(2,1)S(1)} %get-tuple-element.53.ka, bf16[3,2,384,128]{3,2,1,0:T(8,128)(2,1)S(1)} %get-tuple-element.54.va, ...), custom_call_target="tpu_custom_call" | custom-call | bytes 1000 | tf_op jit(solution)/shard_map/far/pallas_call | solution.py:311
  94.2 4.9 %far.3 = (f32[2,768,128]{2,1,0:T(8,128)S(1)}, f32[2,8,128]{2,1,0:T(8,128)S(1)}) custom-call(s32[9]{0:T(128)S(1)} %copy-done.6, bf16[2,2,384,128]{3,2,1,0:T(8,128)(2,1)S(1)} %get-tuple-element.52.rest_0_.q, bf16[4,2,384,128]{3,2,1,0:T(8,128)(2,1)S(1)} %in_order.1.ka.va, bf16[4,2,384,128]{3,2,1,0:T(8,128)(2,1)S(1)} %in_order.1.ka.va, ...), custom_call_target="tpu_custom_call" | custom-call | bytes 1000 | tf_op jit(solution)/shard_map/far/pallas_call | solution.py:311
  108.7 2.8 %collective-permute-done.18.refs_3_ = bf16[3,192,128]{2,1,0:T(8,128)(2,1)S(1)} collective-permute-done((bf16[3,192,128]{2,1,0:T(8,128)(2,1)S(1)}, bf16[3,192,128]{2,1,0:T(8,128)(2,1)S(1)}, u32[]{:S(2)}, u32[]{:S(2)}) %collective-permute-start.18) | collective-permute-done | bytes 147488 | tf_op jit(solution)/shard_map/ppermute | solution.py:44
  114.7 1.7 %finish.1 = bf16[192,2560]{1,0:T(8,128)(2,1)} custom-call(s32[9]{0:T(128)S(1)} %copy-done.6, f32[1,2560]{1,0:T(1,128)S(1)} %fusion.4.refs_7_.gate, bf16[3,192,128]{2,1,0:T(8,128)(2,1)S(1)} %get-tuple-element.62.rest_0_.refs_0_, bf16[3,192,128]{2,1,0:T(8,128)(2,1)S(1)} %collective-permute-done.16.refs_1_, ...), custom_call_target="tpu_custom_call" | custom-call | bytes 1000 | tf_op jit(solution)/shard_map/finish/pallas_call | solution.py:372
  (61 shorter events, 26.7 us)
Async XLA Ops:
  4.1 12.4 %collective-permute-start = (bf16[9,192,128]{2,1,0:T(8,128)(2,1)}, bf16[9,192,128]{2,1,0:T(8,128)(2,1)S(1)}, u32[]{:S(2)}, u32[]{:S(2)}) collective-permute-start(bf16[9,192,128]{2,1,0:T(8,128)(2,1)} %get-tuple-element.39), channel_id=1, source_target_pairs={{0,4},{1,5},{2,6},{3,7},{4,0},{5,1},{6,2},{7,3},{8,12},{9,13},{10,... | collective-permute-start | bytes 1327112 | tf_op jit(solution)/shard_map/ppermute | solution.py:44
  5.7 13.3 %collective-permute-start.1 = (bf16[9,192,128]{2,1,0:T(8,128)(2,1)}, bf16[9,192,128]{2,1,0:T(8,128)(2,1)S(1)}, u32[]{:S(2)}, u32[]{:S(2)}) collective-permute-start(bf16[9,192,128]{2,1,0:T(8,128)(2,1)} %get-tuple-element.40), channel_id=1, source_target_pairs={{0,2},{1,3},{2,0},{3,1},{4,6},{5,7},{6,4},{7,5},{8,10},{9,11},{10,... | collective-permute-start | bytes 1327112 | tf_op jit(solution)/shard_map/ppermute | solution.py:44
  7.2 19.9 %collective-permute-start.2 = (bf16[9,192,128]{2,1,0:T(8,128)(2,1)}, bf16[9,192,128]{2,1,0:T(8,128)(2,1)}, u32[]{:S(2)}, u32[]{:S(2)}) collective-permute-start(bf16[9,192,128]{2,1,0:T(8,128)(2,1)} %get-tuple-element.41), channel_id=1, source_target_pairs={{0,6},{1,7},{2,4},{3,5},{4,2},{5,3},{6,0},{7,1},{8,14},{9,15},{10,... | collective-permute-start | bytes 1327112 | tf_op jit(solution)/shard_map/ppermute | solution.py:44
  13.3 13.7 %copy-start.1 = (bf16[9,192,128]{2,1,0:T(8,128)(2,1)S(1)}, bf16[9,192,128]{2,1,0:T(8,128)(2,1)}, u32[]{:S(2)}) copy-start(bf16[9,192,128]{2,1,0:T(8,128)(2,1)} %get-tuple-element.38.rest_0_.refs_0_) | copy-start | bytes 1327108
  28.9 9.1 %collective-permute-start.7 = (bf16[6,2,384,128]{3,2,1,0:T(8,128)(2,1)S(1)}, bf16[6,2,384,128]{3,2,1,0:T(8,128)(2,1)S(1)}, u32[]{:S(2)}, u32[]{:S(2)}) collective-permute-start(bf16[6,2,384,128]{3,2,1,0:T(8,128)(2,1)S(1)} %get-tuple-element.46.ka.va), channel_id=1, source_target_pairs={{0,1},{1,0},{2,3},{3,2},{4,5},{5,4},{6,7},{7,6},{8,9},{9,8},{10,11... | collective-permute-start | bytes 3538952 | tf_op jit(solution)/shard_map/ppermute | solution.py:44
  29.0 30.7 %collective-permute-start.3 = (bf16[6,2,384,128]{3,2,1,0:T(8,128)(2,1)S(1)}, bf16[6,2,384,128]{3,2,1,0:T(8,128)(2,1)S(1)}, u32[]{:S(2)}, u32[]{:S(2)}) collective-permute-start(bf16[6,2,384,128]{3,2,1,0:T(8,128)(2,1)S(1)} %get-tuple-element.46.ka.va), channel_id=1, source_target_pairs={{0,8},{1,9},{2,10},{3,11},{4,12},{5,13},{6,14},{7,15},{8,16},{9,17... | collective-permute-start | bytes 3538952 | tf_op jit(solution)/shard_map/ppermute | solution.py:44
  32.5 18.8 %collective-permute-start.8 = (bf16[3,2,384,128]{3,2,1,0:T(8,128)(2,1)S(1)}, bf16[3,2,384,128]{3,2,1,0:T(8,128)(2,1)S(1)}, u32[]{:S(2)}, u32[]{:S(2)}) collective-permute-start(bf16[3,2,384,128]{3,2,1,0:T(8,128)(2,1)S(1)} %get-tuple-element.45.q.rest_0_), channel_id=1, source_target_pairs={{8,0},{9,1},{10,2},{11,3},{12,4},{13,5},{14,6},{15,7},{16,8},{17,9... | collective-permute-start | bytes 1769480 | tf_op jit(solution)/shard_map/ppermute | solution.py:44
  35.0 9.1 %collective-permute-start.4 = (bf16[6,192,128]{2,1,0:T(8,128)(2,1)S(1)}, bf16[6,192,128]{2,1,0:T(8,128)(2,1)S(1)}, u32[]{:S(2)}, u32[]{:S(2)}) collective-permute-start(bf16[6,192,128]{2,1,0:T(8,128)(2,1)S(1)} %get-tuple-element.48), channel_id=1, source_target_pairs={{0,4},{1,5},{2,6},{3,7},{4,0},{5,1},{6,2},{7,3},{8,12},{9,13},{10,... | collective-permute-start | bytes 884744 | tf_op jit(solution)/shard_map/ppermute | solution.py:44
  36.5 9.9 %collective-permute-start.5 = (bf16[6,192,128]{2,1,0:T(8,128)(2,1)S(1)}, bf16[6,192,128]{2,1,0:T(8,128)(2,1)S(1)}, u32[]{:S(2)}, u32[]{:S(2)}) collective-permute-start(bf16[6,192,128]{2,1,0:T(8,128)(2,1)S(1)} %get-tuple-element.49), channel_id=1, source_target_pairs={{0,2},{1,3},{2,0},{3,1},{4,6},{5,7},{6,4},{7,5},{8,10},{9,11},{10,... | collective-permute-start | bytes 884744 | tf_op jit(solution)/shard_map/ppermute | solution.py:44
  38.0 13.3 %collective-permute-start.6 = (bf16[6,192,128]{2,1,0:T(8,128)(2,1)S(1)}, bf16[6,192,128]{2,1,0:T(8,128)(2,1)S(1)}, u32[]{:S(2)}, u32[]{:S(2)}) collective-permute-start(bf16[6,192,128]{2,1,0:T(8,128)(2,1)S(1)} %get-tuple-element.50), channel_id=1, source_target_pairs={{0,6},{1,7},{2,4},{3,5},{4,2},{5,3},{6,0},{7,1},{8,14},{9,15},{10,... | collective-permute-start | bytes 884744 | tf_op jit(solution)/shard_map/ppermute | solution.py:44
  52.5 21.0 %collective-permute-start.13 = (bf16[4,2,384,128]{3,2,1,0:T(8,128)(2,1)S(1)}, bf16[4,2,384,128]{3,2,1,0:T(8,128)(2,1)S(1)}, u32[]{:S(2)}, u32[]{:S(2)}) collective-permute-start(bf16[4,2,384,128]{3,2,1,0:T(8,128)(2,1)S(1)} %get-tuple-element.56.ka.va), channel_id=1, source_target_pairs={{0,1},{1,0},{2,3},{3,2},{4,5},{5,4},{6,7},{7,6},{8,9},{9,8},{10,11... | collective-permute-start | bytes 2359304 | tf_op jit(solution)/shard_map/ppermute | solution.py:44
  52.6 24.4 %collective-permute-start.12 = (bf16[4,2,384,128]{3,2,1,0:T(8,128)(2,1)S(1)}, bf16[4,2,384,128]{3,2,1,0:T(8,128)(2,1)S(1)}, u32[]{:S(2)}, u32[]{:S(2)}) collective-permute-start(bf16[4,2,384,128]{3,2,1,0:T(8,128)(2,1)S(1)} %get-tuple-element.56.ka.va), channel_id=1, source_target_pairs={{0,8},{1,9},{2,10},{3,11},{4,12},{5,13},{6,14},{7,15},{8,16},{9,17... | collective-permute-start | bytes 2359304 | tf_op jit(solution)/shard_map/ppermute | solution.py:44
  59.9 2.5 %collective-permute-start.9 = (bf16[3,2,384,128]{3,2,1,0:T(8,128)(2,1)S(1)}, bf16[3,2,384,128]{3,2,1,0:T(8,128)(2,1)S(1)}, u32[]{:S(2)}, u32[]{:S(2)}) collective-permute-start(bf16[3,2,384,128]{3,2,1,0:T(8,128)(2,1)S(1)} %get-tuple-element.53.ka), channel_id=1, source_target_pairs={{0,1},{1,0},{2,3},{3,2},{4,5},{5,4},{6,7},{7,6},{8,9},{9,8},{10,11... | collective-permute-start | bytes 1769480 | tf_op jit(solution)/shard_map/ppermute | solution.py:44
  60.0 2.8 %collective-permute-start.10 = (bf16[3,2,384,128]{3,2,1,0:T(8,128)(2,1)S(1)}, bf16[3,2,384,128]{3,2,1,0:T(8,128)(2,1)S(1)}, u32[]{:S(2)}, u32[]{:S(2)}) collective-permute-start(bf16[3,2,384,128]{3,2,1,0:T(8,128)(2,1)S(1)} %get-tuple-element.54.va), channel_id=1, source_target_pairs={{0,1},{1,0},{2,3},{3,2},{4,5},{5,4},{6,7},{7,6},{8,9},{9,8},{10,11... | collective-permute-start | bytes 1769480 | tf_op jit(solution)/shard_map/ppermute | solution.py:44
  60.5 13.0 %collective-permute-start.11 = (bf16[2,2,384,128]{3,2,1,0:T(8,128)(2,1)S(1)}, bf16[2,2,384,128]{3,2,1,0:T(8,128)(2,1)S(1)}, u32[]{:S(2)}, u32[]{:S(2)}) collective-permute-start(bf16[2,2,384,128]{3,2,1,0:T(8,128)(2,1)S(1)} %get-tuple-element.52.rest_0_.q), channel_id=1, source_target_pairs={{8,0},{9,1},{10,2},{11,3},{12,4},{13,5},{14,6},{15,7},{16,8},{17,9... | collective-permute-start | bytes 1179656 | tf_op jit(solution)/shard_map/ppermute | solution.py:44
  77.0 3.6 %collective-permute-start.14 = (bf16[4,2,384,128]{3,2,1,0:T(8,128)(2,1)S(1)}, bf16[4,2,384,128]{3,2,1,0:T(8,128)(2,1)S(1)}, u32[]{:S(2)}, u32[]{:S(2)}) collective-permute-start(bf16[4,2,384,128]{3,2,1,0:T(8,128)(2,1)S(1)} %in_order.1.ka.va), channel_id=1, source_target_pairs={{0,1},{1,0},{2,3},{3,2},{4,5},{5,4},{6,7},{7,6},{8,9},{9,8},{10,11... | collective-permute-start | bytes 2359304 | tf_op jit(solution)/shard_map/ppermute | solution.py:44
  77.1 22.0 %collective-permute-start.15 = (bf16[3,800,128]{2,1,0:T(8,128)(2,1)S(1)}, bf16[3,800,128]{2,1,0:T(8,128)(2,1)S(1)}, u32[]{:S(2)}, u32[]{:S(2)}) collective-permute-start(bf16[3,800,128]{2,1,0:T(8,128)(2,1)S(1)} %remote.2.rest_0_), channel_id=1, source_target_pairs={{0,8},{1,9},{2,10},{3,11},{4,12},{5,13},{6,14},{7,15},{8,16},{9,17... | collective-permute-start | bytes 1843208 | tf_op jit(solution)/shard_map/ppermute | solution.py:44
  84.4 19.6 %collective-permute-start.19 = (bf16[2,800,128]{2,1,0:T(8,128)(2,1)S(1)}, bf16[2,800,128]{2,1,0:T(8,128)(2,1)S(1)}, u32[]{:S(2)}, u32[]{:S(2)}) collective-permute-start(bf16[2,800,128]{2,1,0:T(8,128)(2,1)S(1)} %remote.3.rest_0_), channel_id=1, source_target_pairs={{0,8},{1,9},{2,10},{3,11},{4,12},{5,13},{6,14},{7,15},{8,16},{9,17... | collective-permute-start | bytes 1228808 | tf_op jit(solution)/shard_map/ppermute | solution.py:44
  100.3 7.8 %collective-permute-start.16 = (bf16[3,192,128]{2,1,0:T(8,128)(2,1)S(1)}, bf16[3,192,128]{2,1,0:T(8,128)(2,1)S(1)}, u32[]{:S(2)}, u32[]{:S(2)}) collective-permute-start(bf16[3,192,128]{2,1,0:T(8,128)(2,1)S(1)} %get-tuple-element.63), channel_id=1, source_target_pairs={{0,4},{1,5},{2,6},{3,7},{4,0},{5,1},{6,2},{7,3},{8,12},{9,13},{10,... | collective-permute-start | bytes 442376 | tf_op jit(solution)/shard_map/ppermute | solution.py:44
  101.9 6.8 %collective-permute-start.17 = (bf16[3,192,128]{2,1,0:T(8,128)(2,1)S(1)}, bf16[3,192,128]{2,1,0:T(8,128)(2,1)S(1)}, u32[]{:S(2)}, u32[]{:S(2)}) collective-permute-start(bf16[3,192,128]{2,1,0:T(8,128)(2,1)S(1)} %get-tuple-element.64), channel_id=1, source_target_pairs={{0,2},{1,3},{2,0},{3,1},{4,6},{5,7},{6,4},{7,5},{8,10},{9,11},{10,... | collective-permute-start | bytes 442376 | tf_op jit(solution)/shard_map/ppermute | solution.py:44
  103.4 8.1 %collective-permute-start.18 = (bf16[3,192,128]{2,1,0:T(8,128)(2,1)S(1)}, bf16[3,192,128]{2,1,0:T(8,128)(2,1)S(1)}, u32[]{:S(2)}, u32[]{:S(2)}) collective-permute-start(bf16[3,192,128]{2,1,0:T(8,128)(2,1)S(1)} %get-tuple-element.65), channel_id=1, source_target_pairs={{0,6},{1,7},{2,4},{3,5},{4,2},{5,3},{6,0},{7,1},{8,14},{9,15},{10,... | collective-permute-start | bytes 442376 | tf_op jit(solution)/shard_map/ppermute | solution.py:44
  105.0 7.6 %collective-permute-start.20 = (bf16[2,192,128]{2,1,0:T(8,128)(2,1)S(1)}, bf16[2,192,128]{2,1,0:T(8,128)(2,1)S(1)}, u32[]{:S(2)}, u32[]{:S(2)}) collective-permute-start(bf16[2,192,128]{2,1,0:T(8,128)(2,1)S(1)} %get-tuple-element.68), channel_id=1, source_target_pairs={{0,4},{1,5},{2,6},{3,7},{4,0},{5,1},{6,2},{7,3},{8,12},{9,13},{10,... | collective-permute-start | bytes 294920 | tf_op jit(solution)/shard_map/ppermute | solution.py:44
  106.6 7.1 %collective-permute-start.21 = (bf16[2,192,128]{2,1,0:T(8,128)(2,1)S(1)}, bf16[2,192,128]{2,1,0:T(8,128)(2,1)S(1)}, u32[]{:S(2)}, u32[]{:S(2)}) collective-permute-start(bf16[2,192,128]{2,1,0:T(8,128)(2,1)S(1)} %get-tuple-element.69), channel_id=1, source_target_pairs={{0,2},{1,3},{2,0},{3,1},{4,6},{5,7},{6,4},{7,5},{8,10},{9,11},{10,... | collective-permute-start | bytes 294920 | tf_op jit(solution)/shard_map/ppermute | solution.py:44
  108.1 6.6 %collective-permute-start.22 = (bf16[2,192,128]{2,1,0:T(8,128)(2,1)S(1)}, bf16[2,192,128]{2,1,0:T(8,128)(2,1)S(1)}, u32[]{:S(2)}, u32[]{:S(2)}) collective-permute-start(bf16[2,192,128]{2,1,0:T(8,128)(2,1)S(1)} %get-tuple-element.70), channel_id=1, source_target_pairs={{0,6},{1,7},{2,4},{3,5},{4,2},{5,3},{6,0},{7,1},{8,14},{9,15},{10,... | collective-permute-start | bytes 294920 | tf_op jit(solution)/shard_map/ppermute | solution.py:44
  (8 other events, 96.0 us)

commit v6 on v5

--- a/solution.py
+++ b/solution.py
@@ -18,7 +18,7 @@
 APART = (0,)
 COSTS = {}
 EARLY = False
-ORDER = "s0 n0 s1+q0 r0 n1+q1 r1 f0 f1 c0 c1"
+ORDER = "s0 n0 s1+q0 r0 f0 r1+q1 n1 f1 c0 c1"
 NT = (((1,), (1,)), ((), ()))
 NN = (((1,), (0,)), ((), ()))
 
@@ -459,7 +459,9 @@
     steps = {"s": spread, "n": near, "r": remote, "f": own_far, "c": close}
     for step in ORDER.split():
         name, *extra = step.split("+")
-        extra = [{"q": q_down, "o": far}[e[0]][int(e[1])] for e in extra]
+        kinds = {"q": q_down, "o": far, "b": results}
+        extra = [kinds[e[0]][int(e[1])] for e in extra]
+        extra = [block for e in extra for block in (e[1:] if isinstance(e, list) else [e])]
         last = steps[name[0]](int(name[1]), last + extra, COSTS.get(name, 0))
     return finish(meta, gate, sum((results[i] for i in chunks), []), firsts, group_width)
 

time: 117 us -> 115 us (0.983)
  waiting for transfers between devices: 35.1 us -> 31.9 us
  starting transfers between devices: 32.5 us -> 33.7 us
    ppermute x23, waiting for transfers between devices: 35.1 us -> 31.9 us  [move(): return lax.ppermute(block, AXES, route)]
    ppermute x23, starting transfers between devices: 32.5 us -> 33.7 us  [move(): return lax.ppermute(block, AXES, route)]
  transfers between devices with their start and end apart: 23 -> 23, of which waited for: 14 -> 13; matrix products, arithmetic and copies ran while one was open for 3% -> 3% of each run, Pallas kernels for 32% -> 32%
where the time goes in v6:
time: 115 us; the launch traced here: 114 us
  Pallas kernels  43.9 us (38%)
  starting transfers between devices  33.7 us (29%)
  waiting for transfers between devices  31.9 us (28%)
  other arithmetic  1.94 us (2%)
  matrix products  1.34 us (1%)
    ppermute x23, starting transfers between devices, move(): return lax.ppermute(block, AXES, route)  33.7 us
    ppermute x23, waiting for transfers between devices, move(): return lax.ppermute(block, AXES, route)  31.9 us
    pallas_call x6, Pallas kernels, attend(): pl.pallas_call(functools.partial(body, len(after)), grid=(heads,), out_sh...  30.1 us
    pallas_call x2, Pallas kernels, pack(): pl.pallas_call(functools.partial(pack_kernel, first, heads, group_width,...  6.57 us
    pallas_call x2, Pallas kernels, stack(): pl.pallas_call(functools.partial(stack_kernel, heads, len(later) + len(af...  3.03 us
  transfers between devices with their start and end apart: 23, of which 13 were waited for; matrix products, arithmetic and copies ran while one was open for 3% of the time, Pallas kernels for 32%

profile of v6, /device:TPU:8, one launch (start us, length us, event | category | flops | bytes accessed | tf_op | source)
XLA Modules:
  0.0 114.4 jit_solution(2890983336870234285)
XLA Ops:
  0.6 3.5 %pack.2 = (bf16[9,192,128]{2,1,0:T(8,128)(2,1)}, bf16[9,192,128]{2,1,0:T(8,128)(2,1)}, bf16[9,192,128]{2,1,0:T(8,128)(2,1)}, bf16[9,192,128]{2,1,0:T(8,128)(2,1)}) custom-call(s32[9]{0:T(128)} %stack.35.meta, bf16[192,2560]{1,0:T(8,128)(2,1)} %q.3, bf16[192,2560]{1,0:T(8,128)(2,1)} %k.3, bf16[192,2560]{1,0:T(8,128)(2,1)} %v.3), custom_call_target="tpu_custom_call" | custom-call | bytes 1000 | tf_op jit(solution)/shard_map/pack/pallas_call | solution.py:95
  10.3 3.1 %pack.3 = (bf16[6,192,128]{2,1,0:T(8,128)(2,1)}, bf16[6,192,128]{2,1,0:T(8,128)(2,1)}, bf16[6,192,128]{2,1,0:T(8,128)(2,1)}, bf16[6,192,128]{2,1,0:T(8,128)(2,1)}) custom-call(s32[9]{0:T(128)} %stack.35.meta, bf16[192,2560]{1,0:T(8,128)(2,1)} %q.3, bf16[192,2560]{1,0:T(8,128)(2,1)} %k.3, bf16[192,2560]{1,0:T(8,128)(2,1)} %v.3, ...), custom_call_target="tpu_custom_call" | custom-call | bytes 1000 | tf_op jit(solution)/shard_map/pack/pallas_call | solution.py:95
  14.7 1.8 %collective-permute-done.refs_1_ = bf16[9,192,128]{2,1,0:T(8,128)(2,1)S(1)} collective-permute-done((bf16[9,192,128]{2,1,0:T(8,128)(2,1)}, bf16[9,192,128]{2,1,0:T(8,128)(2,1)S(1)}, u32[]{:S(2)}, u32[]{:S(2)}) %collective-permute-start) | collective-permute-done | bytes 442400 | tf_op jit(solution)/shard_map/ppermute | solution.py:44
  16.5 2.4 %collective-permute-done.1.refs_2_ = bf16[9,192,128]{2,1,0:T(8,128)(2,1)S(1)} collective-permute-done((bf16[9,192,128]{2,1,0:T(8,128)(2,1)}, bf16[9,192,128]{2,1,0:T(8,128)(2,1)S(1)}, u32[]{:S(2)}, u32[]{:S(2)}) %collective-permute-start.1) | collective-permute-done | bytes 442400 | tf_op jit(solution)/shard_map/ppermute | solution.py:44
  19.0 8.1 %collective-permute-done.2.refs_3_ = bf16[9,192,128]{2,1,0:T(8,128)(2,1)} collective-permute-done((bf16[9,192,128]{2,1,0:T(8,128)(2,1)}, bf16[9,192,128]{2,1,0:T(8,128)(2,1)}, u32[]{:S(2)}, u32[]{:S(2)}) %collective-permute-start.2) | collective-permute-done | bytes 442400 | tf_op jit(solution)/shard_map/ppermute | solution.py:44
  27.1 1.9 %stack.36 = (bf16[3,2,384,128]{3,2,1,0:T(8,128)(2,1)S(1)}, bf16[6,2,384,128]{3,2,1,0:T(8,128)(2,1)S(1)}, bf16[6,192,128]{2,1,0:T(8,128)(2,1)S(1)}, bf16[6,192,12...) custom-call(s32[9]{0:T(128)S(1)} %copy-done.6, ...), custom_call_target="tpu_custom_call", output_to_operand_aliasing={{2}: (5, {}), {3}: (6, {}), {4}: (7, {})} | custom-call | bytes 1000 | tf_op jit(solution)/shard_map/stack/pallas_call | solution.py:131
  29.0 3.5 %collective-permute-start.3 = (bf16[6,2,384,128]{3,2,1,0:T(8,128)(2,1)S(1)}, bf16[6,2,384,128]{3,2,1,0:T(8,128)(2,1)S(1)}, u32[]{:S(2)}, u32[]{:S(2)}) collective-permute-start(bf16[6,2,384,128]{3,2,1,0:T(8,128)(2,1)S(1)} %get-tuple-element.46.ka.va), channel_id=1, source_target_pairs={{0,8},{1,9},{2,10},{3,11},{4,12},{5,13},{6,14},{7,15},{8,16},{9,17... | collective-permute-start | bytes 3538952 | tf_op jit(solution)/shard_map/ppermute | solution.py:44
  32.5 2.4 %collective-permute-start.8 = (bf16[3,2,384,128]{3,2,1,0:T(8,128)(2,1)S(1)}, bf16[3,2,384,128]{3,2,1,0:T(8,128)(2,1)S(1)}, u32[]{:S(2)}, u32[]{:S(2)}) collective-permute-start(bf16[3,2,384,128]{3,2,1,0:T(8,128)(2,1)S(1)} %get-tuple-element.45.q.rest_0_), channel_id=1, source_target_pairs={{8,0},{9,1},{10,2},{11,3},{12,4},{13,5},{14,6},{15,7},{16,8},{17,9... | collective-permute-start | bytes 1769480 | tf_op jit(solution)/shard_map/ppermute | solution.py:44
  38.5 5.2 %near.2 = (f32[3,768,128]{2,1,0:T(8,128)S(1)}, f32[3,8,128]{2,1,0:T(8,128)S(1)}) custom-call(bf16[3,2,384,128]{3,2,1,0:T(8,128)(2,1)S(1)} %get-tuple-element.45.q.rest_0_, bf16[6,2,384,128]{3,2,1,0:T(8,128)(2,1)S(1)} %get-tuple-element.46.ka.va, bf16[6,2,384,128]{3,2,1,0:T(8,128)(2,1)S(1)} %get-tuple-element.46.ka.va, ...), custom_call_target="tpu_custom_call" | custom-call | bytes 1000 | tf_op jit(solution)/shard_map/near/pallas_call | solution.py:311
  44.0 2.4 %collective-permute-done.5.refs_2_ = bf16[6,192,128]{2,1,0:T(8,128)(2,1)S(1)} collective-permute-done((bf16[6,192,128]{2,1,0:T(8,128)(2,1)S(1)}, bf16[6,192,128]{2,1,0:T(8,128)(2,1)S(1)}, u32[]{:S(2)}, u32[]{:S(2)}) %collective-permute-start.5) | collective-permute-done | bytes 294944 | tf_op jit(solution)/shard_map/ppermute | solution.py:44
  46.5 4.9 %collective-permute-done.6.refs_3_ = bf16[6,192,128]{2,1,0:T(8,128)(2,1)S(1)} collective-permute-done((bf16[6,192,128]{2,1,0:T(8,128)(2,1)S(1)}, bf16[6,192,128]{2,1,0:T(8,128)(2,1)S(1)}, u32[]{:S(2)}, u32[]{:S(2)}) %collective-permute-start.6) | collective-permute-done | bytes 294944 | tf_op jit(solution)/shard_map/ppermute | solution.py:44
  52.5 3.4 %collective-permute-start.12 = (bf16[4,2,384,128]{3,2,1,0:T(8,128)(2,1)S(1)}, bf16[4,2,384,128]{3,2,1,0:T(8,128)(2,1)S(1)}, u32[]{:S(2)}, u32[]{:S(2)}) collective-permute-start(bf16[4,2,384,128]{3,2,1,0:T(8,128)(2,1)S(1)} %get-tuple-element.58.ka.va), channel_id=1, source_target_pairs={{0,8},{1,9},{2,10},{3,11},{4,12},{5,13},{6,14},{7,15},{8,16},{9,17... | collective-permute-start | bytes 2359304 | tf_op jit(solution)/shard_map/ppermute | solution.py:44
  55.9 3.7 %collective-permute-done.3.kv = bf16[6,2,384,128]{3,2,1,0:T(8,128)(2,1)S(1)} collective-permute-done((bf16[6,2,384,128]{3,2,1,0:T(8,128)(2,1)S(1)}, bf16[6,2,384,128]{3,2,1,0:T(8,128)(2,1)S(1)}, u32[]{:S(2)}, u32[]{:S(2)}) %collective-permute-start.3) | collective-permute-done | bytes 1179680 | tf_op jit(solution)/shard_map/ppermute | solution.py:44
  60.5 1.9 %collective-permute-start.13 = (bf16[2,2,384,128]{3,2,1,0:T(8,128)(2,1)S(1)}, bf16[2,2,384,128]{3,2,1,0:T(8,128)(2,1)S(1)}, u32[]{:S(2)}, u32[]{:S(2)}) collective-permute-start(bf16[2,2,384,128]{3,2,1,0:T(8,128)(2,1)S(1)} %get-tuple-element.52.rest_0_.q), channel_id=1, source_target_pairs={{8,0},{9,1},{10,2},{11,3},{12,4},{13,5},{14,6},{15,7},{16,8},{17,9... | collective-permute-start | bytes 1179656 | tf_op jit(solution)/shard_map/ppermute | solution.py:44
  62.9 5.7 %remote.2.rest_0_ = bf16[3,800,128]{2,1,0:T(8,128)(2,1)S(1)} custom-call(bf16[3,2,384,128]{3,2,1,0:T(8,128)(2,1)S(1)} %collective-permute-done.8.refs_5_.q, bf16[3,2,384,128]{3,2,1,0:T(8,128)(2,1)S(1)} %get-tuple-element.53.ka, bf16[3,2,384,128]{3,2,1,0:T(8,128)(2,1)S(1)} %get-tuple-element.54.va, bf16[3,2,384,128]{3,2,1,0:T(8,128)(2,1)S(1)} %collective-permute-done.9.kb, ...), custom_call_target="tpu_custom_call" | custom-call | bytes 1000 | tf_op jit(solution)/shard_map/remote/pallas_call | solution.py:311
  68.5 7.0 %far.2 = (f32[3,768,128]{2,1,0:T(8,128)S(1)}, f32[3,8,128]{2,1,0:T(8,128)S(1)}) custom-call(s32[9]{0:T(128)S(1)} %copy-done.6, bf16[3,2,384,128]{3,2,1,0:T(8,128)(2,1)S(1)} %get-tuple-element.45.q.rest_0_, bf16[3,2,384,128]{3,2,1,0:T(8,128)(2,1)S(1)} %get-tuple-element.53.ka, bf16[3,2,384,128]{3,2,1,0:T(8,128)(2,1)S(1)} %get-tuple-element.54.va, ...), custom_call_target="tpu_custom_call" | custom-call | bytes 1000 | tf_op jit(solution)/shard_map/far/pallas_call | solution.py:311
  76.6 3.5 %collective-permute-start.11 = (bf16[3,800,128]{2,1,0:T(8,128)(2,1)S(1)}, bf16[3,800,128]{2,1,0:T(8,128)(2,1)S(1)}, u32[]{:S(2)}, u32[]{:S(2)}) collective-permute-start(bf16[3,800,128]{2,1,0:T(8,128)(2,1)S(1)} %remote.2.rest_0_), channel_id=1, source_target_pairs={{0,8},{1,9},{2,10},{3,11},{4,12},{5,13},{6,14},{7,15},{8,16},{9,17... | collective-permute-start | bytes 1843208 | tf_op jit(solution)/shard_map/ppermute | solution.py:44
  80.1 3.8 %remote.3.rest_0_ = bf16[2,800,128]{2,1,0:T(8,128)(2,1)S(1)} custom-call(bf16[2,2,384,128]{3,2,1,0:T(8,128)(2,1)S(1)} %collective-permute-done.13.refs_2_.q, bf16[4,2,384,128]{3,2,1,0:T(8,128)(2,1)S(1)} %in_order.1.ka.va, bf16[4,2,384,128]{3,2,1,0:T(8,128)(2,1)S(1)} %in_order.1.ka.va, bf16[4,2,384,128]{3,2,1,0:T(8,128)(2,1)S(1)} %collective-permute-done.14.kb.vb, ...), custom_call_target="tpu_custom_call" | custom-call | bytes 1000 | tf_op jit(solution)/shard_map/remote/pallas_call | solution.py:311
  83.9 3.7 %collective-permute-start.19 = (bf16[2,800,128]{2,1,0:T(8,128)(2,1)S(1)}, bf16[2,800,128]{2,1,0:T(8,128)(2,1)S(1)}, u32[]{:S(2)}, u32[]{:S(2)}) collective-permute-start(bf16[2,800,128]{2,1,0:T(8,128)(2,1)S(1)} %remote.3.rest_0_), channel_id=1, source_target_pairs={{0,8},{1,9},{2,10},{3,11},{4,12},{5,13},{6,14},{7,15},{8,16},{9,17... | collective-permute-start | bytes 1228808 | tf_op jit(solution)/shard_map/ppermute | solution.py:44
  87.6 3.5 %near.3 = (f32[2,768,128]{2,1,0:T(8,128)S(1)}, f32[2,8,128]{2,1,0:T(8,128)S(1)}) custom-call(bf16[2,2,384,128]{3,2,1,0:T(8,128)(2,1)S(1)} %get-tuple-element.52.rest_0_.q, bf16[4,2,384,128]{3,2,1,0:T(8,128)(2,1)S(1)} %get-tuple-element.58.ka.va, bf16[4,2,384,128]{3,2,1,0:T(8,128)(2,1)S(1)} %get-tuple-element.58.ka.va, ...), custom_call_target="tpu_custom_call" | custom-call | bytes 1000 | tf_op jit(solution)/shard_map/near/pallas_call | solution.py:311
  91.1 4.9 %far.3 = (f32[2,768,128]{2,1,0:T(8,128)S(1)}, f32[2,8,128]{2,1,0:T(8,128)S(1)}) custom-call(s32[9]{0:T(128)S(1)} %copy-done.6, bf16[2,2,384,128]{3,2,1,0:T(8,128)(2,1)S(1)} %get-tuple-element.52.rest_0_.q, bf16[4,2,384,128]{3,2,1,0:T(8,128)(2,1)S(1)} %in_order.1.ka.va, bf16[4,2,384,128]{3,2,1,0:T(8,128)(2,1)S(1)} %in_order.1.ka.va, ...), custom_call_target="tpu_custom_call" | custom-call | bytes 1000 | tf_op jit(solution)/shard_map/far/pallas_call | solution.py:311
  100.8 2.2 %collective-permute-done.19.o_far = bf16[2,800,128]{2,1,0:T(8,128)(2,1)S(1)} collective-permute-done((bf16[2,800,128]{2,1,0:T(8,128)(2,1)S(1)}, bf16[2,800,128]{2,1,0:T(8,128)(2,1)S(1)}, u32[]{:S(2)}, u32[]{:S(2)}) %collective-permute-start.19) | collective-permute-done | bytes 409632 | tf_op jit(solution)/shard_map/ppermute | solution.py:44
  110.4 2.3 %collective-permute-done.22.refs_7_ = bf16[2,192,128]{2,1,0:T(8,128)(2,1)S(1)} collective-permute-done((bf16[2,192,128]{2,1,0:T(8,128)(2,1)S(1)}, bf16[2,192,128]{2,1,0:T(8,128)(2,1)S(1)}, u32[]{:S(2)}, u32[]{:S(2)}) %collective-permute-start.22) | collective-permute-done | bytes 98336 | tf_op jit(solution)/shard_map/ppermute | solution.py:44
  112.7 1.7 %finish.1 = bf16[192,2560]{1,0:T(8,128)(2,1)} custom-call(s32[9]{0:T(128)S(1)} %copy-done.6, f32[1,2560]{1,0:T(1,128)S(1)} %fusion.4.refs_7_.gate, bf16[3,192,128]{2,1,0:T(8,128)(2,1)S(1)} %get-tuple-element.62.rest_0_.refs_0_, bf16[3,192,128]{2,1,0:T(8,128)(2,1)S(1)} %collective-permute-done.16.refs_1_, ...), custom_call_target="tpu_custom_call" | custom-call | bytes 1000 | tf_op jit(solution)/shard_map/finish/pallas_call | solution.py:372
  (61 shorter events, 26.9 us)
Async XLA Ops:
  4.1 12.4 %collective-permute-start = (bf16[9,192,128]{2,1,0:T(8,128)(2,1)}, bf16[9,192,128]{2,1,0:T(8,128)(2,1)S(1)}, u32[]{:S(2)}, u32[]{:S(2)}) collective-permute-start(bf16[9,192,128]{2,1,0:T(8,128)(2,1)} %get-tuple-element.39), channel_id=1, source_target_pairs={{0,4},{1,5},{2,6},{3,7},{4,0},{5,1},{6,2},{7,3},{8,12},{9,13},{10,... | collective-permute-start | bytes 1327112 | tf_op jit(solution)/shard_map/ppermute | solution.py:44
  5.7 13.3 %collective-permute-start.1 = (bf16[9,192,128]{2,1,0:T(8,128)(2,1)}, bf16[9,192,128]{2,1,0:T(8,128)(2,1)S(1)}, u32[]{:S(2)}, u32[]{:S(2)}) collective-permute-start(bf16[9,192,128]{2,1,0:T(8,128)(2,1)} %get-tuple-element.40), channel_id=1, source_target_pairs={{0,2},{1,3},{2,0},{3,1},{4,6},{5,7},{6,4},{7,5},{8,10},{9,11},{10,... | collective-permute-start | bytes 1327112 | tf_op jit(solution)/shard_map/ppermute | solution.py:44
  7.2 19.9 %collective-permute-start.2 = (bf16[9,192,128]{2,1,0:T(8,128)(2,1)}, bf16[9,192,128]{2,1,0:T(8,128)(2,1)}, u32[]{:S(2)}, u32[]{:S(2)}) collective-permute-start(bf16[9,192,128]{2,1,0:T(8,128)(2,1)} %get-tuple-element.41), channel_id=1, source_target_pairs={{0,6},{1,7},{2,4},{3,5},{4,2},{5,3},{6,0},{7,1},{8,14},{9,15},{10,... | collective-permute-start | bytes 1327112 | tf_op jit(solution)/shard_map/ppermute | solution.py:44
  13.3 13.7 %copy-start.1 = (bf16[9,192,128]{2,1,0:T(8,128)(2,1)S(1)}, bf16[9,192,128]{2,1,0:T(8,128)(2,1)}, u32[]{:S(2)}) copy-start(bf16[9,192,128]{2,1,0:T(8,128)(2,1)} %get-tuple-element.38.rest_0_.refs_0_) | copy-start | bytes 1327108
  28.9 9.1 %collective-permute-start.7 = (bf16[6,2,384,128]{3,2,1,0:T(8,128)(2,1)S(1)}, bf16[6,2,384,128]{3,2,1,0:T(8,128)(2,1)S(1)}, u32[]{:S(2)}, u32[]{:S(2)}) collective-permute-start(bf16[6,2,384,128]{3,2,1,0:T(8,128)(2,1)S(1)} %get-tuple-element.46.ka.va), channel_id=1, source_target_pairs={{0,1},{1,0},{2,3},{3,2},{4,5},{5,4},{6,7},{7,6},{8,9},{9,8},{10,11... | collective-permute-start | bytes 3538952 | tf_op jit(solution)/shard_map/ppermute | solution.py:44
  29.0 30.7 %collective-permute-start.3 = (bf16[6,2,384,128]{3,2,1,0:T(8,128)(2,1)S(1)}, bf16[6,2,384,128]{3,2,1,0:T(8,128)(2,1)S(1)}, u32[]{:S(2)}, u32[]{:S(2)}) collective-permute-start(bf16[6,2,384,128]{3,2,1,0:T(8,128)(2,1)S(1)} %get-tuple-element.46.ka.va), channel_id=1, source_target_pairs={{0,8},{1,9},{2,10},{3,11},{4,12},{5,13},{6,14},{7,15},{8,16},{9,17... | collective-permute-start | bytes 3538952 | tf_op jit(solution)/shard_map/ppermute | solution.py:44
  32.5 18.8 %collective-permute-start.8 = (bf16[3,2,384,128]{3,2,1,0:T(8,128)(2,1)S(1)}, bf16[3,2,384,128]{3,2,1,0:T(8,128)(2,1)S(1)}, u32[]{:S(2)}, u32[]{:S(2)}) collective-permute-start(bf16[3,2,384,128]{3,2,1,0:T(8,128)(2,1)S(1)} %get-tuple-element.45.q.rest_0_), channel_id=1, source_target_pairs={{8,0},{9,1},{10,2},{11,3},{12,4},{13,5},{14,6},{15,7},{16,8},{17,9... | collective-permute-start | bytes 1769480 | tf_op jit(solution)/shard_map/ppermute | solution.py:44
  35.0 9.1 %collective-permute-start.4 = (bf16[6,192,128]{2,1,0:T(8,128)(2,1)S(1)}, bf16[6,192,128]{2,1,0:T(8,128)(2,1)S(1)}, u32[]{:S(2)}, u32[]{:S(2)}) collective-permute-start(bf16[6,192,128]{2,1,0:T(8,128)(2,1)S(1)} %get-tuple-element.48), channel_id=1, source_target_pairs={{0,4},{1,5},{2,6},{3,7},{4,0},{5,1},{6,2},{7,3},{8,12},{9,13},{10,... | collective-permute-start | bytes 884744 | tf_op jit(solution)/shard_map/ppermute | solution.py:44
  36.5 9.9 %collective-permute-start.5 = (bf16[6,192,128]{2,1,0:T(8,128)(2,1)S(1)}, bf16[6,192,128]{2,1,0:T(8,128)(2,1)S(1)}, u32[]{:S(2)}, u32[]{:S(2)}) collective-permute-start(bf16[6,192,128]{2,1,0:T(8,128)(2,1)S(1)} %get-tuple-element.49), channel_id=1, source_target_pairs={{0,2},{1,3},{2,0},{3,1},{4,6},{5,7},{6,4},{7,5},{8,10},{9,11},{10,... | collective-permute-start | bytes 884744 | tf_op jit(solution)/shard_map/ppermute | solution.py:44
  38.0 13.3 %collective-permute-start.6 = (bf16[6,192,128]{2,1,0:T(8,128)(2,1)S(1)}, bf16[6,192,128]{2,1,0:T(8,128)(2,1)S(1)}, u32[]{:S(2)}, u32[]{:S(2)}) collective-permute-start(bf16[6,192,128]{2,1,0:T(8,128)(2,1)S(1)} %get-tuple-element.50), channel_id=1, source_target_pairs={{0,6},{1,7},{2,4},{3,5},{4,2},{5,3},{6,0},{7,1},{8,14},{9,15},{10,... | collective-permute-start | bytes 884744 | tf_op jit(solution)/shard_map/ppermute | solution.py:44
  52.5 23.6 %collective-permute-start.12 = (bf16[4,2,384,128]{3,2,1,0:T(8,128)(2,1)S(1)}, bf16[4,2,384,128]{3,2,1,0:T(8,128)(2,1)S(1)}, u32[]{:S(2)}, u32[]{:S(2)}) collective-permute-start(bf16[4,2,384,128]{3,2,1,0:T(8,128)(2,1)S(1)} %get-tuple-element.58.ka.va), channel_id=1, source_target_pairs={{0,8},{1,9},{2,10},{3,11},{4,12},{5,13},{6,14},{7,15},{8,16},{9,17... | collective-permute-start | bytes 2359304 | tf_op jit(solution)/shard_map/ppermute | solution.py:44
  59.9 2.5 %collective-permute-start.10 = (bf16[3,2,384,128]{3,2,1,0:T(8,128)(2,1)S(1)}, bf16[3,2,384,128]{3,2,1,0:T(8,128)(2,1)S(1)}, u32[]{:S(2)}, u32[]{:S(2)}) collective-permute-start(bf16[3,2,384,128]{3,2,1,0:T(8,128)(2,1)S(1)} %get-tuple-element.54.va), channel_id=1, source_target_pairs={{0,1},{1,0},{2,3},{3,2},{4,5},{5,4},{6,7},{7,6},{8,9},{9,8},{10,11... | collective-permute-start | bytes 1769480 | tf_op jit(solution)/shard_map/ppermute | solution.py:44
  60.0 2.8 %collective-permute-start.9 = (bf16[3,2,384,128]{3,2,1,0:T(8,128)(2,1)S(1)}, bf16[3,2,384,128]{3,2,1,0:T(8,128)(2,1)S(1)}, u32[]{:S(2)}, u32[]{:S(2)}) collective-permute-start(bf16[3,2,384,128]{3,2,1,0:T(8,128)(2,1)S(1)} %get-tuple-element.53.ka), channel_id=1, source_target_pairs={{0,1},{1,0},{2,3},{3,2},{4,5},{5,4},{6,7},{7,6},{8,9},{9,8},{10,11... | collective-permute-start | bytes 1769480 | tf_op jit(solution)/shard_map/ppermute | solution.py:44
  60.5 15.1 %collective-permute-start.13 = (bf16[2,2,384,128]{3,2,1,0:T(8,128)(2,1)S(1)}, bf16[2,2,384,128]{3,2,1,0:T(8,128)(2,1)S(1)}, u32[]{:S(2)}, u32[]{:S(2)}) collective-permute-start(bf16[2,2,384,128]{3,2,1,0:T(8,128)(2,1)S(1)} %get-tuple-element.52.rest_0_.q), channel_id=1, source_target_pairs={{8,0},{9,1},{10,2},{11,3},{12,4},{13,5},{14,6},{15,7},{16,8},{17,9... | collective-permute-start | bytes 1179656 | tf_op jit(solution)/shard_map/ppermute | solution.py:44
  76.1 4.0 %collective-permute-start.14 = (bf16[4,2,384,128]{3,2,1,0:T(8,128)(2,1)S(1)}, bf16[4,2,384,128]{3,2,1,0:T(8,128)(2,1)S(1)}, u32[]{:S(2)}, u32[]{:S(2)}) collective-permute-start(bf16[4,2,384,128]{3,2,1,0:T(8,128)(2,1)S(1)} %in_order.1.ka.va), channel_id=1, source_target_pairs={{0,1},{1,0},{2,3},{3,2},{4,5},{5,4},{6,7},{7,6},{8,9},{9,8},{10,11... | collective-permute-start | bytes 2359304 | tf_op jit(solution)/shard_map/ppermute | solution.py:44
  76.1 11.5 %collective-permute-start.15 = (bf16[4,2,384,128]{3,2,1,0:T(8,128)(2,1)S(1)}, bf16[4,2,384,128]{3,2,1,0:T(8,128)(2,1)S(1)}, u32[]{:S(2)}, u32[]{:S(2)}) collective-permute-start(bf16[4,2,384,128]{3,2,1,0:T(8,128)(2,1)S(1)} %get-tuple-element.58.ka.va), channel_id=1, source_target_pairs={{0,1},{1,0},{2,3},{3,2},{4,5},{5,4},{6,7},{7,6},{8,9},{9,8},{10,11... | collective-permute-start | bytes 2359304 | tf_op jit(solution)/shard_map/ppermute | solution.py:44
  76.6 19.4 %collective-permute-start.11 = (bf16[3,800,128]{2,1,0:T(8,128)(2,1)S(1)}, bf16[3,800,128]{2,1,0:T(8,128)(2,1)S(1)}, u32[]{:S(2)}, u32[]{:S(2)}) collective-permute-start(bf16[3,800,128]{2,1,0:T(8,128)(2,1)S(1)} %remote.2.rest_0_), channel_id=1, source_target_pairs={{0,8},{1,9},{2,10},{3,11},{4,12},{5,13},{6,14},{7,15},{8,16},{9,17... | collective-permute-start | bytes 1843208 | tf_op jit(solution)/shard_map/ppermute | solution.py:44
  83.9 19.1 %collective-permute-start.19 = (bf16[2,800,128]{2,1,0:T(8,128)(2,1)S(1)}, bf16[2,800,128]{2,1,0:T(8,128)(2,1)S(1)}, u32[]{:S(2)}, u32[]{:S(2)}) collective-permute-start(bf16[2,800,128]{2,1,0:T(8,128)(2,1)S(1)} %remote.3.rest_0_), channel_id=1, source_target_pairs={{0,8},{1,9},{2,10},{3,11},{4,12},{5,13},{6,14},{7,15},{8,16},{9,17... | collective-permute-start | bytes 1228808 | tf_op jit(solution)/shard_map/ppermute | solution.py:44
  97.3 9.9 %collective-permute-start.16 = (bf16[3,192,128]{2,1,0:T(8,128)(2,1)S(1)}, bf16[3,192,128]{2,1,0:T(8,128)(2,1)S(1)}, u32[]{:S(2)}, u32[]{:S(2)}) collective-permute-start(bf16[3,192,128]{2,1,0:T(8,128)(2,1)S(1)} %get-tuple-element.63), channel_id=1, source_target_pairs={{0,4},{1,5},{2,6},{3,7},{4,0},{5,1},{6,2},{7,3},{8,12},{9,13},{10,... | collective-permute-start | bytes 442376 | tf_op jit(solution)/shard_map/ppermute | solution.py:44
  98.9 8.8 %collective-permute-start.17 = (bf16[3,192,128]{2,1,0:T(8,128)(2,1)S(1)}, bf16[3,192,128]{2,1,0:T(8,128)(2,1)S(1)}, u32[]{:S(2)}, u32[]{:S(2)}) collective-permute-start(bf16[3,192,128]{2,1,0:T(8,128)(2,1)S(1)} %get-tuple-element.64), channel_id=1, source_target_pairs={{0,2},{1,3},{2,0},{3,1},{4,6},{5,7},{6,4},{7,5},{8,10},{9,11},{10,... | collective-permute-start | bytes 442376 | tf_op jit(solution)/shard_map/ppermute | solution.py:44
  100.4 7.3 %collective-permute-start.18 = (bf16[3,192,128]{2,1,0:T(8,128)(2,1)S(1)}, bf16[3,192,128]{2,1,0:T(8,128)(2,1)S(1)}, u32[]{:S(2)}, u32[]{:S(2)}) collective-permute-start(bf16[3,192,128]{2,1,0:T(8,128)(2,1)S(1)} %get-tuple-element.65), channel_id=1, source_target_pairs={{0,6},{1,7},{2,4},{3,5},{4,2},{5,3},{6,0},{7,1},{8,14},{9,15},{10,... | collective-permute-start | bytes 442376 | tf_op jit(solution)/shard_map/ppermute | solution.py:44
  104.1 5.2 %collective-permute-start.20 = (bf16[2,192,128]{2,1,0:T(8,128)(2,1)S(1)}, bf16[2,192,128]{2,1,0:T(8,128)(2,1)S(1)}, u32[]{:S(2)}, u32[]{:S(2)}) collective-permute-start(bf16[2,192,128]{2,1,0:T(8,128)(2,1)S(1)} %get-tuple-element.68), channel_id=1, source_target_pairs={{0,4},{1,5},{2,6},{3,7},{4,0},{5,1},{6,2},{7,3},{8,12},{9,13},{10,... | collective-permute-start | bytes 294920 | tf_op jit(solution)/shard_map/ppermute | solution.py:44
  105.7 4.7 %collective-permute-start.21 = (bf16[2,192,128]{2,1,0:T(8,128)(2,1)S(1)}, bf16[2,192,128]{2,1,0:T(8,128)(2,1)S(1)}, u32[]{:S(2)}, u32[]{:S(2)}) collective-permute-start(bf16[2,192,128]{2,1,0:T(8,128)(2,1)S(1)} %get-tuple-element.69), channel_id=1, source_target_pairs={{0,2},{1,3},{2,0},{3,1},{4,6},{5,7},{6,4},{7,5},{8,10},{9,11},{10,... | collective-permute-start | bytes 294920 | tf_op jit(solution)/shard_map/ppermute | solution.py:44
  107.2 5.5 %collective-permute-start.22 = (bf16[2,192,128]{2,1,0:T(8,128)(2,1)S(1)}, bf16[2,192,128]{2,1,0:T(8,128)(2,1)S(1)}, u32[]{:S(2)}, u32[]{:S(2)}) collective-permute-start(bf16[2,192,128]{2,1,0:T(8,128)(2,1)S(1)} %get-tuple-element.70), channel_id=1, source_target_pairs={{0,6},{1,7},{2,4},{3,5},{4,2},{5,3},{6,0},{7,1},{8,14},{9,15},{10,... | collective-permute-start | bytes 294920 | tf_op jit(solution)/shard_map/ppermute | solution.py:44
  (8 other events, 96.0 us)

commit v7 on v6

--- a/solution.py
+++ b/solution.py
@@ -79,28 +79,30 @@
     )
 
 
-def pack_kernel(first, heads, group_width, count, meta, q, k, v, *rest):
+def pack_kernel(first, heads, group_width, count, q, k, v, *rest):
     outs = rest[count:]
-    for j in range(4):
+    x, y = lax.axis_index("seq") // 2, lax.axis_index("span") % 2
+    for j, (dx, dy) in enumerate(PLACES):
+        group = 2 * (x ^ dx) + (y ^ dy)
         for t, ref in enumerate((q, k, v)):
             for h in range(heads):
-                column = meta[j] * group_width + (first + h) * HEAD_DIM
+                column = group * group_width + (first + h) * HEAD_DIM
                 at = pl.ds(pl.multiple_of(column, HEAD_DIM), HEAD_DIM)
                 outs[j][t * heads + h] = ref[:, at]
 
 
-def pack(meta, q, k, v, first, heads, group_width, after):
+def pack(q, k, v, first, heads, group_width, after):
     rows = q.shape[0]
     whole = pl.BlockSpec(memory_space=pltpu.VMEM)
     return pl.pallas_call(
         functools.partial(pack_kernel, first, heads, group_width, len(after)),
         out_shape=[jax.ShapeDtypeStruct((3 * heads, rows, HEAD_DIM), q.dtype)] * 4,
-        in_specs=[SMEM, whole, whole, whole] + [ANY] * len(after),
+        in_specs=[whole, whole, whole] + [ANY] * len(after),
         out_specs=[whole] * 4,
         compiler_params=params(60),
         cost_estimate=estimate(0),
         name="pack",
-    )(meta, q, k, v, *after)
+    )(q, k, v, *after)
 
 
 def stack_kernel(heads, count, meta, *refs):
@@ -356,28 +358,39 @@
     )(meta, o, lse, o_far, *after)
 
 
-def finish_kernel(firsts, group_width, meta, gate, *refs):
-    pieces, out = refs[:-1], refs[-1]
-    for i, piece in enumerate(pieces):
-        chunk, j = divmod(i, 4)
+def finish_kernel(first, group_width, count, meta, gate, *refs):
+    pieces, (out, rows, sems) = refs[:4], refs[4 + count :]
+    copies = []
+    for j, piece in enumerate(pieces):
         for h in range(piece.shape[0]):
-            column = meta[j] * group_width + (firsts[chunk] + h) * HEAD_DIM
+            column = meta[j] * group_width + (first + h) * HEAD_DIM
             at = pl.ds(pl.multiple_of(column, HEAD_DIM), HEAD_DIM)
-            out[:, at] = (gate[:, at] * piece[h].astype(jnp.float32)).astype(out.dtype)
-
-
-def finish(meta, gate, pieces, firsts, group_width, cost=0):
-    rows = pieces[0].shape[1]
+            rows[j, h] = (gate[:, at] * piece[h].astype(jnp.float32)).astype(rows.dtype)
+            copy = pltpu.make_async_copy(rows.at[j, h], out.at[:, at], sems.at[j, h])
+            copy.start()
+            copies.append(copy)
+    for copy in copies:
+        copy.wait()
+
+
+def finish(meta, gate, pieces, first, group_width, base):
+    heads, rows, _ = pieces[0].shape
     whole = pl.BlockSpec(memory_space=pltpu.VMEM)
-    return pl.pallas_call(
-        functools.partial(finish_kernel, firsts, group_width),
+    base = [] if base is None else [base]
+    return pl.pallas_call(
+        functools.partial(finish_kernel, first, group_width, len(base)),
         out_shape=jax.ShapeDtypeStruct((rows, 4 * group_width), jnp.bfloat16),
-        in_specs=[SMEM] + [whole] * (1 + len(pieces)),
-        out_specs=whole,
+        in_specs=[SMEM] + [whole] * 5 + [ANY] * len(base),
+        out_specs=ANY,
+        scratch_shapes=[
+            pltpu.VMEM((4, heads, rows, HEAD_DIM), jnp.bfloat16),
+            pltpu.SemaphoreType.DMA((4, heads)),
+        ],
+        input_output_aliases={6: 0} if base else {},
         compiler_params=params(16),
-        cost_estimate=estimate(cost),
+        cost_estimate=estimate(0),
         name="finish",
-    )(meta, gate, *pieces)
+    )(meta, gate, *pieces, *base)
 
 
 def chunk_sizes(heads):
@@ -407,7 +420,7 @@
 
     sent, packed = [], []
     for first, size in zip(firsts, sizes):
-        sent.append(pack(meta, queries, keys, values, first, size, group_width, packed))
+        sent.append(pack(queries, keys, values, first, size, group_width, packed))
         packed = [sent[-1][0]]
     last = [gate]
 
@@ -463,7 +476,10 @@
         extra = [kinds[e[0]][int(e[1])] for e in extra]
         extra = [block for e in extra for block in (e[1:] if isinstance(e, list) else [e])]
         last = steps[name[0]](int(name[1]), last + extra, COSTS.get(name, 0))
-    return finish(meta, gate, sum((results[i] for i in chunks), []), firsts, group_width)
+    out = None
+    for i, first in enumerate(firsts):
+        out = finish(meta, gate, results[i], first, group_width, out)
+    return out
 
 
 def solution(mesh):

time: 115 us -> 114 us (level)
  waiting for transfers between devices: 31.9 us -> 30.3 us
    ppermute x23, waiting for transfers between devices: 31.9 us -> 30.3 us  [move(): return lax.ppermute(block, AXES, route)]
    pallas_call x1 -> x2, Pallas kernels: 1.68 us -> 2.81 us  [finish(): pl.pallas_call(functools.partial(finish_kernel, first, group_width, len(b...]
  transfers between devices with their start and end apart: 23 -> 23, of which waited for: 13 -> 13; matrix products, arithmetic and copies ran while one was open for 3% -> 3% of each run, Pallas kernels for 32% -> 34%
where the time goes in v7:
time: 114 us
  Pallas kernels  45 us (39%)
  starting transfers between devices  33.7 us (30%)
  waiting for transfers between devices  30.3 us (27%)
  other arithmetic  2.08 us (2%)
  matrix products  1.34 us (1%)
    ppermute x23, starting transfers between devices, move(): return lax.ppermute(block, AXES, route)  33.7 us
    ppermute x23, waiting for transfers between devices, move(): return lax.ppermute(block, AXES, route)  30.3 us
    pallas_call x6, Pallas kernels, attend(): pl.pallas_call(functools.partial(body, len(after)), grid=(heads,), out_sh...  30.1 us
    pallas_call x2, Pallas kernels, pack(): pl.pallas_call(functools.partial(pack_kernel, first, heads, group_width,...  6.51 us
    pallas_call x2, Pallas kernels, stack(): pl.pallas_call(functools.partial(stack_kernel, heads, len(later) + len(af...  3.03 us
    pallas_call x2, Pallas kernels, finish(): pl.pallas_call(functools.partial(finish_kernel, first, group_width, len(b...  2.81 us
  transfers between devices with their start and end apart: 23, of which 13 were waited for; matrix products, arithmetic and copies ran while one was open for 3% of the time, Pallas kernels for 34%

profile of v7, /device:TPU:8, one launch (start us, length us, event | category | flops | bytes accessed | tf_op | source)
XLA Modules:
  0.0 113.5 jit_solution(13876282243843005862)
XLA Ops:
  0.0 3.5 %pack.2 = (bf16[9,192,128]{2,1,0:T(8,128)(2,1)}, bf16[9,192,128]{2,1,0:T(8,128)(2,1)}, bf16[9,192,128]{2,1,0:T(8,128)(2,1)}, bf16[9,192,128]{2,1,0:T(8,128)(2,1)}) custom-call(bf16[192,2560]{1,0:T(8,128)(2,1)} %q.3, bf16[192,2560]{1,0:T(8,128)(2,1)} %k.3, bf16[192,2560]{1,0:T(8,128)(2,1)} %v.3), custom_call_target="tpu_custom_call" | custom-call | bytes 1000 | tf_op jit(solution)/shard_map/pack/pallas_call | solution.py:97
  9.7 3.0 %pack.3 = (bf16[6,192,128]{2,1,0:T(8,128)(2,1)}, bf16[6,192,128]{2,1,0:T(8,128)(2,1)}, bf16[6,192,128]{2,1,0:T(8,128)(2,1)}, bf16[6,192,128]{2,1,0:T(8,128)(2,1)}) custom-call(bf16[192,2560]{1,0:T(8,128)(2,1)} %q.3, bf16[192,2560]{1,0:T(8,128)(2,1)} %k.3, bf16[192,2560]{1,0:T(8,128)(2,1)} %v.3, bf16[9,192,128]{2,1,0:T(8,128)(2,1)} %get-tuple-element.38.rest_0_.refs_0_), custom_call_target="tpu_custom_call" | custom-call | bytes 1000 | tf_op jit(solution)/shard_map/pack/pallas_call | solution.py:97
  14.2 1.7 %collective-permute-done.refs_1_ = bf16[9,192,128]{2,1,0:T(8,128)(2,1)S(1)} collective-permute-done((bf16[9,192,128]{2,1,0:T(8,128)(2,1)}, bf16[9,192,128]{2,1,0:T(8,128)(2,1)S(1)}, u32[]{:S(2)}, u32[]{:S(2)}) %collective-permute-start) | collective-permute-done | bytes 442400 | tf_op jit(solution)/shard_map/ppermute | solution.py:44
  15.9 2.4 %collective-permute-done.1.refs_2_ = bf16[9,192,128]{2,1,0:T(8,128)(2,1)S(1)} collective-permute-done((bf16[9,192,128]{2,1,0:T(8,128)(2,1)}, bf16[9,192,128]{2,1,0:T(8,128)(2,1)S(1)}, u32[]{:S(2)}, u32[]{:S(2)}) %collective-permute-start.1) | collective-permute-done | bytes 442400 | tf_op jit(solution)/shard_map/ppermute | solution.py:44
  18.3 8.1 %collective-permute-done.2.refs_3_ = bf16[9,192,128]{2,1,0:T(8,128)(2,1)} collective-permute-done((bf16[9,192,128]{2,1,0:T(8,128)(2,1)}, bf16[9,192,128]{2,1,0:T(8,128)(2,1)}, u32[]{:S(2)}, u32[]{:S(2)}) %collective-permute-start.2) | collective-permute-done | bytes 442400 | tf_op jit(solution)/shard_map/ppermute | solution.py:44
  26.4 1.9 %stack.36 = (bf16[3,2,384,128]{3,2,1,0:T(8,128)(2,1)S(1)}, bf16[6,2,384,128]{3,2,1,0:T(8,128)(2,1)S(1)}, bf16[6,192,128]{2,1,0:T(8,128)(2,1)S(1)}, bf16[6,192,12...) custom-call(s32[9]{0:T(128)S(1)} %stack.35.meta, ...), custom_call_target="tpu_custom_call", output_to_operand_aliasing={{2}: (5, {}), {3}: (6, {}), {4}: (7, {})} | custom-call | bytes 1000 | tf_op jit(solution)/shard_map/stack/pallas_call | solution.py:133
  28.4 3.5 %collective-permute-start.9 = (bf16[6,2,384,128]{3,2,1,0:T(8,128)(2,1)S(1)}, bf16[6,2,384,128]{3,2,1,0:T(8,128)(2,1)S(1)}, u32[]{:S(2)}, u32[]{:S(2)}) collective-permute-start(bf16[6,2,384,128]{3,2,1,0:T(8,128)(2,1)S(1)} %get-tuple-element.50.ka.va), channel_id=1, source_target_pairs={{0,8},{1,9},{2,10},{3,11},{4,12},{5,13},{6,14},{7,15},{8,16},{9,17... | collective-permute-start | bytes 3538952 | tf_op jit(solution)/shard_map/ppermute | solution.py:44
  31.9 2.4 %collective-permute-start.7 = (bf16[3,2,384,128]{3,2,1,0:T(8,128)(2,1)S(1)}, bf16[3,2,384,128]{3,2,1,0:T(8,128)(2,1)S(1)}, u32[]{:S(2)}, u32[]{:S(2)}) collective-permute-start(bf16[3,2,384,128]{3,2,1,0:T(8,128)(2,1)S(1)} %get-tuple-element.49.q.rest_0_), channel_id=1, source_target_pairs={{8,0},{9,1},{10,2},{11,3},{12,4},{13,5},{14,6},{15,7},{16,8},{17,9... | collective-permute-start | bytes 1769480 | tf_op jit(solution)/shard_map/ppermute | solution.py:44
  34.3 1.6 %collective-permute-start.3 = (bf16[6,192,128]{2,1,0:T(8,128)(2,1)S(1)}, bf16[6,192,128]{2,1,0:T(8,128)(2,1)S(1)}, u32[]{:S(2)}, u32[]{:S(2)}) collective-permute-start(bf16[6,192,128]{2,1,0:T(8,128)(2,1)S(1)} %get-tuple-element.46), channel_id=1, source_target_pairs={{0,4},{1,5},{2,6},{3,7},{4,0},{5,1},{6,2},{7,3},{8,12},{9,13},{10,... | collective-permute-start | bytes 884744 | tf_op jit(solution)/shard_map/ppermute | solution.py:44
  37.9 5.2 %near.2 = (f32[3,768,128]{2,1,0:T(8,128)S(1)}, f32[3,8,128]{2,1,0:T(8,128)S(1)}) custom-call(bf16[3,2,384,128]{3,2,1,0:T(8,128)(2,1)S(1)} %get-tuple-element.49.q.rest_0_, bf16[6,2,384,128]{3,2,1,0:T(8,128)(2,1)S(1)} %get-tuple-element.50.ka.va, bf16[6,2,384,128]{3,2,1,0:T(8,128)(2,1)S(1)} %get-tuple-element.50.ka.va, ...), custom_call_target="tpu_custom_call" | custom-call | bytes 1000 | tf_op jit(solution)/shard_map/near/pallas_call | solution.py:313
  43.4 2.4 %collective-permute-done.4.refs_2_ = bf16[6,192,128]{2,1,0:T(8,128)(2,1)S(1)} collective-permute-done((bf16[6,192,128]{2,1,0:T(8,128)(2,1)S(1)}, bf16[6,192,128]{2,1,0:T(8,128)(2,1)S(1)}, u32[]{:S(2)}, u32[]{:S(2)}) %collective-permute-start.4) | collective-permute-done | bytes 294944 | tf_op jit(solution)/shard_map/ppermute | solution.py:44
  45.8 4.9 %collective-permute-done.5.refs_3_ = bf16[6,192,128]{2,1,0:T(8,128)(2,1)S(1)} collective-permute-done((bf16[6,192,128]{2,1,0:T(8,128)(2,1)S(1)}, bf16[6,192,128]{2,1,0:T(8,128)(2,1)S(1)}, u32[]{:S(2)}, u32[]{:S(2)}) %collective-permute-start.5) | collective-permute-done | bytes 294944 | tf_op jit(solution)/shard_map/ppermute | solution.py:44
  51.9 3.4 %collective-permute-start.8 = (bf16[4,2,384,128]{3,2,1,0:T(8,128)(2,1)S(1)}, bf16[4,2,384,128]{3,2,1,0:T(8,128)(2,1)S(1)}, u32[]{:S(2)}, u32[]{:S(2)}) collective-permute-start(bf16[4,2,384,128]{3,2,1,0:T(8,128)(2,1)S(1)} %get-tuple-element.53.ka.va), channel_id=1, source_target_pairs={{0,8},{1,9},{2,10},{3,11},{4,12},{5,13},{6,14},{7,15},{8,16},{9,17... | collective-permute-start | bytes 2359304 | tf_op jit(solution)/shard_map/ppermute | solution.py:44
  55.3 3.7 %collective-permute-done.9.kv = bf16[6,2,384,128]{3,2,1,0:T(8,128)(2,1)S(1)} collective-permute-done((bf16[6,2,384,128]{3,2,1,0:T(8,128)(2,1)S(1)}, bf16[6,2,384,128]{3,2,1,0:T(8,128)(2,1)S(1)}, u32[]{:S(2)}, u32[]{:S(2)}) %collective-permute-start.9) | collective-permute-done | bytes 1179680 | tf_op jit(solution)/shard_map/ppermute | solution.py:44
  59.9 1.9 %collective-permute-start.12 = (bf16[2,2,384,128]{3,2,1,0:T(8,128)(2,1)S(1)}, bf16[2,2,384,128]{3,2,1,0:T(8,128)(2,1)S(1)}, u32[]{:S(2)}, u32[]{:S(2)}) collective-permute-start(bf16[2,2,384,128]{3,2,1,0:T(8,128)(2,1)S(1)} %get-tuple-element.52.rest_0_.q), channel_id=1, source_target_pairs={{8,0},{9,1},{10,2},{11,3},{12,4},{13,5},{14,6},{15,7},{16,8},{17,9... | collective-permute-start | bytes 1179656 | tf_op jit(solution)/shard_map/ppermute | solution.py:44
  62.2 5.6 %remote.2.rest_0_ = bf16[3,800,128]{2,1,0:T(8,128)(2,1)S(1)} custom-call(bf16[3,2,384,128]{3,2,1,0:T(8,128)(2,1)S(1)} %collective-permute-done.7.refs_5_.q, bf16[3,2,384,128]{3,2,1,0:T(8,128)(2,1)S(1)} %get-tuple-element.54.ka, bf16[3,2,384,128]{3,2,1,0:T(8,128)(2,1)S(1)} %get-tuple-element.55.va, bf16[3,2,384,128]{3,2,1,0:T(8,128)(2,1)S(1)} %collective-permute-done.10.kb, ...), custom_call_target="tpu_custom_call" | custom-call | bytes 1000 | tf_op jit(solution)/shard_map/remote/pallas_call | solution.py:313
  67.9 7.1 %far.2 = (f32[3,768,128]{2,1,0:T(8,128)S(1)}, f32[3,8,128]{2,1,0:T(8,128)S(1)}) custom-call(s32[9]{0:T(128)S(1)} %stack.35.meta, bf16[3,2,384,128]{3,2,1,0:T(8,128)(2,1)S(1)} %get-tuple-element.49.q.rest_0_, bf16[3,2,384,128]{3,2,1,0:T(8,128)(2,1)S(1)} %get-tuple-element.54.ka, bf16[3,2,384,128]{3,2,1,0:T(8,128)(2,1)S(1)} %get-tuple-element.55.va, ...), custom_call_target="tpu_custom_call" | custom-call | bytes 1000 | tf_op jit(solution)/shard_map/far/pallas_call | solution.py:313
  76.0 3.5 %collective-permute-start.16 = (bf16[3,800,128]{2,1,0:T(8,128)(2,1)S(1)}, bf16[3,800,128]{2,1,0:T(8,128)(2,1)S(1)}, u32[]{:S(2)}, u32[]{:S(2)}) collective-permute-start(bf16[3,800,128]{2,1,0:T(8,128)(2,1)S(1)} %remote.2.rest_0_), channel_id=1, source_target_pairs={{0,8},{1,9},{2,10},{3,11},{4,12},{5,13},{6,14},{7,15},{8,16},{9,17... | collective-permute-start | bytes 1843208 | tf_op jit(solution)/shard_map/ppermute | solution.py:44
  79.5 3.8 %remote.3.rest_0_ = bf16[2,800,128]{2,1,0:T(8,128)(2,1)S(1)} custom-call(bf16[2,2,384,128]{3,2,1,0:T(8,128)(2,1)S(1)} %collective-permute-done.12.refs_2_.q, bf16[4,2,384,128]{3,2,1,0:T(8,128)(2,1)S(1)} %in_order.1.ka.va, bf16[4,2,384,128]{3,2,1,0:T(8,128)(2,1)S(1)} %in_order.1.ka.va, bf16[4,2,384,128]{3,2,1,0:T(8,128)(2,1)S(1)} %collective-permute-done.13.kb.vb, ...), custom_call_target="tpu_custom_call" | custom-call | bytes 1000 | tf_op jit(solution)/shard_map/remote/pallas_call | solution.py:313
  83.3 3.7 %collective-permute-start.15 = (bf16[2,800,128]{2,1,0:T(8,128)(2,1)S(1)}, bf16[2,800,128]{2,1,0:T(8,128)(2,1)S(1)}, u32[]{:S(2)}, u32[]{:S(2)}) collective-permute-start(bf16[2,800,128]{2,1,0:T(8,128)(2,1)S(1)} %remote.3.rest_0_), channel_id=1, source_target_pairs={{0,8},{1,9},{2,10},{3,11},{4,12},{5,13},{6,14},{7,15},{8,16},{9,17... | collective-permute-start | bytes 1228808 | tf_op jit(solution)/shard_map/ppermute | solution.py:44
  87.0 3.5 %near.3 = (f32[2,768,128]{2,1,0:T(8,128)S(1)}, f32[2,8,128]{2,1,0:T(8,128)S(1)}) custom-call(bf16[2,2,384,128]{3,2,1,0:T(8,128)(2,1)S(1)} %get-tuple-element.52.rest_0_.q, bf16[4,2,384,128]{3,2,1,0:T(8,128)(2,1)S(1)} %get-tuple-element.53.ka.va, bf16[4,2,384,128]{3,2,1,0:T(8,128)(2,1)S(1)} %get-tuple-element.53.ka.va, ...), custom_call_target="tpu_custom_call" | custom-call | bytes 1000 | tf_op jit(solution)/shard_map/near/pallas_call | solution.py:313
  90.5 4.9 %far.3 = (f32[2,768,128]{2,1,0:T(8,128)S(1)}, f32[2,8,128]{2,1,0:T(8,128)S(1)}) custom-call(s32[9]{0:T(128)S(1)} %stack.35.meta, bf16[2,2,384,128]{3,2,1,0:T(8,128)(2,1)S(1)} %get-tuple-element.52.rest_0_.q, bf16[4,2,384,128]{3,2,1,0:T(8,128)(2,1)S(1)} %in_order.1.ka.va, bf16[4,2,384,128]{3,2,1,0:T(8,128)(2,1)S(1)} %in_order.1.ka.va, ...), custom_call_target="tpu_custom_call" | custom-call | bytes 1000 | tf_op jit(solution)/shard_map/far/pallas_call | solution.py:313
  100.2 2.2 %collective-permute-done.15.o_far = bf16[2,800,128]{2,1,0:T(8,128)(2,1)S(1)} collective-permute-done((bf16[2,800,128]{2,1,0:T(8,128)(2,1)S(1)}, bf16[2,800,128]{2,1,0:T(8,128)(2,1)S(1)}, u32[]{:S(2)}, u32[]{:S(2)}) %collective-permute-start.15) | collective-permute-done | bytes 409632 | tf_op jit(solution)/shard_map/ppermute | solution.py:44
  109.7 2.3 %collective-permute-done.19.refs_3_ = bf16[2,192,128]{2,1,0:T(8,128)(2,1)S(1)} collective-permute-done((bf16[2,192,128]{2,1,0:T(8,128)(2,1)S(1)}, bf16[2,192,128]{2,1,0:T(8,128)(2,1)S(1)}, u32[]{:S(2)}, u32[]{:S(2)}) %collective-permute-start.19) | collective-permute-done | bytes 98336 | tf_op jit(solution)/shard_map/ppermute | solution.py:44
  (60 shorter events, 26.2 us)
Async XLA Ops:
  3.5 12.4 %collective-permute-start = (bf16[9,192,128]{2,1,0:T(8,128)(2,1)}, bf16[9,192,128]{2,1,0:T(8,128)(2,1)S(1)}, u32[]{:S(2)}, u32[]{:S(2)}) collective-permute-start(bf16[9,192,128]{2,1,0:T(8,128)(2,1)} %get-tuple-element.40), channel_id=1, source_target_pairs={{0,4},{1,5},{2,6},{3,7},{4,0},{5,1},{6,2},{7,3},{8,12},{9,13},{10,... | collective-permute-start | bytes 1327112 | tf_op jit(solution)/shard_map/ppermute | solution.py:44
  5.0 13.3 %collective-permute-start.1 = (bf16[9,192,128]{2,1,0:T(8,128)(2,1)}, bf16[9,192,128]{2,1,0:T(8,128)(2,1)S(1)}, u32[]{:S(2)}, u32[]{:S(2)}) collective-permute-start(bf16[9,192,128]{2,1,0:T(8,128)(2,1)} %get-tuple-element.41), channel_id=1, source_target_pairs={{0,2},{1,3},{2,0},{3,1},{4,6},{5,7},{6,4},{7,5},{8,10},{9,11},{10,... | collective-permute-start | bytes 1327112 | tf_op jit(solution)/shard_map/ppermute | solution.py:44
  6.5 19.9 %collective-permute-start.2 = (bf16[9,192,128]{2,1,0:T(8,128)(2,1)}, bf16[9,192,128]{2,1,0:T(8,128)(2,1)}, u32[]{:S(2)}, u32[]{:S(2)}) collective-permute-start(bf16[9,192,128]{2,1,0:T(8,128)(2,1)} %get-tuple-element.42), channel_id=1, source_target_pairs={{0,6},{1,7},{2,4},{3,5},{4,2},{5,3},{6,0},{7,1},{8,14},{9,15},{10,... | collective-permute-start | bytes 1327112 | tf_op jit(solution)/shard_map/ppermute | solution.py:44
  12.8 13.6 %copy-start.1 = (bf16[9,192,128]{2,1,0:T(8,128)(2,1)S(1)}, bf16[9,192,128]{2,1,0:T(8,128)(2,1)}, u32[]{:S(2)}) copy-start(bf16[9,192,128]{2,1,0:T(8,128)(2,1)} %get-tuple-element.38.rest_0_.refs_0_) | copy-start | bytes 1327108
  28.3 9.1 %collective-permute-start.6 = (bf16[6,2,384,128]{3,2,1,0:T(8,128)(2,1)S(1)}, bf16[6,2,384,128]{3,2,1,0:T(8,128)(2,1)S(1)}, u32[]{:S(2)}, u32[]{:S(2)}) collective-permute-start(bf16[6,2,384,128]{3,2,1,0:T(8,128)(2,1)S(1)} %get-tuple-element.50.ka.va), channel_id=1, source_target_pairs={{0,1},{1,0},{2,3},{3,2},{4,5},{5,4},{6,7},{7,6},{8,9},{9,8},{10,11... | collective-permute-start | bytes 3538952 | tf_op jit(solution)/shard_map/ppermute | solution.py:44
  28.4 30.7 %collective-permute-start.9 = (bf16[6,2,384,128]{3,2,1,0:T(8,128)(2,1)S(1)}, bf16[6,2,384,128]{3,2,1,0:T(8,128)(2,1)S(1)}, u32[]{:S(2)}, u32[]{:S(2)}) collective-permute-start(bf16[6,2,384,128]{3,2,1,0:T(8,128)(2,1)S(1)} %get-tuple-element.50.ka.va), channel_id=1, source_target_pairs={{0,8},{1,9},{2,10},{3,11},{4,12},{5,13},{6,14},{7,15},{8,16},{9,17... | collective-permute-start | bytes 3538952 | tf_op jit(solution)/shard_map/ppermute | solution.py:44
  31.9 18.8 %collective-permute-start.7 = (bf16[3,2,384,128]{3,2,1,0:T(8,128)(2,1)S(1)}, bf16[3,2,384,128]{3,2,1,0:T(8,128)(2,1)S(1)}, u32[]{:S(2)}, u32[]{:S(2)}) collective-permute-start(bf16[3,2,384,128]{3,2,1,0:T(8,128)(2,1)S(1)} %get-tuple-element.49.q.rest_0_), channel_id=1, source_target_pairs={{8,0},{9,1},{10,2},{11,3},{12,4},{13,5},{14,6},{15,7},{16,8},{17,9... | collective-permute-start | bytes 1769480 | tf_op jit(solution)/shard_map/ppermute | solution.py:44
  34.3 9.1 %collective-permute-start.3 = (bf16[6,192,128]{2,1,0:T(8,128)(2,1)S(1)}, bf16[6,192,128]{2,1,0:T(8,128)(2,1)S(1)}, u32[]{:S(2)}, u32[]{:S(2)}) collective-permute-start(bf16[6,192,128]{2,1,0:T(8,128)(2,1)S(1)} %get-tuple-element.46), channel_id=1, source_target_pairs={{0,4},{1,5},{2,6},{3,7},{4,0},{5,1},{6,2},{7,3},{8,12},{9,13},{10,... | collective-permute-start | bytes 884744 | tf_op jit(solution)/shard_map/ppermute | solution.py:44
  35.9 9.9 %collective-permute-start.4 = (bf16[6,192,128]{2,1,0:T(8,128)(2,1)S(1)}, bf16[6,192,128]{2,1,0:T(8,128)(2,1)S(1)}, u32[]{:S(2)}, u32[]{:S(2)}) collective-permute-start(bf16[6,192,128]{2,1,0:T(8,128)(2,1)S(1)} %get-tuple-element.47), channel_id=1, source_target_pairs={{0,2},{1,3},{2,0},{3,1},{4,6},{5,7},{6,4},{7,5},{8,10},{9,11},{10,... | collective-permute-start | bytes 884744 | tf_op jit(solution)/shard_map/ppermute | solution.py:44
  37.4 13.3 %collective-permute-start.5 = (bf16[6,192,128]{2,1,0:T(8,128)(2,1)S(1)}, bf16[6,192,128]{2,1,0:T(8,128)(2,1)S(1)}, u32[]{:S(2)}, u32[]{:S(2)}) collective-permute-start(bf16[6,192,128]{2,1,0:T(8,128)(2,1)S(1)} %get-tuple-element.48), channel_id=1, source_target_pairs={{0,6},{1,7},{2,4},{3,5},{4,2},{5,3},{6,0},{7,1},{8,14},{9,15},{10,... | collective-permute-start | bytes 884744 | tf_op jit(solution)/shard_map/ppermute | solution.py:44
  51.9 23.6 %collective-permute-start.8 = (bf16[4,2,384,128]{3,2,1,0:T(8,128)(2,1)S(1)}, bf16[4,2,384,128]{3,2,1,0:T(8,128)(2,1)S(1)}, u32[]{:S(2)}, u32[]{:S(2)}) collective-permute-start(bf16[4,2,384,128]{3,2,1,0:T(8,128)(2,1)S(1)} %get-tuple-element.53.ka.va), channel_id=1, source_target_pairs={{0,8},{1,9},{2,10},{3,11},{4,12},{5,13},{6,14},{7,15},{8,16},{9,17... | collective-permute-start | bytes 2359304 | tf_op jit(solution)/shard_map/ppermute | solution.py:44
  59.3 2.5 %collective-permute-start.10 = (bf16[3,2,384,128]{3,2,1,0:T(8,128)(2,1)S(1)}, bf16[3,2,384,128]{3,2,1,0:T(8,128)(2,1)S(1)}, u32[]{:S(2)}, u32[]{:S(2)}) collective-permute-start(bf16[3,2,384,128]{3,2,1,0:T(8,128)(2,1)S(1)} %get-tuple-element.54.ka), channel_id=1, source_target_pairs={{0,1},{1,0},{2,3},{3,2},{4,5},{5,4},{6,7},{7,6},{8,9},{9,8},{10,11... | collective-permute-start | bytes 1769480 | tf_op jit(solution)/shard_map/ppermute | solution.py:44
  59.4 2.8 %collective-permute-start.11 = (bf16[3,2,384,128]{3,2,1,0:T(8,128)(2,1)S(1)}, bf16[3,2,384,128]{3,2,1,0:T(8,128)(2,1)S(1)}, u32[]{:S(2)}, u32[]{:S(2)}) collective-permute-start(bf16[3,2,384,128]{3,2,1,0:T(8,128)(2,1)S(1)} %get-tuple-element.55.va), channel_id=1, source_target_pairs={{0,1},{1,0},{2,3},{3,2},{4,5},{5,4},{6,7},{7,6},{8,9},{9,8},{10,11... | collective-permute-start | bytes 1769480 | tf_op jit(solution)/shard_map/ppermute | solution.py:44
  59.9 15.1 %collective-permute-start.12 = (bf16[2,2,384,128]{3,2,1,0:T(8,128)(2,1)S(1)}, bf16[2,2,384,128]{3,2,1,0:T(8,128)(2,1)S(1)}, u32[]{:S(2)}, u32[]{:S(2)}) collective-permute-start(bf16[2,2,384,128]{3,2,1,0:T(8,128)(2,1)S(1)} %get-tuple-element.52.rest_0_.q), channel_id=1, source_target_pairs={{8,0},{9,1},{10,2},{11,3},{12,4},{13,5},{14,6},{15,7},{16,8},{17,9... | collective-permute-start | bytes 1179656 | tf_op jit(solution)/shard_map/ppermute | solution.py:44
  75.5 4.0 %collective-permute-start.13 = (bf16[4,2,384,128]{3,2,1,0:T(8,128)(2,1)S(1)}, bf16[4,2,384,128]{3,2,1,0:T(8,128)(2,1)S(1)}, u32[]{:S(2)}, u32[]{:S(2)}) collective-permute-start(bf16[4,2,384,128]{3,2,1,0:T(8,128)(2,1)S(1)} %in_order.1.ka.va), channel_id=1, source_target_pairs={{0,1},{1,0},{2,3},{3,2},{4,5},{5,4},{6,7},{7,6},{8,9},{9,8},{10,11... | collective-permute-start | bytes 2359304 | tf_op jit(solution)/shard_map/ppermute | solution.py:44
  75.5 11.5 %collective-permute-start.14 = (bf16[4,2,384,128]{3,2,1,0:T(8,128)(2,1)S(1)}, bf16[4,2,384,128]{3,2,1,0:T(8,128)(2,1)S(1)}, u32[]{:S(2)}, u32[]{:S(2)}) collective-permute-start(bf16[4,2,384,128]{3,2,1,0:T(8,128)(2,1)S(1)} %get-tuple-element.53.ka.va), channel_id=1, source_target_pairs={{0,1},{1,0},{2,3},{3,2},{4,5},{5,4},{6,7},{7,6},{8,9},{9,8},{10,11... | collective-permute-start | bytes 2359304 | tf_op jit(solution)/shard_map/ppermute | solution.py:44
  76.0 19.4 %collective-permute-start.16 = (bf16[3,800,128]{2,1,0:T(8,128)(2,1)S(1)}, bf16[3,800,128]{2,1,0:T(8,128)(2,1)S(1)}, u32[]{:S(2)}, u32[]{:S(2)}) collective-permute-start(bf16[3,800,128]{2,1,0:T(8,128)(2,1)S(1)} %remote.2.rest_0_), channel_id=1, source_target_pairs={{0,8},{1,9},{2,10},{3,11},{4,12},{5,13},{6,14},{7,15},{8,16},{9,17... | collective-permute-start | bytes 1843208 | tf_op jit(solution)/shard_map/ppermute | solution.py:44
  83.3 19.1 %collective-permute-start.15 = (bf16[2,800,128]{2,1,0:T(8,128)(2,1)S(1)}, bf16[2,800,128]{2,1,0:T(8,128)(2,1)S(1)}, u32[]{:S(2)}, u32[]{:S(2)}) collective-permute-start(bf16[2,800,128]{2,1,0:T(8,128)(2,1)S(1)} %remote.3.rest_0_), channel_id=1, source_target_pairs={{0,8},{1,9},{2,10},{3,11},{4,12},{5,13},{6,14},{7,15},{8,16},{9,17... | collective-permute-start | bytes 1228808 | tf_op jit(solution)/shard_map/ppermute | solution.py:44
  96.6 9.9 %collective-permute-start.20 = (bf16[3,192,128]{2,1,0:T(8,128)(2,1)S(1)}, bf16[3,192,128]{2,1,0:T(8,128)(2,1)S(1)}, u32[]{:S(2)}, u32[]{:S(2)}) collective-permute-start(bf16[3,192,128]{2,1,0:T(8,128)(2,1)S(1)} %get-tuple-element.68), channel_id=1, source_target_pairs={{0,4},{1,5},{2,6},{3,7},{4,0},{5,1},{6,2},{7,3},{8,12},{9,13},{10,... | collective-permute-start | bytes 442376 | tf_op jit(solution)/shard_map/ppermute | solution.py:44
  98.2 8.8 %collective-permute-start.21 = (bf16[3,192,128]{2,1,0:T(8,128)(2,1)S(1)}, bf16[3,192,128]{2,1,0:T(8,128)(2,1)S(1)}, u32[]{:S(2)}, u32[]{:S(2)}) collective-permute-start(bf16[3,192,128]{2,1,0:T(8,128)(2,1)S(1)} %get-tuple-element.69), channel_id=1, source_target_pairs={{0,2},{1,3},{2,0},{3,1},{4,6},{5,7},{6,4},{7,5},{8,10},{9,11},{10,... | collective-permute-start | bytes 442376 | tf_op jit(solution)/shard_map/ppermute | solution.py:44
  99.7 7.3 %collective-permute-start.22 = (bf16[3,192,128]{2,1,0:T(8,128)(2,1)S(1)}, bf16[3,192,128]{2,1,0:T(8,128)(2,1)S(1)}, u32[]{:S(2)}, u32[]{:S(2)}) collective-permute-start(bf16[3,192,128]{2,1,0:T(8,128)(2,1)S(1)} %get-tuple-element.70), channel_id=1, source_target_pairs={{0,6},{1,7},{2,4},{3,5},{4,2},{5,3},{6,0},{7,1},{8,14},{9,15},{10,... | collective-permute-start | bytes 442376 | tf_op jit(solution)/shard_map/ppermute | solution.py:44
  103.4 5.1 %collective-permute-start.17 = (bf16[2,192,128]{2,1,0:T(8,128)(2,1)S(1)}, bf16[2,192,128]{2,1,0:T(8,128)(2,1)S(1)}, u32[]{:S(2)}, u32[]{:S(2)}) collective-permute-start(bf16[2,192,128]{2,1,0:T(8,128)(2,1)S(1)} %get-tuple-element.65), channel_id=1, source_target_pairs={{0,4},{1,5},{2,6},{3,7},{4,0},{5,1},{6,2},{7,3},{8,12},{9,13},{10,... | collective-permute-start | bytes 294920 | tf_op jit(solution)/shard_map/ppermute | solution.py:44
  105.0 4.7 %collective-permute-start.18 = (bf16[2,192,128]{2,1,0:T(8,128)(2,1)S(1)}, bf16[2,192,128]{2,1,0:T(8,128)(2,1)S(1)}, u32[]{:S(2)}, u32[]{:S(2)}) collective-permute-start(bf16[2,192,128]{2,1,0:T(8,128)(2,1)S(1)} %get-tuple-element.66), channel_id=1, source_target_pairs={{0,2},{1,3},{2,0},{3,1},{4,6},{5,7},{6,4},{7,5},{8,10},{9,11},{10,... | collective-permute-start | bytes 294920 | tf_op jit(solution)/shard_map/ppermute | solution.py:44
  106.5 5.5 %collective-permute-start.19 = (bf16[2,192,128]{2,1,0:T(8,128)(2,1)S(1)}, bf16[2,192,128]{2,1,0:T(8,128)(2,1)S(1)}, u32[]{:S(2)}, u32[]{:S(2)}) collective-permute-start(bf16[2,192,128]{2,1,0:T(8,128)(2,1)S(1)} %get-tuple-element.67), channel_id=1, source_target_pairs={{0,6},{1,7},{2,4},{3,5},{4,2},{5,3},{6,0},{7,1},{8,14},{9,15},{10,... | collective-permute-start | bytes 294920 | tf_op jit(solution)/shard_map/ppermute | solution.py:44
  (7 other events, 81.5 us)

commit v8 on v7

--- a/solution.py
+++ b/solution.py
@@ -60,7 +60,7 @@
     return span - 2, member
 
 
-PLACES = ((0, 0), (0, 1), (1, 0), (1, 1))
+PLACES = ((0, 0), (1, 1), (0, 1), (1, 0))
 
 
 def timestep_gate(level_index, plan, gate_weight, span_number):

time: 114 us -> 113 us (level)
  waiting for transfers between devices: 30.3 us -> 29.1 us
    ppermute x23, waiting for transfers between devices: 30.3 us -> 29.1 us  [move(): return lax.ppermute(block, AXES, route)]
  transfers between devices with their start and end apart: 23 -> 23, of which waited for: 13 -> 12; matrix products, arithmetic and copies ran while one was open for 3% -> 3% of each run, Pallas kernels for 34% -> 34%
where the time goes in v8:
time: 113 us; the launch traced here: 112 us
  Pallas kernels  45 us (40%)
  starting transfers between devices  33.7 us (30%)
  waiting for transfers between devices  29.1 us (26%)
  other arithmetic  2.08 us (2%)
  matrix products  1.34 us (1%)
    ppermute x23, starting transfers between devices, move(): return lax.ppermute(block, AXES, route)  33.7 us
    pallas_call x6, Pallas kernels, attend(): pl.pallas_call(functools.partial(body, len(after)), grid=(heads,), out_sh...  30.2 us
    ppermute x23, waiting for transfers between devices, move(): return lax.ppermute(block, AXES, route)  29.1 us
    pallas_call x2, Pallas kernels, pack(): pl.pallas_call(functools.partial(pack_kernel, first, heads, group_width,...  6.51 us
    pallas_call x2, Pallas kernels, stack(): pl.pallas_call(functools.partial(stack_kernel, heads, len(later) + len(af...  3.03 us
    pallas_call x2, Pallas kernels, finish(): pl.pallas_call(functools.partial(finish_kernel, first, group_width, len(b...  2.81 us
  transfers between devices with their start and end apart: 23, of which 12 were waited for; matrix products, arithmetic and copies ran while one was open for 3% of the time, Pallas kernels for 34%

profile of v8, /device:TPU:8, one launch (start us, length us, event | category | flops | bytes accessed | tf_op | source)
XLA Modules:
  0.0 112.4 jit_solution(2881273460718313825)
XLA Ops:
  0.0 3.5 %pack.2 = (bf16[9,192,128]{2,1,0:T(8,128)(2,1)}, bf16[9,192,128]{2,1,0:T(8,128)(2,1)}, bf16[9,192,128]{2,1,0:T(8,128)(2,1)}, bf16[9,192,128]{2,1,0:T(8,128)(2,1)}) custom-call(bf16[192,2560]{1,0:T(8,128)(2,1)} %q.3, bf16[192,2560]{1,0:T(8,128)(2,1)} %k.3, bf16[192,2560]{1,0:T(8,128)(2,1)} %v.3), custom_call_target="tpu_custom_call" | custom-call | bytes 1000 | tf_op jit(solution)/shard_map/pack/pallas_call | solution.py:97
  3.5 2.4 %collective-permute-start = (bf16[9,192,128]{2,1,0:T(8,128)(2,1)}, bf16[9,192,128]{2,1,0:T(8,128)(2,1)S(1)}, u32[]{:S(2)}, u32[]{:S(2)}) collective-permute-start(bf16[9,192,128]{2,1,0:T(8,128)(2,1)} %get-tuple-element.40), channel_id=1, source_target_pairs={{0,6},{1,7},{2,4},{3,5},{4,2},{5,3},{6,0},{7,1},{8,14},{9,15},{10,... | collective-permute-start | bytes 1327112 | tf_op jit(solution)/shard_map/ppermute | solution.py:44
  9.7 3.0 %pack.3 = (bf16[6,192,128]{2,1,0:T(8,128)(2,1)}, bf16[6,192,128]{2,1,0:T(8,128)(2,1)}, bf16[6,192,128]{2,1,0:T(8,128)(2,1)}, bf16[6,192,128]{2,1,0:T(8,128)(2,1)}) custom-call(bf16[192,2560]{1,0:T(8,128)(2,1)} %q.3, bf16[192,2560]{1,0:T(8,128)(2,1)} %k.3, bf16[192,2560]{1,0:T(8,128)(2,1)} %v.3, bf16[9,192,128]{2,1,0:T(8,128)(2,1)} %get-tuple-element.38.rest_0_.refs_0_), custom_call_target="tpu_custom_call" | custom-call | bytes 1000 | tf_op jit(solution)/shard_map/pack/pallas_call | solution.py:97
  14.2 3.5 %collective-permute-done.refs_1_ = bf16[9,192,128]{2,1,0:T(8,128)(2,1)S(1)} collective-permute-done((bf16[9,192,128]{2,1,0:T(8,128)(2,1)}, bf16[9,192,128]{2,1,0:T(8,128)(2,1)S(1)}, u32[]{:S(2)}, u32[]{:S(2)}) %collective-permute-start) | collective-permute-done | bytes 442400 | tf_op jit(solution)/shard_map/ppermute | solution.py:44
  17.7 8.3 %collective-permute-done.1.refs_2_ = bf16[9,192,128]{2,1,0:T(8,128)(2,1)S(1)} collective-permute-done((bf16[9,192,128]{2,1,0:T(8,128)(2,1)}, bf16[9,192,128]{2,1,0:T(8,128)(2,1)S(1)}, u32[]{:S(2)}, u32[]{:S(2)}) %collective-permute-start.1) | collective-permute-done | bytes 442400 | tf_op jit(solution)/shard_map/ppermute | solution.py:44
  26.2 1.9 %stack.36 = (bf16[3,2,384,128]{3,2,1,0:T(8,128)(2,1)S(1)}, bf16[6,2,384,128]{3,2,1,0:T(8,128)(2,1)S(1)}, bf16[6,192,128]{2,1,0:T(8,128)(2,1)S(1)}, bf16[6,192,12...) custom-call(s32[9]{0:T(128)S(1)} %stack.35.meta, ...), custom_call_target="tpu_custom_call", output_to_operand_aliasing={{2}: (5, {}), {3}: (6, {}), {4}: (7, {})} | custom-call | bytes 1000 | tf_op jit(solution)/shard_map/stack/pallas_call | solution.py:133
  28.2 3.5 %collective-permute-start.9 = (bf16[6,2,384,128]{3,2,1,0:T(8,128)(2,1)S(1)}, bf16[6,2,384,128]{3,2,1,0:T(8,128)(2,1)S(1)}, u32[]{:S(2)}, u32[]{:S(2)}) collective-permute-start(bf16[6,2,384,128]{3,2,1,0:T(8,128)(2,1)S(1)} %get-tuple-element.50.ka.va), channel_id=1, source_target_pairs={{0,8},{1,9},{2,10},{3,11},{4,12},{5,13},{6,14},{7,15},{8,16},{9,17... | collective-permute-start | bytes 3538952 | tf_op jit(solution)/shard_map/ppermute | solution.py:44
  31.7 2.4 %collective-permute-start.7 = (bf16[3,2,384,128]{3,2,1,0:T(8,128)(2,1)S(1)}, bf16[3,2,384,128]{3,2,1,0:T(8,128)(2,1)S(1)}, u32[]{:S(2)}, u32[]{:S(2)}) collective-permute-start(bf16[3,2,384,128]{3,2,1,0:T(8,128)(2,1)S(1)} %get-tuple-element.49.q.rest_0_), channel_id=1, source_target_pairs={{8,0},{9,1},{10,2},{11,3},{12,4},{13,5},{14,6},{15,7},{16,8},{17,9... | collective-permute-start | bytes 1769480 | tf_op jit(solution)/shard_map/ppermute | solution.py:44
  34.1 1.6 %collective-permute-start.3 = (bf16[6,192,128]{2,1,0:T(8,128)(2,1)S(1)}, bf16[6,192,128]{2,1,0:T(8,128)(2,1)S(1)}, u32[]{:S(2)}, u32[]{:S(2)}) collective-permute-start(bf16[6,192,128]{2,1,0:T(8,128)(2,1)S(1)} %get-tuple-element.46), channel_id=1, source_target_pairs={{0,6},{1,7},{2,4},{3,5},{4,2},{5,3},{6,0},{7,1},{8,14},{9,15},{10,... | collective-permute-start | bytes 884744 | tf_op jit(solution)/shard_map/ppermute | solution.py:44
  37.7 5.2 %near.2 = (f32[3,768,128]{2,1,0:T(8,128)S(1)}, f32[3,8,128]{2,1,0:T(8,128)S(1)}) custom-call(bf16[3,2,384,128]{3,2,1,0:T(8,128)(2,1)S(1)} %get-tuple-element.49.q.rest_0_, bf16[6,2,384,128]{3,2,1,0:T(8,128)(2,1)S(1)} %get-tuple-element.50.ka.va, bf16[6,2,384,128]{3,2,1,0:T(8,128)(2,1)S(1)} %get-tuple-element.50.ka.va, ...), custom_call_target="tpu_custom_call" | custom-call | bytes 1000 | tf_op jit(solution)/shard_map/near/pallas_call | solution.py:313
  42.9 2.1 %collective-permute-done.3.refs_1_ = bf16[6,192,128]{2,1,0:T(8,128)(2,1)S(1)} collective-permute-done((bf16[6,192,128]{2,1,0:T(8,128)(2,1)S(1)}, bf16[6,192,128]{2,1,0:T(8,128)(2,1)S(1)}, u32[]{:S(2)}, u32[]{:S(2)}) %collective-permute-start.3) | collective-permute-done | bytes 294944 | tf_op jit(solution)/shard_map/ppermute | solution.py:44
  45.0 5.2 %collective-permute-done.4.refs_2_ = bf16[6,192,128]{2,1,0:T(8,128)(2,1)S(1)} collective-permute-done((bf16[6,192,128]{2,1,0:T(8,128)(2,1)S(1)}, bf16[6,192,128]{2,1,0:T(8,128)(2,1)S(1)}, u32[]{:S(2)}, u32[]{:S(2)}) %collective-permute-start.4) | collective-permute-done | bytes 294944 | tf_op jit(solution)/shard_map/ppermute | solution.py:44
  51.4 3.4 %collective-permute-start.8 = (bf16[4,2,384,128]{3,2,1,0:T(8,128)(2,1)S(1)}, bf16[4,2,384,128]{3,2,1,0:T(8,128)(2,1)S(1)}, u32[]{:S(2)}, u32[]{:S(2)}) collective-permute-start(bf16[4,2,384,128]{3,2,1,0:T(8,128)(2,1)S(1)} %get-tuple-element.53.ka.va), channel_id=1, source_target_pairs={{0,8},{1,9},{2,10},{3,11},{4,12},{5,13},{6,14},{7,15},{8,16},{9,17... | collective-permute-start | bytes 2359304 | tf_op jit(solution)/shard_map/ppermute | solution.py:44
  54.8 4.0 %collective-permute-done.9.kv = bf16[6,2,384,128]{3,2,1,0:T(8,128)(2,1)S(1)} collective-permute-done((bf16[6,2,384,128]{3,2,1,0:T(8,128)(2,1)S(1)}, bf16[6,2,384,128]{3,2,1,0:T(8,128)(2,1)S(1)}, u32[]{:S(2)}, u32[]{:S(2)}) %collective-permute-start.9) | collective-permute-done | bytes 1179680 | tf_op jit(solution)/shard_map/ppermute | solution.py:44
  59.7 1.9 %collective-permute-start.12 = (bf16[2,2,384,128]{3,2,1,0:T(8,128)(2,1)S(1)}, bf16[2,2,384,128]{3,2,1,0:T(8,128)(2,1)S(1)}, u32[]{:S(2)}, u32[]{:S(2)}) collective-permute-start(bf16[2,2,384,128]{3,2,1,0:T(8,128)(2,1)S(1)} %get-tuple-element.52.rest_0_.q), channel_id=1, source_target_pairs={{8,0},{9,1},{10,2},{11,3},{12,4},{13,5},{14,6},{15,7},{16,8},{17,9... | collective-permute-start | bytes 1179656 | tf_op jit(solution)/shard_map/ppermute | solution.py:44
  62.0 5.7 %remote.2.rest_0_ = bf16[3,800,128]{2,1,0:T(8,128)(2,1)S(1)} custom-call(bf16[3,2,384,128]{3,2,1,0:T(8,128)(2,1)S(1)} %collective-permute-done.7.refs_5_.q, bf16[3,2,384,128]{3,2,1,0:T(8,128)(2,1)S(1)} %get-tuple-element.54.ka, bf16[3,2,384,128]{3,2,1,0:T(8,128)(2,1)S(1)} %get-tuple-element.55.va, bf16[3,2,384,128]{3,2,1,0:T(8,128)(2,1)S(1)} %collective-permute-done.10.kb, ...), custom_call_target="tpu_custom_call" | custom-call | bytes 1000 | tf_op jit(solution)/shard_map/remote/pallas_call | solution.py:313
  67.7 7.1 %far.2 = (f32[3,768,128]{2,1,0:T(8,128)S(1)}, f32[3,8,128]{2,1,0:T(8,128)S(1)}) custom-call(s32[9]{0:T(128)S(1)} %stack.35.meta, bf16[3,2,384,128]{3,2,1,0:T(8,128)(2,1)S(1)} %get-tuple-element.49.q.rest_0_, bf16[3,2,384,128]{3,2,1,0:T(8,128)(2,1)S(1)} %get-tuple-element.54.ka, bf16[3,2,384,128]{3,2,1,0:T(8,128)(2,1)S(1)} %get-tuple-element.55.va, ...), custom_call_target="tpu_custom_call" | custom-call | bytes 1000 | tf_op jit(solution)/shard_map/far/pallas_call | solution.py:313
  75.8 3.5 %collective-permute-start.16 = (bf16[3,800,128]{2,1,0:T(8,128)(2,1)S(1)}, bf16[3,800,128]{2,1,0:T(8,128)(2,1)S(1)}, u32[]{:S(2)}, u32[]{:S(2)}) collective-permute-start(bf16[3,800,128]{2,1,0:T(8,128)(2,1)S(1)} %remote.2.rest_0_), channel_id=1, source_target_pairs={{0,8},{1,9},{2,10},{3,11},{4,12},{5,13},{6,14},{7,15},{8,16},{9,17... | collective-permute-start | bytes 1843208 | tf_op jit(solution)/shard_map/ppermute | solution.py:44
  79.3 3.8 %remote.3.rest_0_ = bf16[2,800,128]{2,1,0:T(8,128)(2,1)S(1)} custom-call(bf16[2,2,384,128]{3,2,1,0:T(8,128)(2,1)S(1)} %collective-permute-done.12.refs_2_.q, bf16[4,2,384,128]{3,2,1,0:T(8,128)(2,1)S(1)} %in_order.1.ka.va, bf16[4,2,384,128]{3,2,1,0:T(8,128)(2,1)S(1)} %in_order.1.ka.va, bf16[4,2,384,128]{3,2,1,0:T(8,128)(2,1)S(1)} %collective-permute-done.13.kb.vb, ...), custom_call_target="tpu_custom_call" | custom-call | bytes 1000 | tf_op jit(solution)/shard_map/remote/pallas_call | solution.py:313
  83.1 3.7 %collective-permute-start.15 = (bf16[2,800,128]{2,1,0:T(8,128)(2,1)S(1)}, bf16[2,800,128]{2,1,0:T(8,128)(2,1)S(1)}, u32[]{:S(2)}, u32[]{:S(2)}) collective-permute-start(bf16[2,800,128]{2,1,0:T(8,128)(2,1)S(1)} %remote.3.rest_0_), channel_id=1, source_target_pairs={{0,8},{1,9},{2,10},{3,11},{4,12},{5,13},{6,14},{7,15},{8,16},{9,17... | collective-permute-start | bytes 1228808 | tf_op jit(solution)/shard_map/ppermute | solution.py:44
  86.8 3.5 %near.3 = (f32[2,768,128]{2,1,0:T(8,128)S(1)}, f32[2,8,128]{2,1,0:T(8,128)S(1)}) custom-call(bf16[2,2,384,128]{3,2,1,0:T(8,128)(2,1)S(1)} %get-tuple-element.52.rest_0_.q, bf16[4,2,384,128]{3,2,1,0:T(8,128)(2,1)S(1)} %get-tuple-element.53.ka.va, bf16[4,2,384,128]{3,2,1,0:T(8,128)(2,1)S(1)} %get-tuple-element.53.ka.va, ...), custom_call_target="tpu_custom_call" | custom-call | bytes 1000 | tf_op jit(solution)/shard_map/near/pallas_call | solution.py:313
  90.3 4.9 %far.3 = (f32[2,768,128]{2,1,0:T(8,128)S(1)}, f32[2,8,128]{2,1,0:T(8,128)S(1)}) custom-call(s32[9]{0:T(128)S(1)} %stack.35.meta, bf16[2,2,384,128]{3,2,1,0:T(8,128)(2,1)S(1)} %get-tuple-element.52.rest_0_.q, bf16[4,2,384,128]{3,2,1,0:T(8,128)(2,1)S(1)} %in_order.1.ka.va, bf16[4,2,384,128]{3,2,1,0:T(8,128)(2,1)S(1)} %in_order.1.ka.va, ...), custom_call_target="tpu_custom_call" | custom-call | bytes 1000 | tf_op jit(solution)/shard_map/far/pallas_call | solution.py:313
  96.4 1.6 %collective-permute-start.20 = (bf16[3,192,128]{2,1,0:T(8,128)(2,1)S(1)}, bf16[3,192,128]{2,1,0:T(8,128)(2,1)S(1)}, u32[]{:S(2)}, u32[]{:S(2)}) collective-permute-start(bf16[3,192,128]{2,1,0:T(8,128)(2,1)S(1)} %get-tuple-element.68), channel_id=1, source_target_pairs={{0,6},{1,7},{2,4},{3,5},{4,2},{5,3},{6,0},{7,1},{8,14},{9,15},{10,... | collective-permute-start | bytes 442376 | tf_op jit(solution)/shard_map/ppermute | solution.py:44
  100.0 2.2 %collective-permute-done.15.o_far = bf16[2,800,128]{2,1,0:T(8,128)(2,1)S(1)} collective-permute-done((bf16[2,800,128]{2,1,0:T(8,128)(2,1)S(1)}, bf16[2,800,128]{2,1,0:T(8,128)(2,1)S(1)}, u32[]{:S(2)}, u32[]{:S(2)}) %collective-permute-start.15) | collective-permute-done | bytes 409632 | tf_op jit(solution)/shard_map/ppermute | solution.py:44
  (60 shorter events, 23.4 us)
Async XLA Ops:
  3.5 14.2 %collective-permute-start = (bf16[9,192,128]{2,1,0:T(8,128)(2,1)}, bf16[9,192,128]{2,1,0:T(8,128)(2,1)S(1)}, u32[]{:S(2)}, u32[]{:S(2)}) collective-permute-start(bf16[9,192,128]{2,1,0:T(8,128)(2,1)} %get-tuple-element.40), channel_id=1, source_target_pairs={{0,6},{1,7},{2,4},{3,5},{4,2},{5,3},{6,0},{7,1},{8,14},{9,15},{10,... | collective-permute-start | bytes 1327112 | tf_op jit(solution)/shard_map/ppermute | solution.py:44
  5.9 20.1 %collective-permute-start.1 = (bf16[9,192,128]{2,1,0:T(8,128)(2,1)}, bf16[9,192,128]{2,1,0:T(8,128)(2,1)S(1)}, u32[]{:S(2)}, u32[]{:S(2)}) collective-permute-start(bf16[9,192,128]{2,1,0:T(8,128)(2,1)} %get-tuple-element.41), channel_id=1, source_target_pairs={{0,4},{1,5},{2,6},{3,7},{4,0},{5,1},{6,2},{7,3},{8,12},{9,13},{10,... | collective-permute-start | bytes 1327112 | tf_op jit(solution)/shard_map/ppermute | solution.py:44
  6.5 19.7 %collective-permute-start.2 = (bf16[9,192,128]{2,1,0:T(8,128)(2,1)}, bf16[9,192,128]{2,1,0:T(8,128)(2,1)}, u32[]{:S(2)}, u32[]{:S(2)}) collective-permute-start(bf16[9,192,128]{2,1,0:T(8,128)(2,1)} %get-tuple-element.42), channel_id=1, source_target_pairs={{0,2},{1,3},{2,0},{3,1},{4,6},{5,7},{6,4},{7,5},{8,10},{9,11},{10,... | collective-permute-start | bytes 1327112 | tf_op jit(solution)/shard_map/ppermute | solution.py:44
  12.8 13.4 %copy-start.1 = (bf16[9,192,128]{2,1,0:T(8,128)(2,1)S(1)}, bf16[9,192,128]{2,1,0:T(8,128)(2,1)}, u32[]{:S(2)}) copy-start(bf16[9,192,128]{2,1,0:T(8,128)(2,1)} %get-tuple-element.38.rest_0_.refs_0_) | copy-start | bytes 1327108
  28.1 9.0 %collective-permute-start.6 = (bf16[6,2,384,128]{3,2,1,0:T(8,128)(2,1)S(1)}, bf16[6,2,384,128]{3,2,1,0:T(8,128)(2,1)S(1)}, u32[]{:S(2)}, u32[]{:S(2)}) collective-permute-start(bf16[6,2,384,128]{3,2,1,0:T(8,128)(2,1)S(1)} %get-tuple-element.50.ka.va), channel_id=1, source_target_pairs={{0,1},{1,0},{2,3},{3,2},{4,5},{5,4},{6,7},{7,6},{8,9},{9,8},{10,11... | collective-permute-start | bytes 3538952 | tf_op jit(solution)/shard_map/ppermute | solution.py:44
  28.2 30.7 %collective-permute-start.9 = (bf16[6,2,384,128]{3,2,1,0:T(8,128)(2,1)S(1)}, bf16[6,2,384,128]{3,2,1,0:T(8,128)(2,1)S(1)}, u32[]{:S(2)}, u32[]{:S(2)}) collective-permute-start(bf16[6,2,384,128]{3,2,1,0:T(8,128)(2,1)S(1)} %get-tuple-element.50.ka.va), channel_id=1, source_target_pairs={{0,8},{1,9},{2,10},{3,11},{4,12},{5,13},{6,14},{7,15},{8,16},{9,17... | collective-permute-start | bytes 3538952 | tf_op jit(solution)/shard_map/ppermute | solution.py:44
  31.7 18.6 %collective-permute-start.7 = (bf16[3,2,384,128]{3,2,1,0:T(8,128)(2,1)S(1)}, bf16[3,2,384,128]{3,2,1,0:T(8,128)(2,1)S(1)}, u32[]{:S(2)}, u32[]{:S(2)}) collective-permute-start(bf16[3,2,384,128]{3,2,1,0:T(8,128)(2,1)S(1)} %get-tuple-element.49.q.rest_0_), channel_id=1, source_target_pairs={{8,0},{9,1},{10,2},{11,3},{12,4},{13,5},{14,6},{15,7},{16,8},{17,9... | collective-permute-start | bytes 1769480 | tf_op jit(solution)/shard_map/ppermute | solution.py:44
  34.1 10.9 %collective-permute-start.3 = (bf16[6,192,128]{2,1,0:T(8,128)(2,1)S(1)}, bf16[6,192,128]{2,1,0:T(8,128)(2,1)S(1)}, u32[]{:S(2)}, u32[]{:S(2)}) collective-permute-start(bf16[6,192,128]{2,1,0:T(8,128)(2,1)S(1)} %get-tuple-element.46), channel_id=1, source_target_pairs={{0,6},{1,7},{2,4},{3,5},{4,2},{5,3},{6,0},{7,1},{8,14},{9,15},{10,... | collective-permute-start | bytes 884744 | tf_op jit(solution)/shard_map/ppermute | solution.py:44
  35.7 14.5 %collective-permute-start.4 = (bf16[6,192,128]{2,1,0:T(8,128)(2,1)S(1)}, bf16[6,192,128]{2,1,0:T(8,128)(2,1)S(1)}, u32[]{:S(2)}, u32[]{:S(2)}) collective-permute-start(bf16[6,192,128]{2,1,0:T(8,128)(2,1)S(1)} %get-tuple-element.47), channel_id=1, source_target_pairs={{0,4},{1,5},{2,6},{3,7},{4,0},{5,1},{6,2},{7,3},{8,12},{9,13},{10,... | collective-permute-start | bytes 884744 | tf_op jit(solution)/shard_map/ppermute | solution.py:44
  37.1 13.1 %collective-permute-start.5 = (bf16[6,192,128]{2,1,0:T(8,128)(2,1)S(1)}, bf16[6,192,128]{2,1,0:T(8,128)(2,1)S(1)}, u32[]{:S(2)}, u32[]{:S(2)}) collective-permute-start(bf16[6,192,128]{2,1,0:T(8,128)(2,1)S(1)} %get-tuple-element.48), channel_id=1, source_target_pairs={{0,2},{1,3},{2,0},{3,1},{4,6},{5,7},{6,4},{7,5},{8,10},{9,11},{10,... | collective-permute-start | bytes 884744 | tf_op jit(solution)/shard_map/ppermute | solution.py:44
  51.4 23.9 %collective-permute-start.8 = (bf16[4,2,384,128]{3,2,1,0:T(8,128)(2,1)S(1)}, bf16[4,2,384,128]{3,2,1,0:T(8,128)(2,1)S(1)}, u32[]{:S(2)}, u32[]{:S(2)}) collective-permute-start(bf16[4,2,384,128]{3,2,1,0:T(8,128)(2,1)S(1)} %get-tuple-element.53.ka.va), channel_id=1, source_target_pairs={{0,8},{1,9},{2,10},{3,11},{4,12},{5,13},{6,14},{7,15},{8,16},{9,17... | collective-permute-start | bytes 2359304 | tf_op jit(solution)/shard_map/ppermute | solution.py:44
  59.1 2.5 %collective-permute-start.10 = (bf16[3,2,384,128]{3,2,1,0:T(8,128)(2,1)S(1)}, bf16[3,2,384,128]{3,2,1,0:T(8,128)(2,1)S(1)}, u32[]{:S(2)}, u32[]{:S(2)}) collective-permute-start(bf16[3,2,384,128]{3,2,1,0:T(8,128)(2,1)S(1)} %get-tuple-element.54.ka), channel_id=1, source_target_pairs={{0,1},{1,0},{2,3},{3,2},{4,5},{5,4},{6,7},{7,6},{8,9},{9,8},{10,11... | collective-permute-start | bytes 1769480 | tf_op jit(solution)/shard_map/ppermute | solution.py:44
  59.2 2.8 %collective-permute-start.11 = (bf16[3,2,384,128]{3,2,1,0:T(8,128)(2,1)S(1)}, bf16[3,2,384,128]{3,2,1,0:T(8,128)(2,1)S(1)}, u32[]{:S(2)}, u32[]{:S(2)}) collective-permute-start(bf16[3,2,384,128]{3,2,1,0:T(8,128)(2,1)S(1)} %get-tuple-element.55.va), channel_id=1, source_target_pairs={{0,1},{1,0},{2,3},{3,2},{4,5},{5,4},{6,7},{7,6},{8,9},{9,8},{10,11... | collective-permute-start | bytes 1769480 | tf_op jit(solution)/shard_map/ppermute | solution.py:44
  59.7 15.1 %collective-permute-start.12 = (bf16[2,2,384,128]{3,2,1,0:T(8,128)(2,1)S(1)}, bf16[2,2,384,128]{3,2,1,0:T(8,128)(2,1)S(1)}, u32[]{:S(2)}, u32[]{:S(2)}) collective-permute-start(bf16[2,2,384,128]{3,2,1,0:T(8,128)(2,1)S(1)} %get-tuple-element.52.rest_0_.q), channel_id=1, source_target_pairs={{8,0},{9,1},{10,2},{11,3},{12,4},{13,5},{14,6},{15,7},{16,8},{17,9... | collective-permute-start | bytes 1179656 | tf_op jit(solution)/shard_map/ppermute | solution.py:44
  75.3 4.0 %collective-permute-start.13 = (bf16[4,2,384,128]{3,2,1,0:T(8,128)(2,1)S(1)}, bf16[4,2,384,128]{3,2,1,0:T(8,128)(2,1)S(1)}, u32[]{:S(2)}, u32[]{:S(2)}) collective-permute-start(bf16[4,2,384,128]{3,2,1,0:T(8,128)(2,1)S(1)} %in_order.1.ka.va), channel_id=1, source_target_pairs={{0,1},{1,0},{2,3},{3,2},{4,5},{5,4},{6,7},{7,6},{8,9},{9,8},{10,11... | collective-permute-start | bytes 2359304 | tf_op jit(solution)/shard_map/ppermute | solution.py:44
  75.3 11.5 %collective-permute-start.14 = (bf16[4,2,384,128]{3,2,1,0:T(8,128)(2,1)S(1)}, bf16[4,2,384,128]{3,2,1,0:T(8,128)(2,1)S(1)}, u32[]{:S(2)}, u32[]{:S(2)}) collective-permute-start(bf16[4,2,384,128]{3,2,1,0:T(8,128)(2,1)S(1)} %get-tuple-element.53.ka.va), channel_id=1, source_target_pairs={{0,1},{1,0},{2,3},{3,2},{4,5},{5,4},{6,7},{7,6},{8,9},{9,8},{10,11... | collective-permute-start | bytes 2359304 | tf_op jit(solution)/shard_map/ppermute | solution.py:44
  75.8 19.4 %collective-permute-start.16 = (bf16[3,800,128]{2,1,0:T(8,128)(2,1)S(1)}, bf16[3,800,128]{2,1,0:T(8,128)(2,1)S(1)}, u32[]{:S(2)}, u32[]{:S(2)}) collective-permute-start(bf16[3,800,128]{2,1,0:T(8,128)(2,1)S(1)} %remote.2.rest_0_), channel_id=1, source_target_pairs={{0,8},{1,9},{2,10},{3,11},{4,12},{5,13},{6,14},{7,15},{8,16},{9,17... | collective-permute-start | bytes 1843208 | tf_op jit(solution)/shard_map/ppermute | solution.py:44
  83.1 19.1 %collective-permute-start.15 = (bf16[2,800,128]{2,1,0:T(8,128)(2,1)S(1)}, bf16[2,800,128]{2,1,0:T(8,128)(2,1)S(1)}, u32[]{:S(2)}, u32[]{:S(2)}) collective-permute-start(bf16[2,800,128]{2,1,0:T(8,128)(2,1)S(1)} %remote.3.rest_0_), channel_id=1, source_target_pairs={{0,8},{1,9},{2,10},{3,11},{4,12},{5,13},{6,14},{7,15},{8,16},{9,17... | collective-permute-start | bytes 1228808 | tf_op jit(solution)/shard_map/ppermute | solution.py:44
  96.4 9.8 %collective-permute-start.20 = (bf16[3,192,128]{2,1,0:T(8,128)(2,1)S(1)}, bf16[3,192,128]{2,1,0:T(8,128)(2,1)S(1)}, u32[]{:S(2)}, u32[]{:S(2)}) collective-permute-start(bf16[3,192,128]{2,1,0:T(8,128)(2,1)S(1)} %get-tuple-element.68), channel_id=1, source_target_pairs={{0,6},{1,7},{2,4},{3,5},{4,2},{5,3},{6,0},{7,1},{8,14},{9,15},{10,... | collective-permute-start | bytes 442376 | tf_op jit(solution)/shard_map/ppermute | solution.py:44
  98.1 8.7 %collective-permute-start.21 = (bf16[3,192,128]{2,1,0:T(8,128)(2,1)S(1)}, bf16[3,192,128]{2,1,0:T(8,128)(2,1)S(1)}, u32[]{:S(2)}, u32[]{:S(2)}) collective-permute-start(bf16[3,192,128]{2,1,0:T(8,128)(2,1)S(1)} %get-tuple-element.69), channel_id=1, source_target_pairs={{0,4},{1,5},{2,6},{3,7},{4,0},{5,1},{6,2},{7,3},{8,12},{9,13},{10,... | collective-permute-start | bytes 442376 | tf_op jit(solution)/shard_map/ppermute | solution.py:44
  99.5 7.3 %collective-permute-start.22 = (bf16[3,192,128]{2,1,0:T(8,128)(2,1)S(1)}, bf16[3,192,128]{2,1,0:T(8,128)(2,1)S(1)}, u32[]{:S(2)}, u32[]{:S(2)}) collective-permute-start(bf16[3,192,128]{2,1,0:T(8,128)(2,1)S(1)} %get-tuple-element.70), channel_id=1, source_target_pairs={{0,2},{1,3},{2,0},{3,1},{4,6},{5,7},{6,4},{7,5},{8,10},{9,11},{10,... | collective-permute-start | bytes 442376 | tf_op jit(solution)/shard_map/ppermute | solution.py:44
  103.2 6.5 %collective-permute-start.17 = (bf16[2,192,128]{2,1,0:T(8,128)(2,1)S(1)}, bf16[2,192,128]{2,1,0:T(8,128)(2,1)S(1)}, u32[]{:S(2)}, u32[]{:S(2)}) collective-permute-start(bf16[2,192,128]{2,1,0:T(8,128)(2,1)S(1)} %get-tuple-element.65), channel_id=1, source_target_pairs={{0,6},{1,7},{2,4},{3,5},{4,2},{5,3},{6,0},{7,1},{8,14},{9,15},{10,... | collective-permute-start | bytes 294920 | tf_op jit(solution)/shard_map/ppermute | solution.py:44
  104.9 5.3 %collective-permute-start.18 = (bf16[2,192,128]{2,1,0:T(8,128)(2,1)S(1)}, bf16[2,192,128]{2,1,0:T(8,128)(2,1)S(1)}, u32[]{:S(2)}, u32[]{:S(2)}) collective-permute-start(bf16[2,192,128]{2,1,0:T(8,128)(2,1)S(1)} %get-tuple-element.66), channel_id=1, source_target_pairs={{0,4},{1,5},{2,6},{3,7},{4,0},{5,1},{6,2},{7,3},{8,12},{9,13},{10,... | collective-permute-start | bytes 294920 | tf_op jit(solution)/shard_map/ppermute | solution.py:44
  106.3 4.6 %collective-permute-start.19 = (bf16[2,192,128]{2,1,0:T(8,128)(2,1)S(1)}, bf16[2,192,128]{2,1,0:T(8,128)(2,1)S(1)}, u32[]{:S(2)}, u32[]{:S(2)}) collective-permute-start(bf16[2,192,128]{2,1,0:T(8,128)(2,1)S(1)} %get-tuple-element.67), channel_id=1, source_target_pairs={{0,2},{1,3},{2,0},{3,1},{4,6},{5,7},{6,4},{7,5},{8,10},{9,11},{10,... | collective-permute-start | bytes 294920 | tf_op jit(solution)/shard_map/ppermute | solution.py:44
  (7 other events, 80.8 us)

commit v9 on v8

--- a/solution.py
+++ b/solution.py
@@ -178,12 +178,51 @@
         lse_ref[pl.ds(p * (rows // TILE) + t, 1)] = column.T[:1]
 
 
+def attend_with_extra(q_ref, joint, extra, half, o_ref, lse_ref):
+    rows = q_ref.shape[2]
+    scale = math.log2(math.e) / math.sqrt(HEAD_DIM)
+
+    def scores_of(q, blocks):
+        keys = [kv[0][0, i] for kv, i in blocks]
+        return [lax.dot_general(q, k, NT, preferred_element_type=jnp.float32) for k in keys]
+
+    def sums(scores, peak, blocks):
+        weights = [jnp.exp2(s * scale - peak) for s in scores]
+        values = [kv[1][0, i] for kv, i in blocks]
+        out = [
+            lax.dot_general(w.astype(jnp.bfloat16), v, NN, preferred_element_type=jnp.float32)
+            for w, v in zip(weights, values)
+        ]
+        total = functools.reduce(jnp.add, weights).sum(axis=1, keepdims=True)
+        return total, functools.reduce(jnp.add, out)
+
+    def top(scores):
+        return functools.reduce(jnp.maximum, scores).max(axis=1, keepdims=True) * scale
+
+    every = scores_of(q_ref[0].reshape(2 * rows, HEAD_DIM), joint)
+    more = scores_of(q_ref[0, half], extra)
+    peak = top(every)
+    peaks = [peak[:rows], peak[rows:]]
+    peaks[half] = jnp.maximum(peaks[half], top(more))
+    total, out = sums(every, jnp.concatenate(peaks, axis=0), joint)
+    more_total, more_out = sums(more, peaks[half], extra)
+    for p in range(2):
+        part = slice(p * rows, (p + 1) * rows)
+        sum_p, out_p = total[part], out[part]
+        if p == half:
+            sum_p, out_p = sum_p + more_total, out_p + more_out
+        o_ref[0, pl.ds(p * rows, rows)] = (out_p / sum_p).astype(o_ref.dtype)
+        lse = peaks[p] + jnp.log2(sum_p)
+        for t in range(rows // TILE):
+            column = jnp.broadcast_to(lse[t * TILE : (t + 1) * TILE], (TILE, TILE))
+            lse_ref[pl.ds(p * (rows // TILE) + t, 1)] = column.T[:1]
+
+
 def remote_kernel(count, q, ka, va, kb, vb, *rest):
     o, lse = rest[count:]
     a, b = (ka, va), (kb, vb)
     every = [(a, 0), (b, 0), (a, 1), (b, 1)]
-    attend_rows(q, 0, every, o, lse)
-    attend_rows(q, 1, every[2:], o, lse)
+    attend_with_extra(q, every[2:], every[:2], 0, o, lse)
     left, terms = lse[...], []
     for _ in range(3):
         terms.append(left.astype(jnp.bfloat16))

time: 113 us -> 113 us (level)
  transfers between devices with their start and end apart: 23 -> 23, of which waited for: 12 -> 12; matrix products, arithmetic and copies ran while one was open for 3% -> 3% of each run, Pallas kernels for 34% -> 33%
where the time goes in v9:
time: 113 us; the launch traced here: 112 us
  Pallas kernels  44.2 us (39%)
  starting transfers between devices  33.7 us (30%)
  waiting for transfers between devices  30 us (27%)
  other arithmetic  2.08 us (2%)
  matrix products  1.34 us (1%)
    ppermute x23, starting transfers between devices, move(): return lax.ppermute(block, AXES, route)  33.7 us
    ppermute x23, waiting for transfers between devices, move(): return lax.ppermute(block, AXES, route)  30 us
    pallas_call x6, Pallas kernels, attend(): pl.pallas_call(functools.partial(body, len(after)), grid=(heads,), out_sh...  29.3 us
    pallas_call x2, Pallas kernels, pack(): pl.pallas_call(functools.partial(pack_kernel, first, heads, group_width,...  6.51 us
    pallas_call x2, Pallas kernels, stack(): pl.pallas_call(functools.partial(stack_kernel, heads, len(later) + len(af...  3.03 us
    pallas_call x2, Pallas kernels, finish(): pl.pallas_call(functools.partial(finish_kernel, first, group_width, len(b...  2.81 us
  transfers between devices with their start and end apart: 23, of which 12 were waited for; matrix products, arithmetic and copies ran while one was open for 3% of the time, Pallas kernels for 33%

profile of v9, /device:TPU:8, one launch (start us, length us, event | category | flops | bytes accessed | tf_op | source)
XLA Modules:
  0.0 112.4 jit_solution(9811756214147608555)
XLA Ops:
  0.0 3.5 %pack.2 = (bf16[9,192,128]{2,1,0:T(8,128)(2,1)}, bf16[9,192,128]{2,1,0:T(8,128)(2,1)}, bf16[9,192,128]{2,1,0:T(8,128)(2,1)}, bf16[9,192,128]{2,1,0:T(8,128)(2,1)}) custom-call(bf16[192,2560]{1,0:T(8,128)(2,1)} %q.3, bf16[192,2560]{1,0:T(8,128)(2,1)} %k.3, bf16[192,2560]{1,0:T(8,128)(2,1)} %v.3), custom_call_target="tpu_custom_call" | custom-call | bytes 1000 | tf_op jit(solution)/shard_map/pack/pallas_call | solution.py:97
  3.5 2.4 %collective-permute-start = (bf16[9,192,128]{2,1,0:T(8,128)(2,1)}, bf16[9,192,128]{2,1,0:T(8,128)(2,1)S(1)}, u32[]{:S(2)}, u32[]{:S(2)}) collective-permute-start(bf16[9,192,128]{2,1,0:T(8,128)(2,1)} %get-tuple-element.40), channel_id=1, source_target_pairs={{0,6},{1,7},{2,4},{3,5},{4,2},{5,3},{6,0},{7,1},{8,14},{9,15},{10,... | collective-permute-start | bytes 1327112 | tf_op jit(solution)/shard_map/ppermute | solution.py:44
  9.7 3.0 %pack.3 = (bf16[6,192,128]{2,1,0:T(8,128)(2,1)}, bf16[6,192,128]{2,1,0:T(8,128)(2,1)}, bf16[6,192,128]{2,1,0:T(8,128)(2,1)}, bf16[6,192,128]{2,1,0:T(8,128)(2,1)}) custom-call(bf16[192,2560]{1,0:T(8,128)(2,1)} %q.3, bf16[192,2560]{1,0:T(8,128)(2,1)} %k.3, bf16[192,2560]{1,0:T(8,128)(2,1)} %v.3, bf16[9,192,128]{2,1,0:T(8,128)(2,1)} %get-tuple-element.38.rest_0_.refs_0_), custom_call_target="tpu_custom_call" | custom-call | bytes 1000 | tf_op jit(solution)/shard_map/pack/pallas_call | solution.py:97
  14.2 3.5 %collective-permute-done.refs_1_ = bf16[9,192,128]{2,1,0:T(8,128)(2,1)S(1)} collective-permute-done((bf16[9,192,128]{2,1,0:T(8,128)(2,1)}, bf16[9,192,128]{2,1,0:T(8,128)(2,1)S(1)}, u32[]{:S(2)}, u32[]{:S(2)}) %collective-permute-start) | collective-permute-done | bytes 442400 | tf_op jit(solution)/shard_map/ppermute | solution.py:44
  17.7 8.3 %collective-permute-done.1.refs_2_ = bf16[9,192,128]{2,1,0:T(8,128)(2,1)S(1)} collective-permute-done((bf16[9,192,128]{2,1,0:T(8,128)(2,1)}, bf16[9,192,128]{2,1,0:T(8,128)(2,1)S(1)}, u32[]{:S(2)}, u32[]{:S(2)}) %collective-permute-start.1) | collective-permute-done | bytes 442400 | tf_op jit(solution)/shard_map/ppermute | solution.py:44
  26.2 1.9 %stack.36 = (bf16[3,2,384,128]{3,2,1,0:T(8,128)(2,1)S(1)}, bf16[6,2,384,128]{3,2,1,0:T(8,128)(2,1)S(1)}, bf16[6,192,128]{2,1,0:T(8,128)(2,1)S(1)}, bf16[6,192,12...) custom-call(s32[9]{0:T(128)S(1)} %stack.35.meta, ...), custom_call_target="tpu_custom_call", output_to_operand_aliasing={{2}: (5, {}), {3}: (6, {}), {4}: (7, {})} | custom-call | bytes 1000 | tf_op jit(solution)/shard_map/stack/pallas_call | solution.py:133
  28.2 3.5 %collective-permute-start.9 = (bf16[6,2,384,128]{3,2,1,0:T(8,128)(2,1)S(1)}, bf16[6,2,384,128]{3,2,1,0:T(8,128)(2,1)S(1)}, u32[]{:S(2)}, u32[]{:S(2)}) collective-permute-start(bf16[6,2,384,128]{3,2,1,0:T(8,128)(2,1)S(1)} %get-tuple-element.50.ka.va), channel_id=1, source_target_pairs={{0,8},{1,9},{2,10},{3,11},{4,12},{5,13},{6,14},{7,15},{8,16},{9,17... | collective-permute-start | bytes 3538952 | tf_op jit(solution)/shard_map/ppermute | solution.py:44
  31.7 2.4 %collective-permute-start.7 = (bf16[3,2,384,128]{3,2,1,0:T(8,128)(2,1)S(1)}, bf16[3,2,384,128]{3,2,1,0:T(8,128)(2,1)S(1)}, u32[]{:S(2)}, u32[]{:S(2)}) collective-permute-start(bf16[3,2,384,128]{3,2,1,0:T(8,128)(2,1)S(1)} %get-tuple-element.49.q.rest_0_), channel_id=1, source_target_pairs={{8,0},{9,1},{10,2},{11,3},{12,4},{13,5},{14,6},{15,7},{16,8},{17,9... | collective-permute-start | bytes 1769480 | tf_op jit(solution)/shard_map/ppermute | solution.py:44
  34.1 1.6 %collective-permute-start.3 = (bf16[6,192,128]{2,1,0:T(8,128)(2,1)S(1)}, bf16[6,192,128]{2,1,0:T(8,128)(2,1)S(1)}, u32[]{:S(2)}, u32[]{:S(2)}) collective-permute-start(bf16[6,192,128]{2,1,0:T(8,128)(2,1)S(1)} %get-tuple-element.46), channel_id=1, source_target_pairs={{0,6},{1,7},{2,4},{3,5},{4,2},{5,3},{6,0},{7,1},{8,14},{9,15},{10,... | collective-permute-start | bytes 884744 | tf_op jit(solution)/shard_map/ppermute | solution.py:44
  37.7 5.2 %near.2 = (f32[3,768,128]{2,1,0:T(8,128)S(1)}, f32[3,8,128]{2,1,0:T(8,128)S(1)}) custom-call(bf16[3,2,384,128]{3,2,1,0:T(8,128)(2,1)S(1)} %get-tuple-element.49.q.rest_0_, bf16[6,2,384,128]{3,2,1,0:T(8,128)(2,1)S(1)} %get-tuple-element.50.ka.va, bf16[6,2,384,128]{3,2,1,0:T(8,128)(2,1)S(1)} %get-tuple-element.50.ka.va, ...), custom_call_target="tpu_custom_call" | custom-call | bytes 1000 | tf_op jit(solution)/shard_map/near/pallas_call | solution.py:352
  42.9 2.1 %collective-permute-done.3.refs_1_ = bf16[6,192,128]{2,1,0:T(8,128)(2,1)S(1)} collective-permute-done((bf16[6,192,128]{2,1,0:T(8,128)(2,1)S(1)}, bf16[6,192,128]{2,1,0:T(8,128)(2,1)S(1)}, u32[]{:S(2)}, u32[]{:S(2)}) %collective-permute-start.3) | collective-permute-done | bytes 294944 | tf_op jit(solution)/shard_map/ppermute | solution.py:44
  45.0 5.2 %collective-permute-done.4.refs_2_ = bf16[6,192,128]{2,1,0:T(8,128)(2,1)S(1)} collective-permute-done((bf16[6,192,128]{2,1,0:T(8,128)(2,1)S(1)}, bf16[6,192,128]{2,1,0:T(8,128)(2,1)S(1)}, u32[]{:S(2)}, u32[]{:S(2)}) %collective-permute-start.4) | collective-permute-done | bytes 294944 | tf_op jit(solution)/shard_map/ppermute | solution.py:44
  51.4 3.4 %collective-permute-start.8 = (bf16[4,2,384,128]{3,2,1,0:T(8,128)(2,1)S(1)}, bf16[4,2,384,128]{3,2,1,0:T(8,128)(2,1)S(1)}, u32[]{:S(2)}, u32[]{:S(2)}) collective-permute-start(bf16[4,2,384,128]{3,2,1,0:T(8,128)(2,1)S(1)} %get-tuple-element.53.ka.va), channel_id=1, source_target_pairs={{0,8},{1,9},{2,10},{3,11},{4,12},{5,13},{6,14},{7,15},{8,16},{9,17... | collective-permute-start | bytes 2359304 | tf_op jit(solution)/shard_map/ppermute | solution.py:44
  54.8 4.0 %collective-permute-done.9.kv = bf16[6,2,384,128]{3,2,1,0:T(8,128)(2,1)S(1)} collective-permute-done((bf16[6,2,384,128]{3,2,1,0:T(8,128)(2,1)S(1)}, bf16[6,2,384,128]{3,2,1,0:T(8,128)(2,1)S(1)}, u32[]{:S(2)}, u32[]{:S(2)}) %collective-permute-start.9) | collective-permute-done | bytes 1179680 | tf_op jit(solution)/shard_map/ppermute | solution.py:44
  59.7 1.9 %collective-permute-start.12 = (bf16[2,2,384,128]{3,2,1,0:T(8,128)(2,1)S(1)}, bf16[2,2,384,128]{3,2,1,0:T(8,128)(2,1)S(1)}, u32[]{:S(2)}, u32[]{:S(2)}) collective-permute-start(bf16[2,2,384,128]{3,2,1,0:T(8,128)(2,1)S(1)} %get-tuple-element.52.rest_0_.q), channel_id=1, source_target_pairs={{8,0},{9,1},{10,2},{11,3},{12,4},{13,5},{14,6},{15,7},{16,8},{17,9... | collective-permute-start | bytes 1179656 | tf_op jit(solution)/shard_map/ppermute | solution.py:44
  62.0 5.1 %remote.2.rest_0_ = bf16[3,800,128]{2,1,0:T(8,128)(2,1)S(1)} custom-call(bf16[3,2,384,128]{3,2,1,0:T(8,128)(2,1)S(1)} %collective-permute-done.7.refs_5_.q, bf16[3,2,384,128]{3,2,1,0:T(8,128)(2,1)S(1)} %get-tuple-element.54.ka, bf16[3,2,384,128]{3,2,1,0:T(8,128)(2,1)S(1)} %get-tuple-element.55.va, bf16[3,2,384,128]{3,2,1,0:T(8,128)(2,1)S(1)} %collective-permute-done.10.kb, ...), custom_call_target="tpu_custom_call" | custom-call | bytes 1000 | tf_op jit(solution)/shard_map/remote/pallas_call | solution.py:352
  67.2 7.1 %far.2 = (f32[3,768,128]{2,1,0:T(8,128)S(1)}, f32[3,8,128]{2,1,0:T(8,128)S(1)}) custom-call(s32[9]{0:T(128)S(1)} %stack.35.meta, bf16[3,2,384,128]{3,2,1,0:T(8,128)(2,1)S(1)} %get-tuple-element.49.q.rest_0_, bf16[3,2,384,128]{3,2,1,0:T(8,128)(2,1)S(1)} %get-tuple-element.54.ka, bf16[3,2,384,128]{3,2,1,0:T(8,128)(2,1)S(1)} %get-tuple-element.55.va, ...), custom_call_target="tpu_custom_call" | custom-call | bytes 1000 | tf_op jit(solution)/shard_map/far/pallas_call | solution.py:352
  75.8 3.5 %collective-permute-start.16 = (bf16[3,800,128]{2,1,0:T(8,128)(2,1)S(1)}, bf16[3,800,128]{2,1,0:T(8,128)(2,1)S(1)}, u32[]{:S(2)}, u32[]{:S(2)}) collective-permute-start(bf16[3,800,128]{2,1,0:T(8,128)(2,1)S(1)} %remote.2.rest_0_), channel_id=1, source_target_pairs={{0,8},{1,9},{2,10},{3,11},{4,12},{5,13},{6,14},{7,15},{8,16},{9,17... | collective-permute-start | bytes 1843208 | tf_op jit(solution)/shard_map/ppermute | solution.py:44
  79.3 3.4 %remote.3.rest_0_ = bf16[2,800,128]{2,1,0:T(8,128)(2,1)S(1)} custom-call(bf16[2,2,384,128]{3,2,1,0:T(8,128)(2,1)S(1)} %collective-permute-done.12.refs_2_.q, bf16[4,2,384,128]{3,2,1,0:T(8,128)(2,1)S(1)} %in_order.1.ka.va, bf16[4,2,384,128]{3,2,1,0:T(8,128)(2,1)S(1)} %in_order.1.ka.va, bf16[4,2,384,128]{3,2,1,0:T(8,128)(2,1)S(1)} %collective-permute-done.13.kb.vb, ...), custom_call_target="tpu_custom_call" | custom-call | bytes 1000 | tf_op jit(solution)/shard_map/remote/pallas_call | solution.py:352
  82.8 3.7 %collective-permute-start.15 = (bf16[2,800,128]{2,1,0:T(8,128)(2,1)S(1)}, bf16[2,800,128]{2,1,0:T(8,128)(2,1)S(1)}, u32[]{:S(2)}, u32[]{:S(2)}) collective-permute-start(bf16[2,800,128]{2,1,0:T(8,128)(2,1)S(1)} %remote.3.rest_0_), channel_id=1, source_target_pairs={{0,8},{1,9},{2,10},{3,11},{4,12},{5,13},{6,14},{7,15},{8,16},{9,17... | collective-permute-start | bytes 1228808 | tf_op jit(solution)/shard_map/ppermute | solution.py:44
  86.4 3.5 %near.3 = (f32[2,768,128]{2,1,0:T(8,128)S(1)}, f32[2,8,128]{2,1,0:T(8,128)S(1)}) custom-call(bf16[2,2,384,128]{3,2,1,0:T(8,128)(2,1)S(1)} %get-tuple-element.52.rest_0_.q, bf16[4,2,384,128]{3,2,1,0:T(8,128)(2,1)S(1)} %get-tuple-element.53.ka.va, bf16[4,2,384,128]{3,2,1,0:T(8,128)(2,1)S(1)} %get-tuple-element.53.ka.va, ...), custom_call_target="tpu_custom_call" | custom-call | bytes 1000 | tf_op jit(solution)/shard_map/near/pallas_call | solution.py:352
  89.9 4.9 %far.3 = (f32[2,768,128]{2,1,0:T(8,128)S(1)}, f32[2,8,128]{2,1,0:T(8,128)S(1)}) custom-call(s32[9]{0:T(128)S(1)} %stack.35.meta, bf16[2,2,384,128]{3,2,1,0:T(8,128)(2,1)S(1)} %get-tuple-element.52.rest_0_.q, bf16[4,2,384,128]{3,2,1,0:T(8,128)(2,1)S(1)} %in_order.1.ka.va, bf16[4,2,384,128]{3,2,1,0:T(8,128)(2,1)S(1)} %in_order.1.ka.va, ...), custom_call_target="tpu_custom_call" | custom-call | bytes 1000 | tf_op jit(solution)/shard_map/far/pallas_call | solution.py:352
  96.1 1.6 %collective-permute-start.20 = (bf16[3,192,128]{2,1,0:T(8,128)(2,1)S(1)}, bf16[3,192,128]{2,1,0:T(8,128)(2,1)S(1)}, u32[]{:S(2)}, u32[]{:S(2)}) collective-permute-start(bf16[3,192,128]{2,1,0:T(8,128)(2,1)S(1)} %get-tuple-element.68), channel_id=1, source_target_pairs={{0,6},{1,7},{2,4},{3,5},{4,2},{5,3},{6,0},{7,1},{8,14},{9,15},{10,... | collective-permute-start | bytes 442376 | tf_op jit(solution)/shard_map/ppermute | solution.py:44
  99.6 2.6 %collective-permute-done.15.o_far = bf16[2,800,128]{2,1,0:T(8,128)(2,1)S(1)} collective-permute-done((bf16[2,800,128]{2,1,0:T(8,128)(2,1)S(1)}, bf16[2,800,128]{2,1,0:T(8,128)(2,1)S(1)}, u32[]{:S(2)}, u32[]{:S(2)}) %collective-permute-start.15) | collective-permute-done | bytes 409632 | tf_op jit(solution)/shard_map/ppermute | solution.py:44
  (60 shorter events, 23.9 us)
Async XLA Ops:
  3.5 14.2 %collective-permute-start = (bf16[9,192,128]{2,1,0:T(8,128)(2,1)}, bf16[9,192,128]{2,1,0:T(8,128)(2,1)S(1)}, u32[]{:S(2)}, u32[]{:S(2)}) collective-permute-start(bf16[9,192,128]{2,1,0:T(8,128)(2,1)} %get-tuple-element.40), channel_id=1, source_target_pairs={{0,6},{1,7},{2,4},{3,5},{4,2},{5,3},{6,0},{7,1},{8,14},{9,15},{10,... | collective-permute-start | bytes 1327112 | tf_op jit(solution)/shard_map/ppermute | solution.py:44
  5.9 20.1 %collective-permute-start.1 = (bf16[9,192,128]{2,1,0:T(8,128)(2,1)}, bf16[9,192,128]{2,1,0:T(8,128)(2,1)S(1)}, u32[]{:S(2)}, u32[]{:S(2)}) collective-permute-start(bf16[9,192,128]{2,1,0:T(8,128)(2,1)} %get-tuple-element.41), channel_id=1, source_target_pairs={{0,4},{1,5},{2,6},{3,7},{4,0},{5,1},{6,2},{7,3},{8,12},{9,13},{10,... | collective-permute-start | bytes 1327112 | tf_op jit(solution)/shard_map/ppermute | solution.py:44
  6.5 19.7 %collective-permute-start.2 = (bf16[9,192,128]{2,1,0:T(8,128)(2,1)}, bf16[9,192,128]{2,1,0:T(8,128)(2,1)}, u32[]{:S(2)}, u32[]{:S(2)}) collective-permute-start(bf16[9,192,128]{2,1,0:T(8,128)(2,1)} %get-tuple-element.42), channel_id=1, source_target_pairs={{0,2},{1,3},{2,0},{3,1},{4,6},{5,7},{6,4},{7,5},{8,10},{9,11},{10,... | collective-permute-start | bytes 1327112 | tf_op jit(solution)/shard_map/ppermute | solution.py:44
  12.8 13.4 %copy-start.1 = (bf16[9,192,128]{2,1,0:T(8,128)(2,1)S(1)}, bf16[9,192,128]{2,1,0:T(8,128)(2,1)}, u32[]{:S(2)}) copy-start(bf16[9,192,128]{2,1,0:T(8,128)(2,1)} %get-tuple-element.38.rest_0_.refs_0_) | copy-start | bytes 1327108
  28.1 9.0 %collective-permute-start.6 = (bf16[6,2,384,128]{3,2,1,0:T(8,128)(2,1)S(1)}, bf16[6,2,384,128]{3,2,1,0:T(8,128)(2,1)S(1)}, u32[]{:S(2)}, u32[]{:S(2)}) collective-permute-start(bf16[6,2,384,128]{3,2,1,0:T(8,128)(2,1)S(1)} %get-tuple-element.50.ka.va), channel_id=1, source_target_pairs={{0,1},{1,0},{2,3},{3,2},{4,5},{5,4},{6,7},{7,6},{8,9},{9,8},{10,11... | collective-permute-start | bytes 3538952 | tf_op jit(solution)/shard_map/ppermute | solution.py:44
  28.2 30.7 %collective-permute-start.9 = (bf16[6,2,384,128]{3,2,1,0:T(8,128)(2,1)S(1)}, bf16[6,2,384,128]{3,2,1,0:T(8,128)(2,1)S(1)}, u32[]{:S(2)}, u32[]{:S(2)}) collective-permute-start(bf16[6,2,384,128]{3,2,1,0:T(8,128)(2,1)S(1)} %get-tuple-element.50.ka.va), channel_id=1, source_target_pairs={{0,8},{1,9},{2,10},{3,11},{4,12},{5,13},{6,14},{7,15},{8,16},{9,17... | collective-permute-start | bytes 3538952 | tf_op jit(solution)/shard_map/ppermute | solution.py:44
  31.7 18.6 %collective-permute-start.7 = (bf16[3,2,384,128]{3,2,1,0:T(8,128)(2,1)S(1)}, bf16[3,2,384,128]{3,2,1,0:T(8,128)(2,1)S(1)}, u32[]{:S(2)}, u32[]{:S(2)}) collective-permute-start(bf16[3,2,384,128]{3,2,1,0:T(8,128)(2,1)S(1)} %get-tuple-element.49.q.rest_0_), channel_id=1, source_target_pairs={{8,0},{9,1},{10,2},{11,3},{12,4},{13,5},{14,6},{15,7},{16,8},{17,9... | collective-permute-start | bytes 1769480 | tf_op jit(solution)/shard_map/ppermute | solution.py:44
  34.1 10.9 %collective-permute-start.3 = (bf16[6,192,128]{2,1,0:T(8,128)(2,1)S(1)}, bf16[6,192,128]{2,1,0:T(8,128)(2,1)S(1)}, u32[]{:S(2)}, u32[]{:S(2)}) collective-permute-start(bf16[6,192,128]{2,1,0:T(8,128)(2,1)S(1)} %get-tuple-element.46), channel_id=1, source_target_pairs={{0,6},{1,7},{2,4},{3,5},{4,2},{5,3},{6,0},{7,1},{8,14},{9,15},{10,... | collective-permute-start | bytes 884744 | tf_op jit(solution)/shard_map/ppermute | solution.py:44
  35.7 14.5 %collective-permute-start.4 = (bf16[6,192,128]{2,1,0:T(8,128)(2,1)S(1)}, bf16[6,192,128]{2,1,0:T(8,128)(2,1)S(1)}, u32[]{:S(2)}, u32[]{:S(2)}) collective-permute-start(bf16[6,192,128]{2,1,0:T(8,128)(2,1)S(1)} %get-tuple-element.47), channel_id=1, source_target_pairs={{0,4},{1,5},{2,6},{3,7},{4,0},{5,1},{6,2},{7,3},{8,12},{9,13},{10,... | collective-permute-start | bytes 884744 | tf_op jit(solution)/shard_map/ppermute | solution.py:44
  37.1 13.1 %collective-permute-start.5 = (bf16[6,192,128]{2,1,0:T(8,128)(2,1)S(1)}, bf16[6,192,128]{2,1,0:T(8,128)(2,1)S(1)}, u32[]{:S(2)}, u32[]{:S(2)}) collective-permute-start(bf16[6,192,128]{2,1,0:T(8,128)(2,1)S(1)} %get-tuple-element.48), channel_id=1, source_target_pairs={{0,2},{1,3},{2,0},{3,1},{4,6},{5,7},{6,4},{7,5},{8,10},{9,11},{10,... | collective-permute-start | bytes 884744 | tf_op jit(solution)/shard_map/ppermute | solution.py:44
  51.4 23.9 %collective-permute-start.8 = (bf16[4,2,384,128]{3,2,1,0:T(8,128)(2,1)S(1)}, bf16[4,2,384,128]{3,2,1,0:T(8,128)(2,1)S(1)}, u32[]{:S(2)}, u32[]{:S(2)}) collective-permute-start(bf16[4,2,384,128]{3,2,1,0:T(8,128)(2,1)S(1)} %get-tuple-element.53.ka.va), channel_id=1, source_target_pairs={{0,8},{1,9},{2,10},{3,11},{4,12},{5,13},{6,14},{7,15},{8,16},{9,17... | collective-permute-start | bytes 2359304 | tf_op jit(solution)/shard_map/ppermute | solution.py:44
  59.1 2.5 %collective-permute-start.10 = (bf16[3,2,384,128]{3,2,1,0:T(8,128)(2,1)S(1)}, bf16[3,2,384,128]{3,2,1,0:T(8,128)(2,1)S(1)}, u32[]{:S(2)}, u32[]{:S(2)}) collective-permute-start(bf16[3,2,384,128]{3,2,1,0:T(8,128)(2,1)S(1)} %get-tuple-element.54.ka), channel_id=1, source_target_pairs={{0,1},{1,0},{2,3},{3,2},{4,5},{5,4},{6,7},{7,6},{8,9},{9,8},{10,11... | collective-permute-start | bytes 1769480 | tf_op jit(solution)/shard_map/ppermute | solution.py:44
  59.2 2.8 %collective-permute-start.11 = (bf16[3,2,384,128]{3,2,1,0:T(8,128)(2,1)S(1)}, bf16[3,2,384,128]{3,2,1,0:T(8,128)(2,1)S(1)}, u32[]{:S(2)}, u32[]{:S(2)}) collective-permute-start(bf16[3,2,384,128]{3,2,1,0:T(8,128)(2,1)S(1)} %get-tuple-element.55.va), channel_id=1, source_target_pairs={{0,1},{1,0},{2,3},{3,2},{4,5},{5,4},{6,7},{7,6},{8,9},{9,8},{10,11... | collective-permute-start | bytes 1769480 | tf_op jit(solution)/shard_map/ppermute | solution.py:44
  59.7 14.6 %collective-permute-start.12 = (bf16[2,2,384,128]{3,2,1,0:T(8,128)(2,1)S(1)}, bf16[2,2,384,128]{3,2,1,0:T(8,128)(2,1)S(1)}, u32[]{:S(2)}, u32[]{:S(2)}) collective-permute-start(bf16[2,2,384,128]{3,2,1,0:T(8,128)(2,1)S(1)} %get-tuple-element.52.rest_0_.q), channel_id=1, source_target_pairs={{8,0},{9,1},{10,2},{11,3},{12,4},{13,5},{14,6},{15,7},{16,8},{17,9... | collective-permute-start | bytes 1179656 | tf_op jit(solution)/shard_map/ppermute | solution.py:44
  75.3 4.0 %collective-permute-start.13 = (bf16[4,2,384,128]{3,2,1,0:T(8,128)(2,1)S(1)}, bf16[4,2,384,128]{3,2,1,0:T(8,128)(2,1)S(1)}, u32[]{:S(2)}, u32[]{:S(2)}) collective-permute-start(bf16[4,2,384,128]{3,2,1,0:T(8,128)(2,1)S(1)} %in_order.1.ka.va), channel_id=1, source_target_pairs={{0,1},{1,0},{2,3},{3,2},{4,5},{5,4},{6,7},{7,6},{8,9},{9,8},{10,11... | collective-permute-start | bytes 2359304 | tf_op jit(solution)/shard_map/ppermute | solution.py:44
  75.3 11.1 %collective-permute-start.14 = (bf16[4,2,384,128]{3,2,1,0:T(8,128)(2,1)S(1)}, bf16[4,2,384,128]{3,2,1,0:T(8,128)(2,1)S(1)}, u32[]{:S(2)}, u32[]{:S(2)}) collective-permute-start(bf16[4,2,384,128]{3,2,1,0:T(8,128)(2,1)S(1)} %get-tuple-element.53.ka.va), channel_id=1, source_target_pairs={{0,1},{1,0},{2,3},{3,2},{4,5},{5,4},{6,7},{7,6},{8,9},{9,8},{10,11... | collective-permute-start | bytes 2359304 | tf_op jit(solution)/shard_map/ppermute | solution.py:44
  75.8 19.0 %collective-permute-start.16 = (bf16[3,800,128]{2,1,0:T(8,128)(2,1)S(1)}, bf16[3,800,128]{2,1,0:T(8,128)(2,1)S(1)}, u32[]{:S(2)}, u32[]{:S(2)}) collective-permute-start(bf16[3,800,128]{2,1,0:T(8,128)(2,1)S(1)} %remote.2.rest_0_), channel_id=1, source_target_pairs={{0,8},{1,9},{2,10},{3,11},{4,12},{5,13},{6,14},{7,15},{8,16},{9,17... | collective-permute-start | bytes 1843208 | tf_op jit(solution)/shard_map/ppermute | solution.py:44
  82.8 19.5 %collective-permute-start.15 = (bf16[2,800,128]{2,1,0:T(8,128)(2,1)S(1)}, bf16[2,800,128]{2,1,0:T(8,128)(2,1)S(1)}, u32[]{:S(2)}, u32[]{:S(2)}) collective-permute-start(bf16[2,800,128]{2,1,0:T(8,128)(2,1)S(1)} %remote.3.rest_0_), channel_id=1, source_target_pairs={{0,8},{1,9},{2,10},{3,11},{4,12},{5,13},{6,14},{7,15},{8,16},{9,17... | collective-permute-start | bytes 1228808 | tf_op jit(solution)/shard_map/ppermute | solution.py:44
  96.1 10.2 %collective-permute-start.20 = (bf16[3,192,128]{2,1,0:T(8,128)(2,1)S(1)}, bf16[3,192,128]{2,1,0:T(8,128)(2,1)S(1)}, u32[]{:S(2)}, u32[]{:S(2)}) collective-permute-start(bf16[3,192,128]{2,1,0:T(8,128)(2,1)S(1)} %get-tuple-element.68), channel_id=1, source_target_pairs={{0,6},{1,7},{2,4},{3,5},{4,2},{5,3},{6,0},{7,1},{8,14},{9,15},{10,... | collective-permute-start | bytes 442376 | tf_op jit(solution)/shard_map/ppermute | solution.py:44
  97.7 9.1 %collective-permute-start.21 = (bf16[3,192,128]{2,1,0:T(8,128)(2,1)S(1)}, bf16[3,192,128]{2,1,0:T(8,128)(2,1)S(1)}, u32[]{:S(2)}, u32[]{:S(2)}) collective-permute-start(bf16[3,192,128]{2,1,0:T(8,128)(2,1)S(1)} %get-tuple-element.69), channel_id=1, source_target_pairs={{0,4},{1,5},{2,6},{3,7},{4,0},{5,1},{6,2},{7,3},{8,12},{9,13},{10,... | collective-permute-start | bytes 442376 | tf_op jit(solution)/shard_map/ppermute | solution.py:44
  99.1 7.7 %collective-permute-start.22 = (bf16[3,192,128]{2,1,0:T(8,128)(2,1)S(1)}, bf16[3,192,128]{2,1,0:T(8,128)(2,1)S(1)}, u32[]{:S(2)}, u32[]{:S(2)}) collective-permute-start(bf16[3,192,128]{2,1,0:T(8,128)(2,1)S(1)} %get-tuple-element.70), channel_id=1, source_target_pairs={{0,2},{1,3},{2,0},{3,1},{4,6},{5,7},{6,4},{7,5},{8,10},{9,11},{10,... | collective-permute-start | bytes 442376 | tf_op jit(solution)/shard_map/ppermute | solution.py:44
  103.2 6.5 %collective-permute-start.17 = (bf16[2,192,128]{2,1,0:T(8,128)(2,1)S(1)}, bf16[2,192,128]{2,1,0:T(8,128)(2,1)S(1)}, u32[]{:S(2)}, u32[]{:S(2)}) collective-permute-start(bf16[2,192,128]{2,1,0:T(8,128)(2,1)S(1)} %get-tuple-element.65), channel_id=1, source_target_pairs={{0,6},{1,7},{2,4},{3,5},{4,2},{5,3},{6,0},{7,1},{8,14},{9,15},{10,... | collective-permute-start | bytes 294920 | tf_op jit(solution)/shard_map/ppermute | solution.py:44
  104.9 5.3 %collective-permute-start.18 = (bf16[2,192,128]{2,1,0:T(8,128)(2,1)S(1)}, bf16[2,192,128]{2,1,0:T(8,128)(2,1)S(1)}, u32[]{:S(2)}, u32[]{:S(2)}) collective-permute-start(bf16[2,192,128]{2,1,0:T(8,128)(2,1)S(1)} %get-tuple-element.66), channel_id=1, source_target_pairs={{0,4},{1,5},{2,6},{3,7},{4,0},{5,1},{6,2},{7,3},{8,12},{9,13},{10,... | collective-permute-start | bytes 294920 | tf_op jit(solution)/shard_map/ppermute | solution.py:44
  106.3 4.6 %collective-permute-start.19 = (bf16[2,192,128]{2,1,0:T(8,128)(2,1)S(1)}, bf16[2,192,128]{2,1,0:T(8,128)(2,1)S(1)}, u32[]{:S(2)}, u32[]{:S(2)}) collective-permute-start(bf16[2,192,128]{2,1,0:T(8,128)(2,1)S(1)} %get-tuple-element.67), channel_id=1, source_target_pairs={{0,2},{1,3},{2,0},{3,1},{4,6},{5,7},{6,4},{7,5},{8,10},{9,11},{10,... | collective-permute-start | bytes 294920 | tf_op jit(solution)/shard_map/ppermute | solution.py:44
  (7 other events, 80.8 us)
